TPU v7x, 128 devices: a whole 4x4x4 slice. The times are simulated.
128 devices in a mesh: vocab: 16 (over x, z), tok: 8 (over y, core).
Axes of the slice: x: 4, y: 4, z: 4, core: 2. Of those that a mesh axis runs over, the one named last changes fastest.
Arguments:
- hidden_states: bfloat16 [1024, 2048], P('tok'), may hold values from -8 to 8, as said below
- tied_table: bfloat16 [131072, 2048], P(('vocab', 'tok')), may hold values from -3 to 3
- labels: int32 [1024], P('tok'), may hold values from 0 to 131071
- dec_ids: int32 [1024], P('tok'), may hold values from 0 to 131071
- enc_ids: int32 [1024], P('tok'), may hold values from 0 to 131071
- dec_grad: bfloat16 [1024, 2048], P('tok'), may hold values from -6 to 6
- enc_grad: bfloat16 [1024, 2048], P('tok'), may hold values from -6 to 6
Outputs:
- grad_table: float32 [131072, 2048], P(('vocab', 'tok'))
- grad_hidden: float32 [1024, 2048], P('tok', 'vocab')
- token_loss: float32 [1024], P('tok')
Inputs may be any that keep to these rules, and one draw needn't show every extreme that they name: `hidden_states`: decoder states, of order one.
All inputs are finite; a program needn't handle non-finite values.
Results may differ from a plain program's by a relative error of at most 0.002.
Values may be sent and summed in bfloat16 or wider, within the bound.
No kernel may reach another device: no remote copies, remote signals or barrier semaphores. Data moves between devices by JAX's collectives and lax.ppermute only.
A program may use at most 128 MiB of HBM per device.

v0:
```python
import jax
import jax.numpy as jnp
from jax import lax
from jax.sharding import PartitionSpec as P


def per_device(hidden_states, tied_table, labels, dec_ids, enc_ids, dec_grad, enc_grad):
    tok_rows = hidden_states.shape[0]
    row_count = tied_table.shape[0]
    model_width = tied_table.shape[1]
    vocab_count = lax.axis_size("vocab")
    tok_count = lax.axis_size("tok")
    whole_hidden, whole_dec, whole_enc = (
        lax.all_gather(hidden_states, "tok", axis=0, tiled=True),
        lax.all_gather(dec_grad, "tok", axis=0, tiled=True),
        lax.all_gather(enc_grad, "tok", axis=0, tiled=True),
    )
    all_labels, all_dec, all_enc = (
        lax.all_gather(labels, "tok", axis=0, tiled=True),
        lax.all_gather(dec_ids, "tok", axis=0, tiled=True),
        lax.all_gather(enc_ids, "tok", axis=0, tiled=True),
    )
    first_row = (lax.axis_index("vocab") * tok_count + lax.axis_index("tok")) * row_count
    row_iota = lax.iota(jnp.int32, row_count)
    logits = lax.dot_general(
        whole_hidden, tied_table, (((1,), (1,)), ((), ())), preferred_element_type=jnp.float32
    )
    is_label = (all_labels - first_row)[:, None] == row_iota[None, :]
    picked_part = jnp.sum(jnp.where(is_label, logits, jnp.zeros_like(logits)), axis=1)
    local_peak = jnp.max(logits, axis=1)
    row_peak = lax.pmax(local_peak, ("vocab", "tok"))
    local_total = jnp.sum(jnp.exp(logits - row_peak[:, None]), axis=1)
    exp_total, picked = lax.psum((local_total, picked_part), ("vocab", "tok"))
    log_norm = row_peak + jnp.log(exp_total)
    loss_all = log_norm - picked
    token_loss = lax.dynamic_slice_in_dim(loss_all, lax.axis_index("tok") * tok_rows, tok_rows)
    logit_grad = (jnp.exp(logits - log_norm[:, None]) - is_label.astype(jnp.float32)).astype(
        jnp.bfloat16
    )
    split_table = tied_table.reshape(row_count, vocab_count, model_width // vocab_count)
    split_grad = logit_grad.reshape(tok_count, tok_rows, row_count)
    partial_hidden = jnp.einsum(
        "tkr,rvc->vtkc", split_grad, split_table, preferred_element_type=jnp.float32
    )
    summed = lax.psum(partial_hidden, ("vocab", "tok"))
    grad_hidden = summed[lax.axis_index("vocab"), lax.axis_index("tok")]
    dec_onehot = ((all_dec - first_row)[None, :] == row_iota[:, None]).astype(jnp.bfloat16)
    enc_onehot = ((all_enc - first_row)[None, :] == row_iota[:, None]).astype(jnp.bfloat16)
    grad_table = lax.dot_general(
        logit_grad, whole_hidden, (((0,), (0,)), ((), ())), preferred_element_type=jnp.float32
    )
    grad_table = grad_table + jnp.dot(dec_onehot, whole_dec, preferred_element_type=jnp.float32)
    grad_table = grad_table + jnp.dot(enc_onehot, whole_enc, preferred_element_type=jnp.float32)
    return (grad_table, grad_hidden, token_loss)


def solution(mesh):
    in_specs = (
        P("tok", None),
        P(("vocab", "tok"), None),
        P("tok"),
        P("tok"),
        P("tok"),
        P("tok", None),
        P("tok", None),
    )
    out_specs = (P(("vocab", "tok"), None), P("tok", "vocab"), P("tok"))
    return jax.shard_map(
        per_device, mesh=mesh, in_specs=in_specs, out_specs=out_specs, check_vma=False
    )
```

profile of v0, /device:TPU:1, one launch (start us, length us, event | category | flops | bytes accessed | tf_op | source)
XLA Modules:
  0.0 365.1 jit_solution(18397980655616743952)
XLA Ops:
  7.2 0.0 all-gather.7.cloned.1.call-start
  7.2 0.7 all-gather.7.cloned.1.call-update
  7.9 0.0 all-gather.11.cloned.1.call-start
  7.9 0.7 all-gather.11.cloned.1.call-update
  8.6 0.0 all-gather.9.cloned.1.call-start
  8.7 0.7 all-gather.9.cloned.1.call-update
  9.4 0.0 all-reduce.3.cloned.1.call-start
  9.4 12.2 %all-gather = s32[8,1,128]{2,1,0:T(1,128)S(1)} all-gather(s32[1,1,128]{2,1,0:T(1,128)} %bitcast.50), channel_id=1, replica_groups=mesh['vocab'=16,'tok'=8] {'tok'}, dimensions={0}, use_global_device_ids=true | all-gather | bytes 4608 | tf_op jit(solution)/shard_map/all_gather | solution.py:19
  21.7 23.8 %all-gather.7.cloned.1.call-done = bf16[1024,2048]{1,0:T(8,128)(2,1)} async-done(((bf16[128,2048]{1,0:T(8,128)(2,1)}), bf16[1024,2048]{1,0:T(8,128)(2,1)}) %all-gather.7.cloned.1.call-update) | async-done | bytes 4194320 | tf_op jit(solution)/shard_map/all_gather | solution.py:14
  45.5 10.0 %fusion.8 = (f32[1024]{0:T(1024)S(1)}, f32[1024,1024]{1,0:T(8,128)}) fusion(bf16[1024,2048]{1,0:T(8,128)(2,1)} %all-gather.7.cloned.1.call-done, bf16[1024,2048]{1,0:T(8,128)(2,1)} %param.8), kind=kOutput, calls=%fused_computation.21 | convolution fusion | flops 4296014848 | bytes 12587008 | tf_op jit(solution)/shard_map/dot_general | solution.py:25
  55.5 65.6 %pmax.7 = f32[1024]{0:T(1024)S(1)} all-reduce(f32[1024]{0:T(1024)S(1)} %get-tuple-element.9), channel_id=1, replica_groups=mesh['vocab'=16,'tok'=8] {'vocab','tok'}, use_global_device_ids=true, to_apply=%region_1.2 | all-reduce | flops 1024 | bytes 8192 | tf_op jit(solution)/shard_map/pmax | solution.py:31
  121.1 3.2 select_reduce_fusion
  124.4 64.3 %all-reduce = (f32[1024]{0:T(1024)S(1)}, f32[1024]{0:T(1024)S(1)}) all-reduce(f32[1024]{0:T(1024)S(1)} %get-tuple-element.4, f32[1024]{0:T(1024)S(1)} %get-tuple-element.3), channel_id=1, replica_groups=mesh['vocab'=16,'tok'=8] {'vocab','tok'}, use_global_device_ids=true, to_apply=%region_3.4 | all-reduce | flops 2048 | bytes 16384 | tf_op jit(solution)/shard_map/psum | solution.py:33
  188.7 0.0 copy-start.2
  188.7 3.0 subtract_convert_fusion
  191.7 0.4 copy-done.2
  192.1 6.7 %fusion.4 = f32[16,8,128,128]{3,2,0,1:T(8,128)} fusion(bf16[8,128,1024,1]{2,1,3,0:T(8,128)(2,1)S(1)} %bitcast.42, bf16[1024,2048]{1,0:T(8,128)(2,1)S(1)} %copy-done.2), kind=kOutput, calls=%fused_computation.12 | convolution fusion | flops 4294967296 | bytes 14680064 | tf_op jit(solution)/shard_map/tkr,rvc->vtkc/dot_general | solution.py:42
  198.8 0.0 copy-start
  198.8 0.0 copy-start.1
  198.8 0.0 all-reduce.3.cloned.1.call-update
  198.8 0.6 copy-done
  199.5 9.1 %all-gather.2 = s32[8,1,128]{2,1,0:T(1,128)S(1)} all-gather(s32[1,1,128]{2,1,0:T(1,128)S(1)} %bitcast.51), channel_id=1, replica_groups=mesh['vocab'=16,'tok'=8] {'tok'}, dimensions={0}, use_global_device_ids=true | all-gather | bytes 4608 | tf_op jit(solution)/shard_map/all_gather | solution.py:21
  208.5 0.0 copy-done.1
  208.5 9.3 %all-gather.1 = s32[8,1,128]{2,1,0:T(1,128)S(1)} all-gather(s32[1,1,128]{2,1,0:T(1,128)S(1)} %bitcast.52), channel_id=1, replica_groups=mesh['vocab'=16,'tok'=8] {'tok'}, dimensions={0}, use_global_device_ids=true | all-gather | bytes 4608 | tf_op jit(solution)/shard_map/all_gather | solution.py:20
  217.9 0.6 dynamic_slice.7
  218.4 0.0 all-gather.11.cloned.1.call-done
  218.4 8.9 %fusion.3 = f32[1024,2048]{1,0:T(8,128)} fusion(bf16[1024,2048]{1,0:T(8,128)(2,1)} %all-gather.11.cloned.1.call-done, s32[1024]{0:T(1024)S(1)} %bitcast.49), kind=kOutput, calls=%fused_computation.11 | convolution fusion | flops 4296015872 | bytes 12587008 | tf_op jit(solution)/shard_map/dot_general | solution.py:53
  227.4 0.0 all-gather.9.cloned.1.call-done
  227.4 0.0 copy-start.3
  227.4 0.0 copy-start.4
  227.4 9.0 %fusion.2 = f32[1024,2048]{1,0:T(8,128)} fusion(bf16[1024,2048]{1,0:T(8,128)(2,1)} %all-gather.9.cloned.1.call-done, s32[1024]{0:T(1024)S(1)} %bitcast.48), kind=kOutput, calls=%fused_computation.10 | convolution fusion | flops 4296015872 | bytes 12587008 | tf_op jit(solution)/shard_map/dot_general | solution.py:52
  236.4 0.0 copy-done.3
  236.4 0.0 copy-done.4
  236.4 9.6 %add_add_fusion = f32[1024,2048]{1,0:T(8,128)} fusion(f32[1024,2048]{1,0:T(8,128)S(1)} %copy-done.4, f32[1024,2048]{1,0:T(8,128)} %fusion.2, bf16[1024,1024]{1,0:T(8,128)(2,1)S(1)} %subtract_convert_fusion, bf16[1024,2048]{1,0:T(8,128)(2,1)S(1)} %copy-done.3), kind=kOutput, calls=%fused_computation | convolution fusion | flops 4299161600 | bytes 31457280 | tf_op jit(solution)/shard_map/dot_general | solution.py:49
  246.0 111.0 %all-reduce.3.cloned.1.call-done = f32[16,8,128,128]{3,2,0,1:T(8,128)} async-done(((f32[16,8,128,128]{3,2,0,1:T(8,128)}), f32[16,8,128,128]{3,2,0,1:T(8,128)}) %all-reduce.3.cloned.1.call-update) | async-done | bytes 8388624 | tf_op jit(solution)/shard_map/psum | solution.py:45
  357.1 1.5 dynamic-slice_bitcast_fusion
  (4 shorter events, 0.0 us)
Async XLA Ops:
  7.2 38.3 %all-gather.7.cloned.1.call-start = ((), (), s32[]{:S(2)}) async-start(), calls=%async_computation | async-start | bytes 4718592 | tf_op jit(solution)/shard_map/all_gather | solution.py:14
  7.9 210.5 %all-gather.11.cloned.1.call-start = ((), (), s32[]{:S(2)}) async-start(), calls=%async_computation.2 | async-start | bytes 4718592 | tf_op jit(solution)/shard_map/all_gather | solution.py:16
  8.6 218.7 %all-gather.9.cloned.1.call-start = ((), (), s32[]{:S(2)}) async-start(), calls=%async_computation.1 | async-start | bytes 4718592 | tf_op jit(solution)/shard_map/all_gather | solution.py:15
  9.4 347.7 %all-reduce.3.cloned.1.call-start = ((), (), s32[]{:S(2)}) async-start(), calls=%async_computation.3 | async-start | bytes 16777216 | tf_op jit(solution)/shard_map/psum | solution.py:45
  188.7 3.4 copy-start.2
  198.8 0.7 copy-start
  198.8 9.7 %copy-start.1 = (s32[128]{0:T(128)S(1)}, s32[128]{0:T(128)}, u32[]{:S(2)}) copy-start(s32[128]{0:T(128)} %param.10) | copy-start | bytes 1540
  227.4 9.1 %copy-start.3 = (bf16[1024,2048]{1,0:T(8,128)(2,1)S(1)}, bf16[1024,2048]{1,0:T(8,128)(2,1)}, u32[]{:S(2)}) copy-start(bf16[1024,2048]{1,0:T(8,128)(2,1)} %all-gather.7.cloned.1.call-done) | copy-start | bytes 12582916
  227.4 9.1 %copy-start.4 = (f32[1024,2048]{1,0:T(8,128)S(1)}, f32[1024,2048]{1,0:T(8,128)}, u32[]{:S(2)}) copy-start(f32[1024,2048]{1,0:T(8,128)} %fusion.3) | copy-start | bytes 25165828
Sparse Core Ops, SparseCore 0:
  9.7 35.7 all-gather.6
  47.2 32.7 all-gather.10
  81.7 32.1 all-gather.8
  199.0 158.0 all-reduce.2
where the time goes:
time: 366 us; the launch traced here: 365 us
  blocking collectives  160 us (44%)
  waiting for transfers between devices  137 us (37%)
  matrix products  44.3 us (12%)
  between operations  13.8 us (4%)
  other arithmetic  6.28 us (2%)
    psum x1, waiting for transfers between devices, per_device(): summed = lax.psum(partial_hidden, ('vocab', 'tok'))  111 us
    pmax x1, blocking collectives, per_device(): row_peak = lax.pmax(local_peak, ('vocab', 'tok'))  65.6 us
    psum x1, blocking collectives, per_device(): exp_total, picked = lax.psum((local_total, picked_part), ('vocab', 'tok'))  64.3 us
    all_gather x1, waiting for transfers between devices, per_device(): lax.all_gather(hidden_states, 'tok', axis=0, tiled=True)  23.8 us
    all_gather x1, blocking collectives, per_device(): lax.all_gather(labels, 'tok', axis=0, tiled=True)  12.2 us
    dot_general x1, matrix products, per_device(): lax.dot_general(whole_hidden, tied_table, (((1,), (1,)), ((), ())), prefe...  10 us
    dot_general x1, matrix products, per_device(): lax.dot_general(logit_grad, whole_hidden, (((0,), (0,)), ((), ())), prefe...  9.57 us
    all_gather x1, blocking collectives, per_device(): lax.all_gather(dec_ids, 'tok', axis=0, tiled=True)  9.31 us
  transfers between devices with their start and end apart: 4, of which 2 were waited for; matrix products, arithmetic and copies ran while one was open for 14% of the time, Pallas kernels for 0%

commit v1 on v0

v1 whole, which is shorter than its diff:
```python
import functools

import jax
import jax.numpy as jnp
from jax import lax
from jax.experimental import pallas as pl
from jax.experimental.pallas import tpu as pltpu
from jax.sharding import PartitionSpec as P

BF = jnp.bfloat16
F32 = jnp.float32
SLOTS = 16
HOPS = (0, 1, 3, 2)


def along_y(x, hop):
    pairs = [(t, ((t // 2 - hop) % 4) * 2 + t % 2) for t in range(8)]
    return lax.ppermute(x, "tok", pairs)


def along_z(x, hop):
    pairs = [(v, (v // 4) * 4 + (v % 4 - hop) % 4) for v in range(16)]
    return lax.ppermute(x, "vocab", pairs)


def along_x(x, hop):
    pairs = [(v, (v - 4 * hop) % 16) for v in range(16)]
    return lax.ppermute(x, "vocab", pairs)


def sibling(x):
    return lax.ppermute(x, "tok", [(t, t ^ 1) for t in range(8)])


def logits_kernel(n, *refs):
    hidden = refs[:n]
    own_ref, sib_ref, label_ref = refs[n : n + 3]
    logits_ref, stats_ref = refs[n + 3 : n + 5]
    grads = refs[n + 5 : 2 * n + 5]
    states, peak, total, picked, acc = refs[2 * n + 5 :]
    phase, step = pl.program_id(0), pl.program_id(1)
    steps = pl.num_programs(1)
    half = steps // 2
    rows = own_ref.shape[0]

    @pl.when((phase == 0) & (step == 0))
    def _():
        for i in range(n):
            states[128 * i : 128 * (i + 1), :] = hidden[i][...]
        peak[...] = jnp.full_like(peak, -jnp.inf)

    def forward(table):
        part = lax.dot_general(
            states[...], table[...], (((1,), (1,)), ((), ())), preferred_element_type=F32
        )
        logits_ref[step] = part
        peak[...] = jnp.maximum(peak[...], jnp.max(part, axis=1, keepdims=True))

    def backward(table, label, first):
        part = logits_ref[step]
        column = lax.broadcasted_iota(jnp.int32, part.shape, 1) + first
        is_label = column == label
        weight = jnp.exp(part - peak[...])
        row_sum = jnp.sum(weight, axis=1, keepdims=True)
        hit = jnp.sum(jnp.where(is_label, part, 0.0), axis=1, keepdims=True)
        masked = jnp.where(is_label, 0.0, weight).astype(BF)
        grad = jnp.dot(masked, table[...], preferred_element_type=F32)

        @pl.when(step == 0)
        def _():
            total[...] = row_sum
            picked[...] = hit
            acc[...] = grad

        @pl.when(step > 0)
        def _():
            total[...] += row_sum
            picked[...] += hit
            acc[...] += grad

    @pl.when((phase == 0) & (step < half))
    def _():
        forward(own_ref)

    @pl.when((phase == 0) & (step >= half))
    def _():
        forward(sib_ref)

    @pl.when((phase == 1) & (step < half))
    def _():
        backward(own_ref, label_ref[:, 0:1], step * rows)

    @pl.when((phase == 1) & (step >= half))
    def _():
        backward(sib_ref, label_ref[:, 1:2], (step - half) * rows)

    @pl.when((phase == 1) & (step == steps - 1))
    def _():
        for i in range(n):
            grads[i][...] = acc[128 * i : 128 * (i + 1), :].astype(BF)
        lane = lax.broadcasted_iota(jnp.int32, (128 * n, 128), 1)
        both = jnp.where(
            lane == 0, peak[...], jnp.where(lane == 1, total[...], jnp.where(lane == 2, picked[...], 0.0))
        )
        stats_ref[...] = both.T[0:8, :]


def logits_and_grads(hidden, own, sib, labels):
    n, width, chunk = len(hidden), own.shape[1], 512
    count = own.shape[0] // chunk
    tokens = 128 * n

    def whole(*shape):
        return pl.BlockSpec(shape, lambda p, j: (0,) * len(shape), pipeline_mode=pl.Buffered(1))

    return pl.pallas_call(
        functools.partial(logits_kernel, n),
        grid=(2, 2 * count),
        in_specs=[whole(128, width)] * n
        + [
            pl.BlockSpec((chunk, width), lambda p, j: (jnp.minimum(j, count - 1), 0)),
            pl.BlockSpec((chunk, width), lambda p, j: (jnp.maximum(j - count, 0), 0)),
            whole(tokens, 2),
        ],
        out_specs=[
            pl.BlockSpec((2 * count, tokens, chunk), lambda p, j: (0, 0, 0)),
            pl.BlockSpec((8, tokens), lambda p, j: (0, 0)),
        ]
        + [pl.BlockSpec((128, width), lambda p, j: (0, 0))] * n,
        out_shape=[
            jax.ShapeDtypeStruct((2 * count, tokens, chunk), F32),
            jax.ShapeDtypeStruct((8, tokens), F32),
        ]
        + [jax.ShapeDtypeStruct((128, width), BF)] * n,
        scratch_shapes=[
            pltpu.VMEM((tokens, width), BF),
            pltpu.VMEM((tokens, 1), F32),
            pltpu.VMEM((tokens, 1), F32),
            pltpu.VMEM((tokens, 1), F32),
            pltpu.VMEM((tokens, width), F32),
        ],
        compiler_params=pltpu.CompilerParams(vmem_limit_bytes=48 << 20),
        cost_estimate=pl.CostEstimate(
            flops=4 * tokens * 4 * chunk * width, bytes_accessed=16 << 20, transcendentals=tokens * 4 * chunk
        ),
    )(*hidden, own, sib, labels)


def table_kernel(p_own, p_sib, h0, h1, h2, h3, h_sib, extra, at_ref, out_ref, states):
    @pl.when(pl.program_id(0) == 0)
    def _():
        for i, h in enumerate((h0, h1, h2, h3)):
            states[128 * i : 128 * (i + 1), :] = h[...]

    dims = (((0,), (0,)), ((), ()))
    rows = out_ref.shape[0]
    row = lax.broadcasted_iota(jnp.int32, (rows, extra.shape[0]), 0) + pl.program_id(0) * rows
    named = jnp.where(row == at_ref[...], 1.0, 0.0).astype(BF)
    out = lax.dot_general(p_own[...], states[...], dims, preferred_element_type=F32)
    out += lax.dot_general(p_sib[...], h_sib[...], dims, preferred_element_type=F32)
    out += jnp.dot(named, extra[...], preferred_element_type=F32)
    out_ref[...] = out


def table_gradient(p_own, p_sib, hidden, h_sib, extra, at):
    tokens, rows = p_own.shape
    width, tile, slots = h_sib.shape[1], 256, extra.shape[0]

    def whole(*shape):
        return pl.BlockSpec(shape, lambda j: (0, 0), pipeline_mode=pl.Buffered(1))

    return pl.pallas_call(
        table_kernel,
        grid=(rows // tile,),
        in_specs=[pl.BlockSpec((tokens, tile), lambda j: (0, j))] * 2
        + [whole(128, width)] * 4
        + [whole(tokens, width), whole(slots, width), whole(1, slots)],
        out_specs=pl.BlockSpec((tile, width), lambda j: (j, 0)),
        out_shape=jax.ShapeDtypeStruct((rows, width), F32),
        scratch_shapes=[pltpu.VMEM((tokens, width), BF)],
        compiler_params=pltpu.CompilerParams(vmem_limit_bytes=40 << 20),
        cost_estimate=pl.CostEstimate(
            flops=2 * rows * (2 * tokens + slots) * width, bytes_accessed=16 << 20, transcendentals=0
        ),
    )(p_own, p_sib, *hidden, h_sib, extra, at)


def ranks(inside):
    n = inside.shape[-1]
    before = jnp.arange(n)[:, None] < jnp.arange(n)[None, :]
    return jnp.einsum(
        "...j,jk->...k", inside.astype(BF), before.astype(BF), preferred_element_type=F32
    ).astype(jnp.int32)


def pick(slot_of, inside, first_slot):
    slots = first_slot + jnp.arange(SLOTS, dtype=jnp.int32)
    return (slot_of[..., None, :] == slots[:, None]) & inside[..., None, :]


def per_device(hidden_states, tied_table, labels, dec_ids, enc_ids, dec_grad, enc_grad):
    row_count, model_width = tied_table.shape
    v, t = lax.axis_index("vocab"), lax.axis_index("tok")
    y, core = t // 2, t % 2
    own_first = (v * 8 + t) * row_count
    sib_first = (v * 8 + (t ^ 1)) * row_count
    chip_rows = 2 * row_count
    chip_first = (v * 4 + y) * chip_rows

    hidden = [hidden_states] + [along_y(hidden_states, h) for h in HOPS[1:]]
    sib_table = sibling(tied_table)

    own_ids = jnp.concatenate([labels[None], dec_ids[None], enc_ids[None], jnp.zeros((5, 128), jnp.int32)])
    ids = jnp.stack([own_ids] + [along_y(own_ids, h) for h in HOPS[1:]])
    ids8 = jnp.concatenate([ids, sibling(ids)])

    lab8 = ids8[:, 0]
    lab_chip = lab8 // chip_rows
    same = lab8[:, :, None] == lab8[:, None, :]
    earlier = jnp.arange(128)[:, None] < jnp.arange(128)[None, :]
    is_first = ~jnp.any(same & earlier[None], axis=1)
    same_chip = lab_chip[:, :, None] == lab_chip[:, None, :]
    first_rank = jnp.sum((same_chip & earlier[None] & is_first[:, :, None]).astype(jnp.int32), axis=1)
    lab_rank = jnp.sum(jnp.where(same & is_first[:, :, None], first_rank[:, :, None], 0), axis=1)
    tok8 = jnp.concatenate([ids8[:, 1], ids8[:, 2]], axis=1)
    tok_chip = tok8 // chip_rows
    tok_inside = tok_chip == v * 4 + y
    tok_rank = ranks(tok_inside)
    all_chips = jnp.arange(64, dtype=jnp.int32)
    tok_most = jnp.max(jnp.sum((tok_chip[:, :, None] == all_chips).astype(jnp.int32), axis=1))
    lab_most = jnp.max(lab_rank) + 1
    lab_rounds = (lab_most + SLOTS - 1) // SLOTS
    tok_rounds = (tok_most + SLOTS - 1) // SLOTS

    own_tok = tok8[0]
    hop_y = jnp.stack([(y + h) % 4 for h in HOPS])
    send_inside = own_tok[None] // chip_rows == (v * 4 + hop_y)[:, None]
    send_rank = ranks(send_inside)
    own_grads = jnp.concatenate([dec_grad, enc_grad])

    def token_rows(first_slot):
        chosen = pick(send_rank, send_inside, first_slot).reshape(4 * SLOTS, 256)
        return jnp.dot(chosen.astype(BF), own_grads, preferred_element_type=F32).astype(BF)

    def token_places(first_slot):
        chosen = pick(tok_rank, tok_inside, first_slot)
        at = jnp.sum(jnp.where(chosen, (tok8 - own_first + row_count * 4)[:, None, :], 0), axis=2)
        return (jnp.where(at == 0, -(1 << 20), at) - row_count * 4).reshape(1, 8 * SLOTS)

    def label_rows(first_slot):
        chosen = pick(lab_rank[:4], (lab_chip[:4] == v * 4 + y) & is_first[:4], first_slot)
        at = jnp.sum(jnp.where(chosen, (lab8[:4] - chip_first + 1)[:, None, :], 0), axis=2) - 1
        at = at.reshape(4 * SLOTS)
        at = jnp.where(at < 0, -(1 << 20), at) + chip_first
        row = jnp.arange(row_count, dtype=jnp.int32)
        from_own = ((at - own_first)[:, None] == row).astype(BF)
        from_sib = ((at - sib_first)[:, None] == row).astype(BF)
        got = jnp.dot(from_own, tied_table, preferred_element_type=F32)
        return (got + jnp.dot(from_sib, sib_table, preferred_element_type=F32)).astype(BF)

    def label_place(rows, first_slot):
        slot = jnp.arange(4 * SLOTS, dtype=jnp.int32)
        source = jnp.repeat(v * 4 + hop_y, SLOTS)
        to = (lab_chip[0][:, None] == source[None]) & (
            lab_rank[0][:, None] == (slot % SLOTS + first_slot)[None]
        )
        return jnp.dot(to.astype(BF), rows, preferred_element_type=F32).astype(BF)

    def exchange(rows):
        return [rows[0]] + [along_y(rows[i], -HOPS[i]) for i in (2, 1, 3)]

    to_send = jnp.concatenate(
        [label_rows(0).reshape(4, SLOTS, -1), token_rows(0).reshape(4, SLOTS, -1)], axis=1
    )
    received = jnp.stack(exchange([to_send[i] for i in range(4)]))
    label_state = label_place(received[:, :SLOTS].reshape(4 * SLOTS, -1), 0)
    tok_received = received[:, SLOTS:].reshape(4 * SLOTS, -1)
    tok_received = jnp.concatenate([tok_received, sibling(tok_received)])

    def more_labels(carry):
        r, state = carry
        rows = label_rows(r * SLOTS).reshape(4, SLOTS, -1)
        got = jnp.concatenate(exchange([rows[i] for i in range(4)]))
        return r + 1, state + label_place(got, r * SLOTS)

    _, label_state = lax.while_loop(lambda c: c[0] < lab_rounds, more_labels, (jnp.int32(1), label_state))

    lab4 = ids[:, 0].reshape(512)
    lab_rel = jnp.stack([lab4 - own_first, lab4 - sib_first], axis=1)
    logits_a, stats_a, grad0, grad1, grad2 = logits_and_grads(hidden[:3], tied_table, sib_table, lab_rel[:384])
    logits_b, stats_b, grad3 = logits_and_grads(hidden[3:], tied_table, sib_table, lab_rel[384:])

    grads = exchange([grad0, grad1, grad2, grad3])

    relative = jnp.concatenate([stats_a, stats_b], axis=1).reshape(8, 4, 128)
    canonical = jnp.stack(
        [
            sum(jnp.where(hop_y[h] == i, relative[:, h], 0.0) for h in range(4))
            for i in range(4)
        ],
        axis=1,
    ).reshape(8, 512)

    def merge(parts):
        peaks = functools.reduce(jnp.maximum, [p[0] for p in parts])
        total = sum(p[1] * jnp.exp(p[0] - peaks) for p in parts)
        return jnp.concatenate(
            [peaks[None], total[None], sum(p[2] for p in parts)[None], jnp.zeros((5, 512), F32)]
        )

    from_y = [canonical] + [along_y(canonical, h) for h in HOPS[1:]]
    stats = merge(from_y)
    stats = merge([stats] + [along_z(stats, h) for h in HOPS[1:]])
    stats = merge([stats] + [along_x(stats, h) for h in HOPS[1:]])
    log_norm, picked = stats[0] + jnp.log(stats[1]), stats[2]

    def mine(x):
        return lax.dynamic_slice_in_dim(x, y * 128, 128)

    my_norm, my_picked = mine(log_norm), mine(picked)
    token_loss = my_norm - my_picked

    scales = jnp.stack([jnp.exp(mine(s[0]) - my_norm) for s in from_y] + [jnp.exp(my_picked - my_norm) - 1.0])
    group_sum = scales[4][:, None] * label_state.astype(F32)
    for i in range(4):
        group_sum = group_sum + scales[i][:, None] * grads[i].astype(F32)
    parts = group_sum.reshape(128, 16, model_width // 16).transpose(1, 0, 2)
    grad_hidden = jnp.sum(lax.all_to_all(parts, "vocab", 0, 0), axis=0)

    norm_rel = jnp.concatenate(
        [lax.dynamic_slice_in_dim(log_norm, hop_y[h] * 128, 128) for h in range(4)]
    )

    def logit_grad(first_chunk, first_row):
        column = jnp.arange(row_count, dtype=jnp.int32) + first_row
        blocks = []
        for logits, lo, hi in ((logits_a, 0, 384), (logits_b, 384, 512)):
            part = logits[first_chunk : first_chunk + 2].transpose(1, 0, 2).reshape(hi - lo, row_count)
            is_label = lab4[lo:hi, None] == column[None]
            blocks.append((jnp.exp(part - norm_rel[lo:hi, None]) - is_label.astype(F32)).astype(BF))
        return jnp.concatenate(blocks)

    p_own = logit_grad(0, own_first)
    p_sib = sibling(logit_grad(2, sib_first))
    hidden_sib = sibling(jnp.concatenate(hidden))
    grad_table = table_gradient(p_own, p_sib, hidden, hidden_sib, tok_received, token_places(0))

    def more_tokens(carry):
        r, grad = carry
        rows = token_rows(r * SLOTS).reshape(4, SLOTS, -1)
        got = jnp.concatenate(exchange([rows[i] for i in range(4)]))
        got = jnp.concatenate([got, sibling(got)])
        named = token_places(r * SLOTS) == jnp.arange(row_count, dtype=jnp.int32)[:, None]
        return r + 1, grad + jnp.dot(named.astype(BF), got, preferred_element_type=F32)

    _, grad_table = lax.while_loop(lambda c: c[0] < tok_rounds, more_tokens, (jnp.int32(1), grad_table))
    return grad_table, grad_hidden, token_loss


def solution(mesh):
    in_specs = (
        P("tok", None),
        P(("vocab", "tok"), None),
        P("tok"),
        P("tok"),
        P("tok"),
        P("tok", None),
        P("tok", None),
    )
    out_specs = (P(("vocab", "tok"), None), P("tok", "vocab"), P("tok"))
    return jax.shard_map(
        per_device, mesh=mesh, in_specs=in_specs, out_specs=out_specs, check_vma=False
    )
```

time: 366 us -> 142 us (0.39)
  the two profiles are of different devices: /device:TPU:1 before, /device:TPU:16 now
where the time goes in v1:
time: 142 us; the launch traced here: 141 us
  starting transfers between devices  44.6 us (31%)
  Pallas kernels  34.1 us (24%)
  other arithmetic  19.9 us (14%)
  waiting for transfers between devices  15.3 us (11%)
  local copies, waits for them, and re-layouts  15.2 us (11%)
  matrix products  9.09 us (6%)
  between operations  2.49 us (2%)
    pallas_call x2, Pallas kernels, logits_and_grads(): pl.pallas_call(functools.partial(logits_kernel, n), grid=(2, 2 * count),...  24.5 us
    ppermute x15, starting transfers between devices, along_y(): return lax.ppermute(x, 'tok', pairs)  23.4 us
    pallas_call x1, Pallas kernels, table_gradient(): pl.pallas_call(table_kernel, grid=(rows // tile,), in_specs=[pl.BlockSpec...  9.57 us
    ppermute x3, starting transfers between devices, along_z(): return lax.ppermute(x, 'vocab', pairs)  7.83 us
    ppermute x3, starting transfers between devices, along_x(): return lax.ppermute(x, 'vocab', pairs)  6.37 us
    all_to_all x1, starting transfers between devices, per_device(): grad_hidden = jnp.sum(lax.all_to_all(parts, 'vocab', 0, 0), axis=0)  5.78 us
    ppermute x15, waiting for transfers between devices, along_y(): return lax.ppermute(x, 'tok', pairs)  5.21 us
    unnamed x37, local copies, waits for them, and re-layouts  5.21 us
  transfers between devices with their start and end apart: 27, of which 6 were waited for; matrix products, arithmetic and copies ran while one was open for 28% of the time, Pallas kernels for 24%

profile of v1, /device:TPU:16, one launch (start us, length us, event | category | flops | bytes accessed | tf_op | source)
XLA Modules:
  0.0 140.8 jit_solution(5588905623149555442)
XLA Ops:
  0.7 0.8 fusion.79
  1.8 2.3 %collective-permute-start.11 = (s32[8,128]{1,0:T(8,128)S(1)}, s32[8,128]{1,0:T(8,128)S(1)}, u32[]{:S(2)}, u32[]{:S(2)}) collective-permute-start(s32[8,128]{1,0:T(8,128)S(1)} %get-tuple-element.508), channel_id=1, source_target_pairs={{0,2},{1,3},{2,4},{3,5},{4,6},{5,7},{6,0},{7,1},{8,10},{9,11},{10,... | collective-permute-start | bytes 12296 | tf_op jit(solution)/shard_map/ppermute | solution.py:18
  4.3 4.0 %collective-permute-start.13 = (bf16[128,2048]{1,0:T(8,128)(2,1)}, bf16[128,2048]{1,0:T(8,128)(2,1)S(1)}, u32[]{:S(2)}, u32[]{:S(2)}) collective-permute-start(bf16[128,2048]{1,0:T(8,128)(2,1)} %h0.1), channel_id=1, source_target_pairs={{0,4},{1,5},{2,6},{3,7},{4,0},{5,1},{6,2},{7,3},{8,12},{9,13},{10,... | collective-permute-start | bytes 1572872 | tf_op jit(solution)/shard_map/ppermute | solution.py:18
  8.3 1.1 constant_dynamic-update-slice_fusion.6
  9.5 1.1 constant_dynamic-update-slice_fusion.5
  10.6 0.7 broadcast_add_fusion.3
  11.3 0.6 and_select_fusion.2
  12.1 0.6 pad.43.clone
  12.8 0.5 slice_bitcast_fusion.9
  13.4 0.6 collective-permute-start.25
  14.3 2.0 %collective-permute-start.7 = (bf16[128,2048]{1,0:T(8,128)(2,1)S(1)}, bf16[128,2048]{1,0:T(8,128)(2,1)S(1)}, u32[]{:S(2)}, u32[]{:S(2)}) collective-permute-start(bf16[128,2048]{1,0:T(8,128)(2,1)S(1)} %copy-done), channel_id=1, source_target_pairs={{0,6},{1,7},{2,0},{3,1},{4,2},{5,3},{6,4},{7,5},{8,14},{9,15},{10,... | collective-permute-start | bytes 1572872 | tf_op jit(solution)/shard_map/ppermute | solution.py:18
  16.3 3.9 %collective-permute-done.25 = s32[4,8,128]{2,0,1:T(4,128)S(1)} collective-permute-done((s32[4,8,128]{2,0,1:T(4,128)S(1)}, s32[4,8,128]{2,0,1:T(4,128)S(1)}, u32[]{:S(2)}, u32[]{:S(2)}) %collective-permute-start.25) | collective-permute-done | bytes 16416 | tf_op jit(solution)/shard_map/ppermute | solution.py:32
  20.5 0.3 convert_reduce_fusion.1
  20.8 0.6 select_reduce_fusion.2
  21.4 0.6 reduce_max.19
  23.0 0.6 reduce_max.18
  24.9 0.6 reduce_sum.86
  25.9 1.5 %convolution_convert_fusion.3 = bf16[64,2048]{1,0:T(8,128)(2,1)S(1)} fusion(pred[64,256]{1,0:T(32,128)(4,1)S(1)} %fusion.40, bf16[256,2048]{1,0:T(8,128)(2,1)} %copy-done.4), kind=kOutput, calls=%fused_computation.61 | convolution fusion | flops 67239936 | bytes 1327104 | tf_op jit(solution)/shard_map/dot_general | solution.py:243
  27.4 3.1 %fusion.30 = f32[64,2048]{1,0:T(8,128)S(1)} fusion(bf16[1024,2048]{1,0:T(8,128)(2,1)} %refs_1_.1, s32[64]{0:T(128)S(1)} %get-tuple-element.517), kind=kOutput, calls=%fused_computation.95 | convolution fusion | flops 268500992 | bytes 4718848 | tf_op jit(solution)/shard_map/dot_general | solution.py:258
  30.5 0.3 collective-permute-done.8.refs_2_.h2
  30.8 1.5 %pad_maximum_fusion.1 = bf16[512,2048]{1,0:T(8,128)(2,1)} fusion(bf16[128,2048]{1,0:T(8,128)(2,1)S(1)} %collective-permute-done.13.refs_0_.h3, bf16[128,2048]{1,0:T(8,128)(2,1)S(1)} %collective-permute-done.8.refs_2_.h2, bf16[128,2048]{1,0:T(8,128)(2,1)S(1)} %collective-permute-done.7.refs_1_.h1, bf16[128,2048]{1,0:T(8,128)(2,1)S(1)} %copy-done), kind=kLoop, calls=%fused_computation.62 | loop fusion | flops 8388608 | bytes 4194304 | tf_op jit(solution)/shard_map/concatenate | solution.py:345
  32.4 1.0 copy-done.3
  33.4 9.8 %shard_map.95 = (f32[4,128,512]{2,1,0:T(8,128)S(1)}, f32[8,128]{1,0:T(8,128)S(1)}, bf16[128,2048]{1,0:T(8,128)(2,1)S(1)}) custom-call(bf16[128,2048]{1,0:T(8,128)(2,1)S(1)} %collective-permute-done.13.refs_0_.h3, bf16[1024,2048]{1,0:T(8,128)(2,1)S(1)} %copy-done.3, bf16[1024,2048]{1,0:T(8,128)(2,1)} %collective-permute-done.9.refs_4_.refs_2_, ...), custom_call_target="tpu_custom_call" | custom-call | flops 2147483648 | bytes 16777216 | tf_op jit(solution)/shard_map/pallas_call | solution.py:116
  43.3 14.7 %shard_map.94 = (f32[4,384,512]{2,1,0:T(8,128)}, f32[8,384]{1,0:T(8,128)S(1)}, bf16[128,2048]{1,0:T(8,128)(2,1)S(1)}, bf16[128,2048]{1,0:T(8,128)(2,1)S(1)}, bf16[128,2048]{1,0:T(8,128)(2,1)S(1)}) custom-call(bf16[128,2048]{1,0:T(8,128)(2,1)S(1)} %copy-done, bf16[128,2048]{1,0:T(8,128)(2,1)S(1)} %collective-permute-done.7.refs_1_.h1, ...), custom_call_target="tpu_custom_call" | custom-call | flops 6442450944 | bytes 16777216 | tf_op jit(solution)/shard_map/pallas_call | solution.py:116
  58.0 2.3 %collective-permute-start.16 = (f32[8,512]{1,0:T(8,128)S(1)}, f32[8,512]{1,0:T(8,128)S(1)}, u32[]{:S(2)}, u32[]{:S(2)}) collective-permute-start(f32[8,512]{1,0:T(8,128)S(1)} %get-tuple-element.494), channel_id=1, source_target_pairs={{0,4},{1,5},{2,6},{3,7},{4,0},{5,1},{6,2},{7,3},{8,12},{9,13},{10,... | collective-permute-start | bytes 49160 | tf_op jit(solution)/shard_map/ppermute | solution.py:18
  60.3 1.8 %collective-permute-start.15 = (f32[8,512]{1,0:T(8,128)S(1)}, f32[8,512]{1,0:T(8,128)S(1)}, u32[]{:S(2)}, u32[]{:S(2)}) collective-permute-start(f32[8,512]{1,0:T(8,128)S(1)} %get-tuple-element.494), channel_id=1, source_target_pairs={{0,2},{1,3},{2,4},{3,5},{4,6},{5,7},{6,0},{7,1},{8,10},{9,11},{10,... | collective-permute-start | bytes 49160 | tf_op jit(solution)/shard_map/ppermute | solution.py:18
  62.4 2.2 %slice_bitcast_fusion.2 = (f32[2,48,8,512]{3,2,1,0:T(8,128)S(1)}, f32[2,48,8,512]{3,2,1,0:T(8,128)S(1)}) fusion(f32[4,384,512]{2,1,0:T(8,128)} %get-tuple-element.333), kind=kLoop, calls=%fused_computation.64 | loop fusion | bytes 6291456
  64.6 3.1 %fusion.28 = bf16[64,2048]{1,0:T(8,128)(2,1)S(1)} fusion(f32[64,2048]{1,0:T(8,128)S(1)} %fusion.30, bf16[1024,2048]{1,0:T(8,128)(2,1)} %collective-permute-done.9.refs_4_.refs_2_, s32[64]{0:T(128)S(1)} %get-tuple-element.516), kind=kOutput, calls=%fused_computation.60 | convolution fusion | flops 268763136 | bytes 4980992 | tf_op jit(solution)/shard_map/dot_general | solution.py:259
  67.8 1.3 copy.63
  69.1 0.9 copy.64
  70.0 0.8 copy.62
  70.8 1.3 copy.61
  72.1 3.9 %collective-permute-start.28 = (bf16[32,2048]{1,0:T(8,128)(2,1)S(1)}, bf16[32,2048]{1,0:T(8,128)(2,1)S(1)}, u32[]{:S(2)}, u32[]{:S(2)}) collective-permute-start(bf16[32,2048]{1,0:T(8,128)(2,1)S(1)} %get-tuple-element.451), channel_id=1, source_target_pairs={{0,4},{1,5},{2,6},{3,7},{4,0},{5,1},{6,2},{7,3},{8,12},{9,13},{10,... | collective-permute-start | bytes 393224 | tf_op jit(solution)/shard_map/ppermute | solution.py:18
  76.0 1.3 collective-permute-start.27
  77.4 0.6 copy-done.11
  78.0 3.9 %collective-permute-start.19 = (f32[8,512]{1,0:T(8,128)S(1)}, f32[8,512]{1,0:T(8,128)}, u32[]{:S(2)}, u32[]{:S(2)}) collective-permute-start(f32[8,512]{1,0:T(8,128)S(1)} %maximum_maximum_fusion), channel_id=1, source_target_pairs={{0,16},{8,24},{16,0},{24,8},{32,48},{40,56},{48,32},{56,40},{64,80... | collective-permute-start | bytes 49160 | tf_op jit(solution)/shard_map/ppermute | solution.py:23
  82.0 0.7 fusion.84
  82.7 1.2 convolution_convert_fusion.2
  83.9 1.8 %collective-permute-start.18 = (f32[8,512]{1,0:T(8,128)S(1)}, f32[8,512]{1,0:T(8,128)S(1)}, u32[]{:S(2)}, u32[]{:S(2)}) collective-permute-start(f32[8,512]{1,0:T(8,128)S(1)} %maximum_maximum_fusion), channel_id=1, source_target_pairs={{0,8},{8,16},{16,24},{24,0},{32,40},{40,48},{48,56},{56,32},{64,72... | collective-permute-start | bytes 49160 | tf_op jit(solution)/shard_map/ppermute | solution.py:23
  85.7 2.1 %collective-permute-start.17 = (f32[8,512]{1,0:T(8,128)S(1)}, f32[8,512]{1,0:T(8,128)S(1)}, u32[]{:S(2)}, u32[]{:S(2)}) collective-permute-start(f32[8,512]{1,0:T(8,128)S(1)} %maximum_maximum_fusion), channel_id=1, source_target_pairs={{0,24},{8,0},{16,8},{24,16},{32,56},{40,32},{48,40},{56,48},{64,88... | collective-permute-start | bytes 49160 | tf_op jit(solution)/shard_map/ppermute | solution.py:23
  87.8 0.8 fusion.89
  88.6 0.5 collective-permute-start.30
  89.1 1.5 %collective-permute-start.31 = (bf16[128,2048]{1,0:T(8,128)(2,1)}, bf16[128,2048]{1,0:T(8,128)(2,1)S(1)}, u32[]{:S(2)}, u32[]{:S(2)}) collective-permute-start(bf16[128,2048]{1,0:T(8,128)(2,1)} %copy-done.1), channel_id=1, source_target_pairs={{0,2},{1,3},{2,4},{3,5},{4,6},{5,7},{6,0},{7,1},{8,10},{9,11},{10,... | collective-permute-start | bytes 1572872 | tf_op jit(solution)/shard_map/ppermute | solution.py:18
  90.6 0.9 maximum_maximum_fusion.2
  91.5 0.7 maximum_maximum_fusion.1
  92.2 3.0 %collective-permute-start.22 = (f32[8,512]{1,0:T(8,128)S(1)}, f32[8,512]{1,0:T(8,128)S(1)}, u32[]{:S(2)}, u32[]{:S(2)}) collective-permute-start(f32[8,512]{1,0:T(8,128)S(1)} %maximum_maximum_fusion.1), channel_id=1, source_target_pairs={{0,64},{8,72},{16,80},{24,88},{32,96},{40,104},{48,112},{56,120},{... | collective-permute-start | bytes 49160 | tf_op jit(solution)/shard_map/ppermute | solution.py:28
  95.3 0.8 fusion.91
  96.1 0.7 collective-permute-start.21
  96.7 0.8 collective-permute-done.22
  97.6 2.7 %collective-permute-start.20 = (f32[8,512]{1,0:T(8,128)S(1)}, f32[8,512]{1,0:T(8,128)S(1)}, u32[]{:S(2)}, u32[]{:S(2)}) collective-permute-start(f32[8,512]{1,0:T(8,128)S(1)} %maximum_maximum_fusion.1), channel_id=1, source_target_pairs={{0,96},{8,104},{16,112},{24,120},{32,0},{40,8},{48,16},{56,24},{64... | collective-permute-start | bytes 49160 | tf_op jit(solution)/shard_map/ppermute | solution.py:28
  100.2 0.9 collective-permute-done.21
  101.1 3.0 %collective-permute-start.32 = (bf16[128,2048]{1,0:T(8,128)(2,1)S(1)}, bf16[128,2048]{1,0:T(8,128)(2,1)S(1)}, u32[]{:S(2)}, u32[]{:S(2)}) collective-permute-start(bf16[128,2048]{1,0:T(8,128)(2,1)S(1)} %get-tuple-element.342), channel_id=1, source_target_pairs={{0,4},{1,5},{2,6},{3,7},{4,0},{5,1},{6,2},{7,3},{8,12},{9,13},{10,... | collective-permute-start | bytes 1572872 | tf_op jit(solution)/shard_map/ppermute | solution.py:18
  104.2 0.6 dynamic-slice_subtract_fusion
  104.8 3.6 %subtract_convert_fusion = (bf16[384,1024]{1,0:T(8,128)(2,1)S(1)}, bf16[384,1024]{1,0:T(8,128)(2,1)}) fusion(f32[384,1024]{1,0:T(8,128)} %bitcast.201, s32[1024]{0:T(1024)S(1)} %get-tuple-element.518, f32[384]{0:T(512)S(1)} %pad_maximum_fusion.8, s32[384]{0:T(512)S(1)} %bitcast.233, s32[1024]{0:T(1024)S(1)} %get-tuple-element.519, f32[384,1024]{1,0:T(8,128)} %bitcast.202), kind=kLoop, calls=%fused_computation.63 | loop fusion | flops 3932160 | bytes 4729856 | tf_op jit(solution)/shard_map/convert_element_type | solution.py:340
  108.5 1.0 subtract_convert_fusion.2
  109.5 1.0 pad_maximum_fusion.3
  110.7 0.6 collective-permute-start.29
  111.2 4.9 %collective-permute-done.32 = bf16[128,2048]{1,0:T(8,128)(2,1)S(1)} collective-permute-done((bf16[128,2048]{1,0:T(8,128)(2,1)S(1)}, bf16[128,2048]{1,0:T(8,128)(2,1)S(1)}, u32[]{:S(2)}, u32[]{:S(2)}) %collective-permute-start.32) | collective-permute-done | bytes 524320 | tf_op jit(solution)/shard_map/ppermute | solution.py:18
  116.1 1.6 %bitcast_bitcast_fusion = f32[16,128,128]{2,1,0:T(8,128)} fusion(bf16[128,2048]{1,0:T(8,128)(2,1)S(1)} %collective-permute-done.32, bf16[128,2048]{1,0:T(8,128)(2,1)S(1)} %collective-permute-done.31, bf16[128,2048]{1,0:T(8,128)(2,1)S(1)} %collective-permute-done.30, bf16[128,2048]{1,0:T(8,128)(2,1)S(1)} %get-tuple-element.339, ...), kind=kLoop, calls=%fused_computation.69 | loop fusion | flops 3670016 | bytes 3672576 | tf_op jit(solution)/shard_map/transpose | solution.py:327
  117.7 5.8 %all-to-all-start = ((f32[16,128,128]{2,1,0:T(8,128)}), f32[16,128,128]{2,1,0:T(8,128)}, u32[]{:S(2)}, u32[]{:S(2)}) async-start(f32[16,128,128]{2,1,0:T(8,128)} %bitcast_bitcast_fusion), calls=%async_computation | async-start | bytes 2097152 | tf_op jit(solution)/shard_map/all_to_all | solution.py:328
  123.6 1.1 pad_maximum_fusion.5.extra
  124.7 9.6 %shard_map.96 = f32[1024,2048]{1,0:T(8,128)} custom-call(bf16[512,1024]{1,0:T(8,128)(2,1)S(1)} %pad_maximum_fusion.2.p_own, bf16[512,1024]{1,0:T(8,128)(2,1)} %collective-permute-done.23.p_sib, bf16[128,2048]{1,0:T(8,128)(2,1)S(1)} %copy-done, bf16[128,2048]{1,0:T(8,128)(2,1)S(1)} %collective-permute-done.7.refs_1_.h1, ...), custom_call_target="tpu_custom_call" | custom-call | flops 4831838208 | bytes 16777216 | tf_op jit(solution)/shard_map/pallas_call | solution.py:172
  134.3 4.5 %all-to-all-done = f32[16,128,128]{2,1,0:T(8,128)} async-done(((f32[16,128,128]{2,1,0:T(8,128)}), f32[16,128,128]{2,1,0:T(8,128)}, u32[]{:S(2)}, u32[]{:S(2)}) %all-to-all-start) | async-done | bytes 1048608 | tf_op jit(solution)/shard_map/all_to_all | solution.py:328
  138.8 1.9 %reduce_sum.88 = f32[128,128]{1,0:T(8,128)} reduce(f32[16,128,128]{2,1,0:T(8,128)} %all-to-all-done, f32[]{:T(128)} %constant.213.clone.1), dimensions={0}, to_apply=%region_14.15 | reduce | flops 245760 | bytes 1114116 | tf_op jit(solution)/shard_map/reduce_sum | solution.py:328
  (119 shorter events, 3.6 us)
Async XLA Ops:
  0.6 12.1 %copy-start = (bf16[128,2048]{1,0:T(8,128)(2,1)S(1)}, bf16[128,2048]{1,0:T(8,128)(2,1)}, u32[]{:S(2)}) copy-start(bf16[128,2048]{1,0:T(8,128)(2,1)} %h0.1) | copy-start | bytes 1572868
  1.5 11.3 %collective-permute-start.12 = (s32[8,128]{1,0:T(8,128)S(1)}, s32[8,128]{1,0:T(8,128)S(1)}, u32[]{:S(2)}, u32[]{:S(2)}) collective-permute-start(s32[8,128]{1,0:T(8,128)S(1)} %get-tuple-element.508), channel_id=1, source_target_pairs={{0,4},{1,5},{2,6},{3,7},{4,0},{5,1},{6,2},{7,3},{8,12},{9,13},{10,... | collective-permute-start | bytes 12296 | tf_op jit(solution)/shard_map/ppermute | solution.py:18
  1.8 11.6 %collective-permute-start.11 = (s32[8,128]{1,0:T(8,128)S(1)}, s32[8,128]{1,0:T(8,128)S(1)}, u32[]{:S(2)}, u32[]{:S(2)}) collective-permute-start(s32[8,128]{1,0:T(8,128)S(1)} %get-tuple-element.508), channel_id=1, source_target_pairs={{0,2},{1,3},{2,4},{3,5},{4,6},{5,7},{6,0},{7,1},{8,10},{9,11},{10,... | collective-permute-start | bytes 12296 | tf_op jit(solution)/shard_map/ppermute | solution.py:18
  4.1 9.3 %collective-permute-start.10 = (s32[8,128]{1,0:T(8,128)S(1)}, s32[8,128]{1,0:T(8,128)S(1)}, u32[]{:S(2)}, u32[]{:S(2)}) collective-permute-start(s32[8,128]{1,0:T(8,128)S(1)} %get-tuple-element.508), channel_id=1, source_target_pairs={{0,6},{1,7},{2,0},{3,1},{4,2},{5,3},{6,4},{7,5},{8,14},{9,15},{10,... | collective-permute-start | bytes 12296 | tf_op jit(solution)/shard_map/ppermute | solution.py:18
  4.3 26.2 %collective-permute-start.13 = (bf16[128,2048]{1,0:T(8,128)(2,1)}, bf16[128,2048]{1,0:T(8,128)(2,1)S(1)}, u32[]{:S(2)}, u32[]{:S(2)}) collective-permute-start(bf16[128,2048]{1,0:T(8,128)(2,1)} %h0.1), channel_id=1, source_target_pairs={{0,4},{1,5},{2,6},{3,7},{4,0},{5,1},{6,2},{7,3},{8,12},{9,13},{10,... | collective-permute-start | bytes 1572872 | tf_op jit(solution)/shard_map/ppermute | solution.py:18
  10.5 1.6 %copy-start.4 = (bf16[256,2048]{1,0:T(8,128)(2,1)}, bf16[256,2048]{1,0:T(8,128)(2,1)S(1)}, u32[]{:S(2)}) copy-start(bf16[256,2048]{1,0:T(8,128)(2,1)S(1)} %constant_dynamic-update-slice_fusion.5) | copy-start | bytes 3145732
  12.7 18.1 %collective-permute-start.8 = (bf16[128,2048]{1,0:T(8,128)(2,1)S(1)}, bf16[128,2048]{1,0:T(8,128)(2,1)S(1)}, u32[]{:S(2)}, u32[]{:S(2)}) collective-permute-start(bf16[128,2048]{1,0:T(8,128)(2,1)S(1)} %copy-done), channel_id=1, source_target_pairs={{0,2},{1,3},{2,4},{3,5},{4,6},{5,7},{6,0},{7,1},{8,10},{9,11},{10,... | collective-permute-start | bytes 1572872 | tf_op jit(solution)/shard_map/ppermute | solution.py:18
  13.3 19.1 %collective-permute-start.9 = (bf16[1024,2048]{1,0:T(8,128)(2,1)}, bf16[1024,2048]{1,0:T(8,128)(2,1)}, u32[]{:S(2)}, u32[]{:S(2)}) collective-permute-start(bf16[1024,2048]{1,0:T(8,128)(2,1)} %refs_1_.1), channel_id=1, source_target_pairs={{0,1},{1,0},{2,3},{3,2},{4,5},{5,4},{6,7},{7,6},{8,9},{9,8},{10,11... | collective-permute-start | bytes 12582920 | tf_op jit(solution)/shard_map/ppermute | solution.py:32
  13.4 6.8 %collective-permute-start.25 = (s32[4,8,128]{2,0,1:T(4,128)S(1)}, s32[4,8,128]{2,0,1:T(4,128)S(1)}, u32[]{:S(2)}, u32[]{:S(2)}) collective-permute-start(s32[4,8,128]{2,0,1:T(4,128)S(1)} %pad_add_fusion), channel_id=1, source_target_pairs={{0,1},{1,0},{2,3},{3,2},{4,5},{5,4},{6,7},{7,6},{8,9},{9,8},{10,11... | collective-permute-start | bytes 49160 | tf_op jit(solution)/shard_map/ppermute | solution.py:32
  14.3 16.6 %collective-permute-start.7 = (bf16[128,2048]{1,0:T(8,128)(2,1)S(1)}, bf16[128,2048]{1,0:T(8,128)(2,1)S(1)}, u32[]{:S(2)}, u32[]{:S(2)}) collective-permute-start(bf16[128,2048]{1,0:T(8,128)(2,1)S(1)} %copy-done), channel_id=1, source_target_pairs={{0,6},{1,7},{2,0},{3,1},{4,2},{5,3},{6,4},{7,5},{8,14},{9,15},{10,... | collective-permute-start | bytes 1572872 | tf_op jit(solution)/shard_map/ppermute | solution.py:18
  30.5 2.9 %copy-start.3 = (bf16[1024,2048]{1,0:T(8,128)(2,1)S(1)}, bf16[1024,2048]{1,0:T(8,128)(2,1)}, u32[]{:S(2)}) copy-start(bf16[1024,2048]{1,0:T(8,128)(2,1)} %refs_1_.1) | copy-start | bytes 12582916
  32.4 92.3 %collective-permute-start.24 = (bf16[512,2048]{1,0:T(8,128)(2,1)}, bf16[512,2048]{1,0:T(8,128)(2,1)}, u32[]{:S(2)}, u32[]{:S(2)}) collective-permute-start(bf16[512,2048]{1,0:T(8,128)(2,1)} %pad_maximum_fusion.1), channel_id=1, source_target_pairs={{0,1},{1,0},{2,3},{3,2},{4,5},{5,4},{6,7},{7,6},{8,9},{9,8},{10,11... | collective-permute-start | bytes 6291464 | tf_op jit(solution)/shard_map/ppermute | solution.py:32
  58.0 6.6 %copy-start.1 = (bf16[128,2048]{1,0:T(8,128)(2,1)}, bf16[128,2048]{1,0:T(8,128)(2,1)S(1)}, u32[]{:S(2)}) copy-start(bf16[128,2048]{1,0:T(8,128)(2,1)S(1)} %get-tuple-element.341) | copy-start | bytes 1572868
  58.0 6.6 %copy-start.2 = (bf16[128,2048]{1,0:T(8,128)(2,1)}, bf16[128,2048]{1,0:T(8,128)(2,1)S(1)}, u32[]{:S(2)}) copy-start(bf16[128,2048]{1,0:T(8,128)(2,1)S(1)} %get-tuple-element.340) | copy-start | bytes 1572868
  58.0 14.1 %collective-permute-start.16 = (f32[8,512]{1,0:T(8,128)S(1)}, f32[8,512]{1,0:T(8,128)S(1)}, u32[]{:S(2)}, u32[]{:S(2)}) collective-permute-start(f32[8,512]{1,0:T(8,128)S(1)} %get-tuple-element.494), channel_id=1, source_target_pairs={{0,4},{1,5},{2,6},{3,7},{4,0},{5,1},{6,2},{7,3},{8,12},{9,13},{10,... | collective-permute-start | bytes 49160 | tf_op jit(solution)/shard_map/ppermute | solution.py:18
  60.3 15.7 %collective-permute-start.15 = (f32[8,512]{1,0:T(8,128)S(1)}, f32[8,512]{1,0:T(8,128)S(1)}, u32[]{:S(2)}, u32[]{:S(2)}) collective-permute-start(f32[8,512]{1,0:T(8,128)S(1)} %get-tuple-element.494), channel_id=1, source_target_pairs={{0,2},{1,3},{2,4},{3,5},{4,6},{5,7},{6,0},{7,1},{8,10},{9,11},{10,... | collective-permute-start | bytes 49160 | tf_op jit(solution)/shard_map/ppermute | solution.py:18
  62.2 15.2 %collective-permute-start.14 = (f32[8,512]{1,0:T(8,128)S(1)}, f32[8,512]{1,0:T(8,128)S(1)}, u32[]{:S(2)}, u32[]{:S(2)}) collective-permute-start(f32[8,512]{1,0:T(8,128)S(1)} %get-tuple-element.494), channel_id=1, source_target_pairs={{0,6},{1,7},{2,0},{3,1},{4,2},{5,3},{6,4},{7,5},{8,14},{9,15},{10,... | collective-permute-start | bytes 49160 | tf_op jit(solution)/shard_map/ppermute | solution.py:18
  70.0 8.0 %copy-start.12 = (f32[8]{0:T(128)S(1)}, f32[8]{0:T(128)}, u32[]{:S(2)}) copy-start(f32[8]{0:T(128)} %pad.43.clone) | copy-start | bytes 100
  70.8 11.9 %copy-start.14 = (s32[64]{0:T(128)S(1)}, s32[64]{0:T(128)}, u32[]{:S(2)}) copy-start(s32[64]{0:T(128)} %and_select_fusion.2) | copy-start | bytes 772
  72.1 9.8 %collective-permute-start.26 = (bf16[32,2048]{1,0:T(8,128)(2,1)S(1)}, bf16[32,2048]{1,0:T(8,128)(2,1)S(1)}, u32[]{:S(2)}, u32[]{:S(2)}) collective-permute-start(bf16[32,2048]{1,0:T(8,128)(2,1)S(1)} %get-tuple-element.450), channel_id=1, source_target_pairs={{0,6},{1,7},{2,0},{3,1},{4,2},{5,3},{6,4},{7,5},{8,14},{9,15},{10,... | collective-permute-start | bytes 393224 | tf_op jit(solution)/shard_map/ppermute | solution.py:18
  72.1 9.8 %collective-permute-start.28 = (bf16[32,2048]{1,0:T(8,128)(2,1)S(1)}, bf16[32,2048]{1,0:T(8,128)(2,1)S(1)}, u32[]{:S(2)}, u32[]{:S(2)}) collective-permute-start(bf16[32,2048]{1,0:T(8,128)(2,1)S(1)} %get-tuple-element.451), channel_id=1, source_target_pairs={{0,4},{1,5},{2,6},{3,7},{4,0},{5,1},{6,2},{7,3},{8,12},{9,13},{10,... | collective-permute-start | bytes 393224 | tf_op jit(solution)/shard_map/ppermute | solution.py:18
  76.0 5.9 %collective-permute-start.27 = (bf16[32,2048]{1,0:T(8,128)(2,1)S(1)}, bf16[32,2048]{1,0:T(8,128)(2,1)S(1)}, u32[]{:S(2)}, u32[]{:S(2)}) collective-permute-start(bf16[32,2048]{1,0:T(8,128)(2,1)S(1)} %get-tuple-element.452), channel_id=1, source_target_pairs={{0,2},{1,3},{2,4},{3,5},{4,6},{5,7},{6,0},{7,1},{8,10},{9,11},{10,... | collective-permute-start | bytes 393224 | tf_op jit(solution)/shard_map/ppermute | solution.py:18
  77.3 0.6 copy-start.11
  78.0 11.1 %collective-permute-start.19 = (f32[8,512]{1,0:T(8,128)S(1)}, f32[8,512]{1,0:T(8,128)}, u32[]{:S(2)}, u32[]{:S(2)}) collective-permute-start(f32[8,512]{1,0:T(8,128)S(1)} %maximum_maximum_fusion), channel_id=1, source_target_pairs={{0,16},{8,24},{16,0},{24,8},{32,48},{40,56},{48,32},{56,40},{64,80... | collective-permute-start | bytes 49160 | tf_op jit(solution)/shard_map/ppermute | solution.py:23
  83.9 6.7 %collective-permute-start.18 = (f32[8,512]{1,0:T(8,128)S(1)}, f32[8,512]{1,0:T(8,128)S(1)}, u32[]{:S(2)}, u32[]{:S(2)}) collective-permute-start(f32[8,512]{1,0:T(8,128)S(1)} %maximum_maximum_fusion), channel_id=1, source_target_pairs={{0,8},{8,16},{16,24},{24,0},{32,40},{40,48},{48,56},{56,32},{64,72... | collective-permute-start | bytes 49160 | tf_op jit(solution)/shard_map/ppermute | solution.py:23
  85.7 5.0 %collective-permute-start.17 = (f32[8,512]{1,0:T(8,128)S(1)}, f32[8,512]{1,0:T(8,128)S(1)}, u32[]{:S(2)}, u32[]{:S(2)}) collective-permute-start(f32[8,512]{1,0:T(8,128)S(1)} %maximum_maximum_fusion), channel_id=1, source_target_pairs={{0,24},{8,0},{16,8},{24,16},{32,56},{40,32},{48,40},{56,48},{64,88... | collective-permute-start | bytes 49160 | tf_op jit(solution)/shard_map/ppermute | solution.py:23
  88.6 22.0 %collective-permute-start.30 = (bf16[128,2048]{1,0:T(8,128)(2,1)}, bf16[128,2048]{1,0:T(8,128)(2,1)S(1)}, u32[]{:S(2)}, u32[]{:S(2)}) collective-permute-start(bf16[128,2048]{1,0:T(8,128)(2,1)} %copy-done.2), channel_id=1, source_target_pairs={{0,6},{1,7},{2,0},{3,1},{4,2},{5,3},{6,4},{7,5},{8,14},{9,15},{10,... | collective-permute-start | bytes 1572872 | tf_op jit(solution)/shard_map/ppermute | solution.py:18
  89.1 22.1 %collective-permute-start.31 = (bf16[128,2048]{1,0:T(8,128)(2,1)}, bf16[128,2048]{1,0:T(8,128)(2,1)S(1)}, u32[]{:S(2)}, u32[]{:S(2)}) collective-permute-start(bf16[128,2048]{1,0:T(8,128)(2,1)} %copy-done.1), channel_id=1, source_target_pairs={{0,2},{1,3},{2,4},{3,5},{4,6},{5,7},{6,0},{7,1},{8,10},{9,11},{10,... | collective-permute-start | bytes 1572872 | tf_op jit(solution)/shard_map/ppermute | solution.py:18
  92.2 5.3 %collective-permute-start.22 = (f32[8,512]{1,0:T(8,128)S(1)}, f32[8,512]{1,0:T(8,128)S(1)}, u32[]{:S(2)}, u32[]{:S(2)}) collective-permute-start(f32[8,512]{1,0:T(8,128)S(1)} %maximum_maximum_fusion.1), channel_id=1, source_target_pairs={{0,64},{8,72},{16,80},{24,88},{32,96},{40,104},{48,112},{56,120},{... | collective-permute-start | bytes 49160 | tf_op jit(solution)/shard_map/ppermute | solution.py:28
  96.1 5.0 %collective-permute-start.21 = (f32[8,512]{1,0:T(8,128)S(1)}, f32[8,512]{1,0:T(8,128)S(1)}, u32[]{:S(2)}, u32[]{:S(2)}) collective-permute-start(f32[8,512]{1,0:T(8,128)S(1)} %maximum_maximum_fusion.1), channel_id=1, source_target_pairs={{0,32},{8,40},{16,48},{24,56},{32,64},{40,72},{48,80},{56,88},{64,... | collective-permute-start | bytes 49160 | tf_op jit(solution)/shard_map/ppermute | solution.py:28
  97.6 6.6 %collective-permute-start.20 = (f32[8,512]{1,0:T(8,128)S(1)}, f32[8,512]{1,0:T(8,128)S(1)}, u32[]{:S(2)}, u32[]{:S(2)}) collective-permute-start(f32[8,512]{1,0:T(8,128)S(1)} %maximum_maximum_fusion.1), channel_id=1, source_target_pairs={{0,96},{8,104},{16,112},{24,120},{32,0},{40,8},{48,16},{56,24},{64... | collective-permute-start | bytes 49160 | tf_op jit(solution)/shard_map/ppermute | solution.py:28
  101.1 15.0 %collective-permute-start.32 = (bf16[128,2048]{1,0:T(8,128)(2,1)S(1)}, bf16[128,2048]{1,0:T(8,128)(2,1)S(1)}, u32[]{:S(2)}, u32[]{:S(2)}) collective-permute-start(bf16[128,2048]{1,0:T(8,128)(2,1)S(1)} %get-tuple-element.342), channel_id=1, source_target_pairs={{0,4},{1,5},{2,6},{3,7},{4,0},{5,1},{6,2},{7,3},{8,12},{9,13},{10,... | collective-permute-start | bytes 1572872 | tf_op jit(solution)/shard_map/ppermute | solution.py:18
  104.8 3.7 %copy-start.8 = (f32[2,16,8,512]{3,2,0,1:T(8,128)S(1)}, f32[2,16,8,512]{3,2,0,1:T(8,128)}, u32[]{:S(2)}) copy-start(f32[2,16,8,512]{3,2,0,1:T(8,128)} %copy.64) | copy-start | bytes 1572868
  104.8 3.7 %copy-start.9 = (f32[2,16,8,512]{3,2,0,1:T(8,128)S(1)}, f32[2,16,8,512]{3,2,0,1:T(8,128)}, u32[]{:S(2)}) copy-start(f32[2,16,8,512]{3,2,0,1:T(8,128)} %copy.62) | copy-start | bytes 1572868
  104.8 3.7 %copy-start.13 = (s32[128]{0:T(128)S(1)}, s32[128]{0:T(128)}, u32[]{:S(2)}) copy-start(s32[128]{0:T(128)} %slice_bitcast_fusion.9) | copy-start | bytes 1540
  108.5 7.6 %copy-start.7 = (bf16[128,2048]{1,0:T(8,128)(2,1)S(1)}, bf16[128,2048]{1,0:T(8,128)(2,1)}, u32[]{:S(2)}) copy-start(bf16[128,2048]{1,0:T(8,128)(2,1)} %get-tuple-element.338) | copy-start | bytes 1572868
  110.6 14.2 %collective-permute-start.23 = (bf16[512,1024]{1,0:T(8,128)(2,1)}, bf16[512,1024]{1,0:T(8,128)(2,1)}, u32[]{:S(2)}, u32[]{:S(2)}) collective-permute-start(bf16[512,1024]{1,0:T(8,128)(2,1)} %pad_maximum_fusion.3), channel_id=1, source_target_pairs={{0,1},{1,0},{2,3},{3,2},{4,5},{5,4},{6,7},{7,6},{8,9},{9,8},{10,11... | collective-permute-start | bytes 3145736 | tf_op jit(solution)/shard_map/ppermute | solution.py:32
  110.7 13.0 %collective-permute-start.29 = (bf16[64,2048]{1,0:T(8,128)(2,1)}, bf16[64,2048]{1,0:T(8,128)(2,1)}, u32[]{:S(2)}, u32[]{:S(2)}) collective-permute-start(bf16[64,2048]{1,0:T(8,128)(2,1)} %bitcast.67), channel_id=1, source_target_pairs={{0,1},{1,0},{2,3},{3,2},{4,5},{5,4},{6,7},{7,6},{8,9},{9,8},{10,11... | collective-permute-start | bytes 786440 | tf_op jit(solution)/shard_map/ppermute | solution.py:32
  116.1 7.4 %copy-start.15 = (s32[1,128]{1,0:T(1,128)S(1)}, s32[1,128]{1,0:T(1,128)}, u32[]{:S(2)}) copy-start(s32[1,128]{1,0:T(1,128)} %reduce_sum.86) | copy-start | bytes 1540
  116.1 7.4 %copy-start.6 = (bf16[384,1024]{1,0:T(8,128)(2,1)S(1)}, bf16[384,1024]{1,0:T(8,128)(2,1)}, u32[]{:S(2)}) copy-start(bf16[384,1024]{1,0:T(8,128)(2,1)} %get-tuple-element.502) | copy-start | bytes 2359300
  117.7 5.8 %copy-start.10 = (bf16[128,1024]{1,0:T(8,128)(2,1)S(1)}, bf16[128,1024]{1,0:T(8,128)(2,1)}, u32[]{:S(2)}) copy-start(bf16[128,1024]{1,0:T(8,128)(2,1)} %get-tuple-element.510) | copy-start | bytes 786436
  117.7 21.1 %all-to-all-start = ((f32[16,128,128]{2,1,0:T(8,128)}), f32[16,128,128]{2,1,0:T(8,128)}, u32[]{:S(2)}, u32[]{:S(2)}) async-start(f32[16,128,128]{2,1,0:T(8,128)} %bitcast_bitcast_fusion), calls=%async_computation | async-start | bytes 2097152 | tf_op jit(solution)/shard_map/all_to_all | solution.py:328
  124.7 16.1 %copy-start.5 = (bf16[256,2048]{1,0:T(8,128)(2,1)S(1)}, bf16[256,2048]{1,0:T(8,128)(2,1)}, u32[]{:S(2)}) copy-start(bf16[256,2048]{1,0:T(8,128)(2,1)} %copy-done.4) | copy-start | bytes 3145732

commit v2 on v0

v2 whole, which is shorter than its diff:
```python
import functools

import jax
import jax.numpy as jnp
from jax import lax
from jax.experimental import pallas as pl
from jax.experimental.pallas import tpu as pltpu
from jax.sharding import PartitionSpec as P

BF = jnp.bfloat16
F32 = jnp.float32
I32 = jnp.int32
SLOTS = 16
HOPS = (0, 1, 3, 2)
BACK = (0, 2, 1, 3)
BLOCK = 128
HALF = 1024
CHUNK = 512
NEAR = 4 * BLOCK
PAYLOAD = BLOCK + 2 * SLOTS


def along_y(x, hop):
    pairs = [(t, ((t // 2 - hop) % 4) * 2 + t % 2) for t in range(8)]
    return lax.ppermute(x, "tok", pairs)


def partner(place, step):
    return 3 - place if step else place ^ 1


def swap_z(x, step):
    return lax.ppermute(x, "vocab", [(v, v // 4 * 4 + partner(v % 4, step)) for v in range(16)])


def swap_x(x, step):
    return lax.ppermute(x, "vocab", [(v, partner(v // 4, step) * 4 + v % 4) for v in range(16)])


def swap_y(x, step):
    return lax.ppermute(x, "tok", [(t, partner(t // 2, step) * 2 + t % 2) for t in range(8)])


def sibling(x):
    return lax.ppermute(x, "tok", [(t, t ^ 1) for t in range(8)])


def place():
    t = lax.axis_index("tok")
    return lax.axis_index("vocab"), t // 2, t % 2


def one(mask):
    return jnp.where(mask, 1.0, 0.0)


def iota(shape, dim):
    return lax.broadcasted_iota(I32, shape, dim)


def transposed(rows):
    return jnp.concatenate([rows, jnp.zeros((120, rows.shape[1]), F32)], axis=0).T


def whole(*shape):
    return pl.BlockSpec(shape, lambda *_: (0,) * len(shape), pipeline_mode=pl.Buffered(1))


VMEM = pl.BlockSpec(memory_space=pltpu.VMEM)


def params(limit=60 << 20):
    return pltpu.CompilerParams(vmem_limit_bytes=limit)


SMALL = 12 << 20


def cost(us):
    return pl.CostEstimate(flops=int(us * 1e9), bytes_accessed=1024, transcendentals=0)


def rows_kernel(label_ref, dec_id_ref, enc_id_ref, dec_ref, enc_ref, rows_ref, ids_out):
    v, y, _ = place()
    ids = jnp.concatenate(
        [label_ref[...], dec_id_ref[...], enc_id_ref[...], jnp.zeros((5, BLOCK), I32)], axis=0
    )
    ids_out[...] = ids
    chip = lax.shift_right_logical(ids, 11)
    inside = []
    for kind in (1, 2):
        inside += [one(chip[kind : kind + 1] == v * 4 + lax.rem(y + h, 4)) for h in HOPS]
        inside += [jnp.zeros((4, BLOCK), F32)]
    inside = jnp.concatenate(inside, axis=0)
    before = one(iota((BLOCK, BLOCK), 0) < iota((BLOCK, BLOCK), 1)).astype(BF)
    rank = jnp.dot(inside.astype(BF), before, preferred_element_type=F32)
    rank_enc = rank[8:16] + jnp.sum(inside[0:8], axis=1, keepdims=True)
    slot = iota((SLOTS, BLOCK), 0).astype(F32)

    def chosen(rank, inside):
        return jnp.concatenate(
            [one(rank[i : i + 1] == slot) * inside[i : i + 1] for i in range(4)], axis=0
        ).astype(BF)

    got = jnp.dot(chosen(rank[0:8], inside[0:8]), dec_ref[...], preferred_element_type=F32)
    got += jnp.dot(chosen(rank_enc, inside[8:16]), enc_ref[...], preferred_element_type=F32)
    rows_ref[...] = got.astype(BF)


def rows_to_send(labels, dec_ids, enc_ids, dec_grad, enc_grad):
    width = dec_grad.shape[1]
    return pl.pallas_call(
        rows_kernel,
        in_specs=[VMEM] * 5,
        out_specs=[VMEM] * 2,
        out_shape=[jax.ShapeDtypeStruct((4 * SLOTS, width), BF), jax.ShapeDtypeStruct((8, BLOCK), I32)],
        compiler_params=params(),
        cost_estimate=cost(1000),
    )(labels[None], dec_ids[None], enc_ids[None], dec_grad, enc_grad)


def plan_kernel(p0, p1, p2, p3, label_col, slot_col, place_col, pick_ref, most_ref):
    v, y, core = place()
    my_chip = v * 4 + y
    pairs = (p0, p1, p2, p3)

    def kind(k):
        return jnp.concatenate(
            [pairs[i][8 * c + k : 8 * c + k + 1, :] for c in range(2) for i in range(4)], axis=0
        )

    lab, dec, enc = kind(0), kind(1), kind(2)

    def relative(ids):
        return ((ids - my_chip * (2 * HALF)) ^ (core * HALF)).astype(F32)

    def chip_of(ids):
        return lax.shift_right_logical(ids, 11).astype(F32)

    mine = my_chip.astype(F32)
    lab_f, lab_rel, lab_chip = lab.astype(F32), relative(lab), chip_of(lab)
    lab_t, rel_t, chip_t = transposed(lab_f), transposed(lab_rel), transposed(lab_chip)
    earlier = one(iota((BLOCK, BLOCK), 0) < iota((BLOCK, BLOCK), 1))
    later = one(iota((BLOCK, BLOCK), 0) > iota((BLOCK, BLOCK), 1))
    slot = iota((SLOTS, BLOCK), 0).astype(F32)
    most = jnp.zeros((1, 1), F32)
    for b in range(8):
        same = one(lab_t[:, b : b + 1] == lab_f[b : b + 1, :])
        same_chip = one(chip_t[:, b : b + 1] == lab_chip[b : b + 1, :])
        first_row = one(jnp.sum(same * earlier, axis=0, keepdims=True) == 0.0)
        first_col = one(jnp.sum(same * later, axis=1, keepdims=True) == 0.0)
        rank = jnp.sum(same_chip * earlier * first_col, axis=0, keepdims=True)
        most = jnp.maximum(most, jnp.max(rank * first_row, axis=1, keepdims=True) + 1.0)
        label_col[BLOCK * b : BLOCK * (b + 1), :] = rel_t[:, b : b + 1].astype(I32)
        if b < 4:
            chosen = one(rank == slot) * (first_row * one(lab_chip[b : b + 1] == mine))
            at = jnp.sum(chosen * (lab_rel[b : b + 1] + 1.0), axis=1, keepdims=True) - 1.0
            slot_col[SLOTS * b : SLOTS * (b + 1), :] = at.astype(I32)
        if b == 0:
            rank_col = jnp.sum(same * (first_row * rank), axis=1, keepdims=True)
            lane = iota((BLOCK, BLOCK), 1)
            source = lane // SLOTS
            hop = jnp.where(source == 2, 3, jnp.where(source == 3, 2, source))
            chip = (v * 4 + lax.rem(y + hop, 4)).astype(F32)
            hit = one(chip_t[:, 0:1] == chip) * one(rank_col == (lane % SLOTS).astype(F32))
            pick_ref[...] = (hit * one(lane < 4 * SLOTS)).astype(BF)

    dec_chip, enc_chip = chip_of(dec), chip_of(enc)
    dec_rel, enc_rel = relative(dec), relative(enc)
    inside = jnp.concatenate([one(dec_chip == mine), one(enc_chip == mine)], axis=0)
    rank = jnp.dot(inside.astype(BF), earlier.astype(BF), preferred_element_type=F32)
    rank_enc = rank[8:16] + jnp.sum(inside[0:8], axis=1, keepdims=True)
    all_chips = iota((64, BLOCK), 0).astype(F32)
    tok_most = jnp.zeros((1, 1), F32)
    for b in range(8):
        row = slice(b, b + 1)
        at = one(rank[row] == slot) * inside[row] * (dec_rel[row] + 1.0)
        at += one(rank_enc[row] == slot) * inside[8 + b : 9 + b] * (enc_rel[row] + 1.0)
        at = jnp.sum(at, axis=1, keepdims=True) - 1.0
        place_col[SLOTS * b : SLOTS * (b + 1), :] = at.astype(I32)
        count = one(dec_chip[row] == all_chips) + one(enc_chip[row] == all_chips)
        count = jnp.sum(count, axis=1, keepdims=True)
        tok_most = jnp.maximum(tok_most, jnp.max(count, axis=0, keepdims=True))
    most_ref[...] = jnp.where(iota((8, BLOCK), 1) == 0, most, tok_most).astype(I32)


def plan(pairs):
    return pl.pallas_call(
        plan_kernel,
        in_specs=[VMEM] * 4,
        out_specs=[VMEM] * 5,
        out_shape=[
            jax.ShapeDtypeStruct((8 * BLOCK, 1), I32),
            jax.ShapeDtypeStruct((4 * SLOTS, 1), I32),
            jax.ShapeDtypeStruct((8 * SLOTS, 1), I32),
            jax.ShapeDtypeStruct((BLOCK, BLOCK), BF),
            jax.ShapeDtypeStruct((8, BLOCK), I32),
        ],
        compiler_params=params(),
        cost_estimate=cost(100),
    )(*pairs)


def logits_kernel(*refs):
    hidden = refs[:4]
    own_ref, sib_ref, label_ref, slot_ref, rows_ref = refs[4:9]
    own_out, sib_out, stats_ref = refs[9:12]
    payload = refs[12:16]
    states, table, logits, weights, in_sem, hidden_sem, out_sem = refs[16:]
    blocks = []
    for i in range(4):
        blocks.append(
            pltpu.make_async_copy(hidden[i], states.at[pl.ds(BLOCK * i, BLOCK)], hidden_sem.at[i])
        )
        blocks[i].start()
    loads = []
    for j in range(4):
        source = own_ref if j < 2 else sib_ref
        loads.append(
            pltpu.make_async_copy(
                source.at[pl.ds(CHUNK * (j % 2), CHUNK)], table.at[pl.ds(CHUNK * j, CHUNK)], in_sem.at[j]
            )
        )
        loads[j].start()
    for i in range(4):
        payload[i][BLOCK + SLOTS : PAYLOAD, :] = rows_ref[SLOTS * i : SLOTS * (i + 1), :]
    for block in blocks:
        block.wait()

    label = label_ref[0:NEAR, :]
    stores = []
    peak = None
    for j in range(4):
        loads[j].wait()
        part = lax.dot_general(
            states[...], table[CHUNK * j : CHUNK * (j + 1), :], (((1,), (1,)), ((), ())), preferred_element_type=F32
        )
        logits[j] = part
        target = own_out if j < 2 else sib_out
        stores.append(pltpu.make_async_copy(logits.at[j], target.at[j % 2], out_sem.at[j]))
        stores[j].start()
        top = jnp.max(part, axis=1, keepdims=True)
        peak = top if peak is None else jnp.maximum(peak, top)

    total = picked = None
    for j in range(4):
        part = logits[j]
        is_label = iota((NEAR, CHUNK), 1) + CHUNK * j == label
        weight = jnp.exp(part - peak)
        row_sum = jnp.sum(weight, axis=1, keepdims=True)
        hit = jnp.sum(jnp.where(is_label, part, 0.0), axis=1, keepdims=True)
        total = row_sum if total is None else total + row_sum
        picked = hit if picked is None else picked + hit
        at = slice(CHUNK * j, CHUNK * (j + 1))
        weights[0:NEAR, at] = jnp.where(is_label, 0.0, weight).astype(BF)
        slots = iota((4 * SLOTS, CHUNK), 1) + CHUNK * j == slot_ref[...]
        weights[NEAR:, at] = one(slots).astype(BF)

    lane = iota((NEAR, 128), 1)
    both = jnp.where(lane == 0, peak, jnp.where(lane == 1, total, jnp.where(lane == 2, picked, 0.0)))
    stats_ref[...] = both.T[0:8, :]
    for j in range(4):
        at = slice(CHUNK * j, CHUNK * (j + 1))
        grad = jnp.dot(weights[...], table[:, at], preferred_element_type=F32).astype(BF)
        for i in range(4):
            payload[i][0:BLOCK, at] = grad[BLOCK * i : BLOCK * (i + 1)]
            payload[i][BLOCK : BLOCK + SLOTS, at] = grad[NEAR + SLOTS * i : NEAR + SLOTS * (i + 1)]
    for store in stores:
        store.wait()


def logits_and_grads(hidden, own, sib, labels, slots, rows):
    width = own.shape[1]
    anywhere = pl.BlockSpec(memory_space=pl.ANY)
    return pl.pallas_call(
        logits_kernel,
        in_specs=[anywhere] * 6 + [VMEM] * 3,
        out_specs=[anywhere] * 2 + [VMEM] * 5,
        out_shape=[jax.ShapeDtypeStruct((2, NEAR, CHUNK), F32)] * 2
        + [jax.ShapeDtypeStruct((8, NEAR), F32)]
        + [jax.ShapeDtypeStruct((PAYLOAD, width), BF)] * 4,
        scratch_shapes=[
            pltpu.VMEM((NEAR, width), BF),
            pltpu.VMEM((2 * HALF, width), BF),
            pltpu.VMEM((4, NEAR, CHUNK), F32),
            pltpu.VMEM((NEAR + 4 * SLOTS, 2 * HALF), BF),
            pltpu.SemaphoreType.DMA((4,)),
            pltpu.SemaphoreType.DMA((4,)),
            pltpu.SemaphoreType.DMA((4,)),
        ],
        compiler_params=params(),
        cost_estimate=cost(12),
    )(*hidden, own, sib, labels, slots, rows)


def merged(parts):
    top = functools.reduce(jnp.maximum, [p[0:1] for p in parts])
    total = sum(p[1:2] * jnp.exp(p[0:1] - top) for p in parts)
    return top, total, sum(p[2:3] for p in parts)


def small(kernel, out_shape, *operands, scratch=()):
    many = isinstance(out_shape, list)
    return pl.pallas_call(
        kernel,
        in_specs=[VMEM] * len(operands),
        out_specs=[VMEM] * len(out_shape) if many else VMEM,
        out_shape=out_shape,
        scratch_shapes=scratch,
        compiler_params=params(SMALL),
    )(*operands)


def order_kernel(stats_ref, out_ref):
    _, y, _ = place()
    stats = stats_ref[...]
    rows = jnp.concatenate([stats[0:3], stats[0:1], jnp.zeros((4, NEAR), F32)], axis=0)
    for i in range(4):
        at = pl.multiple_of(lax.rem(y + HOPS[i], 4) * BLOCK, BLOCK)
        out_ref[:, pl.ds(at, BLOCK)] = rows[:, BLOCK * i : BLOCK * (i + 1)]


def merge_kernel(own_ref, other_ref, out_ref):
    own = own_ref[...]
    out_ref[...] = jnp.concatenate([*merged([own, other_ref[...]]), own[3:8]], axis=0)


def merge_y_kernel(own_ref, other_ref, out_ref):
    _, y, _ = place()
    own, other = own_ref[...], other_ref[...]
    odd = lax.rem(y, 2) == 1
    even_peaks = jnp.where(odd, other[3:4], own[3:4])
    odd_peaks = jnp.where(odd, own[3:4], other[3:4])
    out_ref[...] = jnp.concatenate(
        [*merged([own, other]), even_peaks, odd_peaks, jnp.zeros((3, NEAR), F32)], axis=0
    )


def norm_kernel(own_ref, other_ref, row_ref, col_ref, loss_ref, all_ref):
    _, y, _ = place()
    own, other = own_ref[...], other_ref[...]
    top, total, picked = merged([own, other])
    norm = top + jnp.log(total)
    low = jnp.where(y < 2, own[3:5], other[3:5])
    high = jnp.where(y < 2, other[3:5], own[3:5])
    all_ref[...] = jnp.concatenate([norm, picked, low, high, jnp.zeros((2, NEAR), F32)], axis=0)

    def block(i):
        return all_ref[:, pl.ds(pl.multiple_of(lax.rem(y + HOPS[i], 4) * BLOCK, BLOCK), BLOCK)]

    mine = block(0)
    scales = []
    for i in range(4):
        source = lax.rem(y + HOPS[i], 4)
        peaks = sum(jnp.where(source == k, mine[2 + k : 3 + k], 0.0) for k in range(4))
        scales.append(jnp.exp(peaks - mine[0:1]))
    label = jnp.exp(mine[1:2] - mine[0:1]) - 1.0
    row_ref[...] = jnp.concatenate([*scales, label, jnp.zeros((3, BLOCK), F32)], axis=0)
    loss_ref[...] = mine[0:1] - mine[1:2]
    col_ref[...] = transposed(jnp.concatenate([block(i) for i in range(4)], axis=1))[:, 0:1]


def norms(stats):
    shape = jax.ShapeDtypeStruct((8, NEAR), F32)
    sums = small(order_kernel, shape, stats)
    for swap in (swap_z, swap_x):
        for step in range(2):
            sums = small(merge_kernel, shape, sums, swap(sums, step))
    sums = small(merge_y_kernel, shape, sums, swap_y(sums, 0))
    return small(
        norm_kernel,
        [
            jax.ShapeDtypeStruct((8, BLOCK), F32),
            jax.ShapeDtypeStruct((NEAR, 1), F32),
            jax.ShapeDtypeStruct((1, BLOCK), F32),
        ],
        sums,
        swap_y(sums, 1),
        scratch=[pltpu.VMEM((8, NEAR), F32)],
    )


def combine_kernel(p0, p1, p2, p3, scale_ref, pick_ref, late_ref, parts_ref, rows_ref):
    payload = (p0, p1, p2, p3)
    cols = transposed(scale_ref[...])
    for i in range(4):
        rows_ref[SLOTS * i : SLOTS * (i + 1), :] = payload[i][BLOCK + SLOTS : PAYLOAD, :]
    slots = jnp.concatenate([p[BLOCK : BLOCK + SLOTS, :] for p in payload], axis=0)
    label_rows = jnp.dot(pick_ref[:, 0 : 4 * SLOTS], slots, preferred_element_type=F32)
    total = cols[:, 4:5] * (label_rows + late_ref[...].astype(F32))
    for i in range(4):
        total += cols[:, i : i + 1] * payload[i][0:BLOCK, :].astype(F32)
    for i in range(parts_ref.shape[0]):
        parts_ref[i] = total[:, 128 * i : 128 * (i + 1)]


def sum_kernel(groups_ref, end_ref, out_ref):
    out_ref[...] = jnp.sum(groups_ref[...], axis=0) + end_ref[0:1, :]


def combine(payload, scales, pick, late_rows):
    width = payload[0].shape[1]
    return pl.pallas_call(
        combine_kernel,
        in_specs=[VMEM] * 7,
        out_specs=[VMEM] * 2,
        out_shape=[
            jax.ShapeDtypeStruct((16, BLOCK, width // 16), F32),
            jax.ShapeDtypeStruct((4 * SLOTS, width), BF),
        ],
        compiler_params=params(16 << 20),
        cost_estimate=cost(0.001),
    )(*payload, scales, pick, late_rows)


def table_kernel(*refs):
    logits = refs[0:2]
    norms_of = refs[2:4]
    label_ref, place_ref = refs[4:6]
    hidden = refs[6:14]
    rows_own, rows_sib, out_ref, end_ref, states, grads = refs[14:]
    tokens = NEAR

    @pl.when(pl.program_id(0) == 0)
    def _():
        for i in range(8):
            states[BLOCK * i : BLOCK * (i + 1), :] = hidden[i][...]
        states[2 * tokens : 2 * tokens + 4 * SLOTS, :] = rows_own[...]
        states[2 * tokens + 4 * SLOTS :, :] = rows_sib[...]

    tile = out_ref.shape[0]
    first = pl.program_id(0) * tile
    for k in range(2):
        low = tokens * k
        value = jnp.exp(logits[k][0] - norms_of[k][...])
        is_label = iota((tokens, tile), 1) + first == label_ref[low : low + tokens, :]
        grads[low : low + tokens, :] = (value - one(is_label)).astype(BF)
    named = iota((8 * SLOTS, tile), 1) + first == place_ref[...]
    grads[2 * tokens :, :] = one(named).astype(BF)
    end_ref[...] = jnp.zeros_like(end_ref)
    out_ref[...] = lax.dot_general(
        grads[...], states[...], (((0,), (0,)), ((), ())), preferred_element_type=F32
    )


def table_gradient(logits, norm_own, norm_sib, labels, places, hidden, rows_own, rows_sib):
    width, tile, tokens = hidden[0].shape[1], 256, NEAR
    per = CHUNK // tile
    return pl.pallas_call(
        table_kernel,
        grid=(HALF // tile,),
        in_specs=[pl.BlockSpec((1, l.shape[1], tile), lambda j: (j // per, 0, j % per)) for l in logits]
        + [whole(tokens, 1), whole(tokens, 1), whole(2 * tokens, 1), whole(8 * SLOTS, 1)]
        + [whole(BLOCK, width)] * 8
        + [whole(4 * SLOTS, width)] * 2,
        out_specs=[pl.BlockSpec((tile, width), lambda j: (j, 0)), pl.BlockSpec((8, 128), lambda j: (0, 0))],
        out_shape=[jax.ShapeDtypeStruct((HALF, width), F32), jax.ShapeDtypeStruct((8, 128), F32)],
        scratch_shapes=[
            pltpu.VMEM((2 * tokens + 8 * SLOTS, width), BF),
            pltpu.VMEM((2 * tokens + 8 * SLOTS, tile), BF),
        ],
        compiler_params=params(),
        cost_estimate=pl.CostEstimate(
            flops=2 * HALF * (2 * tokens + 8 * SLOTS) * width, bytes_accessed=16 << 20, transcendentals=0
        ),
    )(*logits, norm_own, norm_sib, labels, places, *hidden, rows_own, rows_sib)


def ranks(inside):
    n = inside.shape[-1]
    before = jnp.arange(n)[:, None] < jnp.arange(n)[None, :]
    return jnp.sum((inside[..., :, None] & before).astype(I32), axis=-2)


def pick(slot_of, inside, first_slot):
    slots = first_slot + jnp.arange(SLOTS, dtype=I32)
    return (slot_of[..., None, :] == slots[:, None]) & inside[..., None, :]


def exchange(rows):
    return [rows[0]] + [along_y(rows[BACK[i]], HOPS[i]) for i in range(1, 4)]


def more_label_rows(pairs, own_table, sib_table, first_slot):
    v, y, core = place()
    labels = jnp.stack([p[0] for p in pairs])
    chip = labels // (2 * HALF)
    same = labels[:, :, None] == labels[:, None, :]
    earlier = jnp.arange(BLOCK)[:, None] < jnp.arange(BLOCK)[None, :]
    is_first = ~jnp.any(same & earlier, axis=1)
    same_chip = chip[:, :, None] == chip[:, None, :]
    first_rank = jnp.sum((same_chip & earlier & is_first[:, :, None]).astype(I32), axis=1)
    rank = jnp.sum(jnp.where(same & is_first[:, :, None], first_rank[:, :, None], 0), axis=1)
    relative = (labels - (v * 4 + y) * (2 * HALF)) ^ (core * HALF)
    chosen = pick(rank, (chip == v * 4 + y) & is_first, first_slot)
    at = (jnp.sum(jnp.where(chosen, relative[:, None, :] + 1, 0), axis=2) - 1).reshape(4 * SLOTS, 1)
    row = jnp.arange(HALF, dtype=I32)
    rows = jnp.dot((at == row).astype(BF), own_table, preferred_element_type=F32)
    rows += jnp.dot((at == row + HALF).astype(BF), sib_table, preferred_element_type=F32)
    rows = rows.astype(BF).reshape(4, SLOTS, -1)
    got = jnp.concatenate(exchange([rows[i] for i in range(4)]))
    slot = jnp.arange(4 * SLOTS, dtype=I32)
    source = jnp.stack([v * 4 + (y + h) % 4 for h in HOPS])[slot // SLOTS]
    hit = (chip[0][:, None] == source[None]) & (rank[0][:, None] == (slot % SLOTS + first_slot)[None])
    return jnp.dot(hit.astype(BF), got, preferred_element_type=F32)


def more_token_rows(pairs, dec_grad, enc_grad, first_slot):
    v, y, core = place()
    own = jnp.concatenate([pairs[0][1], pairs[0][2]])
    chips = jnp.stack([v * 4 + (y + h) % 4 for h in HOPS])
    inside = own[None] // (2 * HALF) == chips[:, None]
    chosen = pick(ranks(inside), inside, first_slot).reshape(4 * SLOTS, 2 * BLOCK)
    rows = jnp.dot(chosen.astype(BF), jnp.concatenate([dec_grad, enc_grad]), preferred_element_type=F32)
    rows = rows.astype(BF).reshape(4, SLOTS, -1)
    got = jnp.concatenate(exchange([rows[i] for i in range(4)]))
    got = jnp.concatenate([got, sibling(got)])
    ids = jnp.stack(
        [jnp.concatenate([p[8 * c + 1], p[8 * c + 2]]) for c in range(2) for p in pairs]
    )
    inside = ids // (2 * HALF) == v * 4 + y
    chosen = pick(ranks(inside), inside, first_slot)
    relative = (ids - (v * 4 + y) * (2 * HALF)) ^ (core * HALF)
    at = jnp.sum(jnp.where(chosen, relative[:, None, :] + 1, 0), axis=2).reshape(1, 8 * SLOTS) - 1
    named = at == jnp.arange(HALF, dtype=I32)[:, None]
    return jnp.dot(named.astype(BF), got, preferred_element_type=F32)


def per_device(hidden_states, tied_table, labels, dec_ids, enc_ids, dec_grad, enc_grad):
    after, before = along_y(hidden_states, 1), along_y(hidden_states, -1)
    sib_table = sibling(tied_table)
    rows, ids = rows_to_send(labels, dec_ids, enc_ids, dec_grad, enc_grad)
    own_pair = jnp.concatenate([ids, sibling(ids)])
    pairs = [own_pair] + [along_y(own_pair, h) for h in HOPS[1:]]
    far = jnp.concatenate([along_y(after[:64], 1), along_y(before[64:], -1)])
    hidden = [hidden_states, after, before, far]
    label_col, slot_col, place_col, label_pick, most = plan(pairs)
    label_rounds = (most[0, 0] + SLOTS - 1) // SLOTS
    token_rounds = (most[0, 1] + SLOTS - 1) // SLOTS

    own_logits, sib_logits, stats, *payload = logits_and_grads(
        hidden, tied_table, sib_table, label_col, slot_col, rows
    )

    payload = exchange(payload)
    scales, norm_col, loss = norms(stats)

    def add_labels(carry):
        r, state = carry
        pairs_r, slot = lax.optimization_barrier((pairs, r * SLOTS))
        return r + 1, state + more_label_rows(pairs_r, tied_table, sib_table, slot).astype(BF)

    none = jnp.zeros((BLOCK, tied_table.shape[1]), BF)
    _, late_rows = lax.while_loop(lambda c: c[0] < label_rounds, add_labels, (jnp.int32(1), none))
    group, rows_own = combine(payload, scales, label_pick, late_rows)
    groups_of = lax.all_to_all(group, "vocab", 0, 0)

    grad_table, end = table_gradient(
        [own_logits, sibling(sib_logits)],
        norm_col,
        sibling(norm_col),
        label_col,
        place_col,
        hidden + [sibling(h) for h in hidden],
        rows_own,
        sibling(rows_own),
    )

    grad_hidden = small(
        sum_kernel, jax.ShapeDtypeStruct(groups_of.shape[1:], F32), groups_of, end
    )

    def add_tokens(carry):
        r, grad = carry
        pairs_r, dec, enc, slot = lax.optimization_barrier((pairs, dec_grad, enc_grad, r * SLOTS))
        return r + 1, grad + more_token_rows(pairs_r, dec, enc, slot)

    _, grad_table = lax.while_loop(lambda c: c[0] < token_rounds, add_tokens, (jnp.int32(1), grad_table))
    return grad_table, grad_hidden, loss.reshape(BLOCK)


def solution(mesh):
    in_specs = (
        P("tok", None),
        P(("vocab", "tok"), None),
        P("tok"),
        P("tok"),
        P("tok"),
        P("tok", None),
        P("tok", None),
    )
    out_specs = (P(("vocab", "tok"), None), P("tok", "vocab"), P("tok"))
    return jax.shard_map(
        per_device, mesh=mesh, in_specs=in_specs, out_specs=out_specs, check_vma=False
    )
```

time: 366 us -> 119 us (0.33)
  blocking collectives: 160 us -> 0 us
  waiting for transfers between devices: 137 us -> 30.9 us
  matrix products: 44.3 us -> 0 us
  starting transfers between devices: 0.15 us -> 41.8 us
  Pallas kernels: 0 us -> 38.6 us
  between operations: 13.8 us -> 2.24 us
  other arithmetic: 6.28 us -> 0 us
    psum x1 -> x0, waiting for transfers between devices: 111 us -> none  [per_device(): summed = lax.psum(partial_hidden, ('vocab', 'tok'))]
    pmax x1 -> x0, blocking collectives: 65.6 us -> none  [per_device(): row_peak = lax.pmax(local_peak, ('vocab', 'tok'))]
    psum x1 -> x0, blocking collectives: 64.3 us -> none  [per_device(): exp_total, picked = lax.psum((local_total, picked_part), ('vocab', 'tok'))]
    dot_general x5 -> x0, matrix products: 44.3 us -> none  [the longest x1 10 us: per_device(): lax.dot_general(whole_hidden, tied_table, (((1,), (1,)), ((), ())), prefe...]
    pallas_call x0 -> x13, Pallas kernels: none -> 38.6 us  [the longest x1 17.3 us: logits_and_grads(): pl.pallas_call(logits_kernel, in_specs=[anywhere] * 6 + [VMEM] * 3, out_s...]
    ppermute x0 -> x25, starting transfers between devices: none -> 34.1 us  [the longest x10 13.6 us: along_y(): return lax.ppermute(x, 'tok', pairs)]
    ppermute x0 -> x25, waiting for transfers between devices: none -> 30.9 us  [the longest x2 14.8 us: swap_y(): lax.ppermute(x, 'tok', [(t, partner(t // 2, step) * 2 + t % 2) for t in r...]
    all_gather x3 -> x0, blocking collectives: 30.6 us -> none  [the longest x1 12.2 us: per_device(): lax.all_gather(labels, 'tok', axis=0, tiled=True)]
  transfers between devices with their start and end apart: 4 -> 26, of which waited for: 2 -> 13; matrix products, arithmetic and copies ran while one was open for 14% -> 3% of each run, Pallas kernels for 0% -> 17%
where the time goes in v2:
time: 119 us
  starting transfers between devices  41.8 us (35%)
  Pallas kernels  38.6 us (32%)
  waiting for transfers between devices  30.9 us (26%)
  local copies, waits for them, and re-layouts  5.31 us (4%)
  between operations  2.24 us (2%)
    pallas_call x1, Pallas kernels, logits_and_grads(): pl.pallas_call(logits_kernel, in_specs=[anywhere] * 6 + [VMEM] * 3, out_s...  17.3 us
    ppermute x2, waiting for transfers between devices, swap_y(): lax.ppermute(x, 'tok', [(t, partner(t // 2, step) * 2 + t % 2) for t in r...  14.8 us
    ppermute x10, starting transfers between devices, along_y(): return lax.ppermute(x, 'tok', pairs)  13.6 us
    pallas_call x1, Pallas kernels, table_gradient(): pl.pallas_call(table_kernel, grid=(HALF // tile,), in_specs=[pl.BlockSpec...  13.1 us
    ppermute x9, starting transfers between devices, sibling(): return lax.ppermute(x, 'tok', [(t, t ^ 1) for t in range(8)])  9.11 us
    all_to_all x1, starting transfers between devices, per_device(): groups_of = lax.all_to_all(group, 'vocab', 0, 0)  7.61 us
    ppermute x10, waiting for transfers between devices, along_y(): return lax.ppermute(x, 'tok', pairs)  7.3 us
    ppermute x2, starting transfers between devices, swap_z(): lax.ppermute(x, 'vocab', [(v, v // 4 * 4 + partner(v % 4, step)) for v in...  5.38 us
  transfers between devices with their start and end apart: 26, of which 13 were waited for; matrix products, arithmetic and copies ran while one was open for 3% of the time, Pallas kernels for 17%

profile of v2, /device:TPU:1, one launch (start us, length us, event | category | flops | bytes accessed | tf_op | source)
XLA Modules:
  0.0 119.1 jit_solution(7444652083733108833)
XLA Ops:
  0.6 3.6 %collective-permute-start.7 = (bf16[128,2048]{1,0:T(8,128)(2,1)}, bf16[128,2048]{1,0:T(8,128)(2,1)}, u32[]{:S(2)}, u32[]{:S(2)}) collective-permute-start(bf16[128,2048]{1,0:T(8,128)(2,1)} %refs_6_.1), channel_id=1, source_target_pairs={{0,6},{1,7},{2,0},{3,1},{4,2},{5,3},{6,4},{7,5},{8,14},{9,15},{10,... | collective-permute-start | bytes 1572872 | tf_op jit(solution)/shard_map/ppermute | solution.py:25
  4.3 2.4 %shard_map.94 = (bf16[64,2048]{1,0:T(8,128)(2,1)}, s32[8,128]{1,0:T(8,128)}) custom-call(s32[1,128]{1,0:T(1,128)} %bitcast.118, s32[1,128]{1,0:T(1,128)} %bitcast.119, s32[1,128]{1,0:T(1,128)} %bitcast.120, bf16[128,2048]{1,0:T(8,128)(2,1)} %dec_ref.1, bf16[128,2048]{1,0:T(8,128)(2,1)} %enc_ref.1), custom_call_target="tpu_custom_call" | custom-call | flops 999999995904 | bytes 1024 | tf_op jit(solution)/shard_map/pallas_call | solution.py:112
  6.7 1.0 collective-permute-start.12
  7.6 0.7 constant_dynamic-update-slice_fusion.8
  8.3 0.3 collective-permute-done.12
  8.7 0.5 collective-permute-start.13
  9.1 1.0 collective-permute-start.14
  10.1 0.4 collective-permute-start.15
  10.5 1.9 %collective-permute-start.8 = (bf16[128,2048]{1,0:T(8,128)(2,1)}, bf16[128,2048]{1,0:T(8,128)(2,1)S(1)}, u32[]{:S(2)}, u32[]{:S(2)}) collective-permute-start(bf16[128,2048]{1,0:T(8,128)(2,1)} %refs_6_.1), channel_id=1, source_target_pairs={{0,2},{1,3},{2,4},{3,5},{4,6},{5,7},{6,0},{7,1},{8,10},{9,11},{10,... | collective-permute-start | bytes 1572872 | tf_op jit(solution)/shard_map/ppermute | solution.py:25
  12.4 2.7 %collective-permute-done.7.refs_1_.refs_7_ = bf16[128,2048]{1,0:T(8,128)(2,1)} collective-permute-done((bf16[128,2048]{1,0:T(8,128)(2,1)}, bf16[128,2048]{1,0:T(8,128)(2,1)}, u32[]{:S(2)}, u32[]{:S(2)}) %collective-permute-start.7) | collective-permute-done | bytes 524320 | tf_op jit(solution)/shard_map/ppermute | solution.py:25
  15.1 1.0 slice.249
  16.1 1.9 %collective-permute-start.11 = (bf16[1024,2048]{1,0:T(8,128)(2,1)}, bf16[1024,2048]{1,0:T(8,128)(2,1)}, u32[]{:S(2)}, u32[]{:S(2)}) collective-permute-start(bf16[1024,2048]{1,0:T(8,128)(2,1)} %refs_4_.1), channel_id=1, source_target_pairs={{0,1},{1,0},{2,3},{3,2},{4,5},{5,4},{6,7},{7,6},{8,9},{9,8},{10,11... | collective-permute-start | bytes 12582920 | tf_op jit(solution)/shard_map/ppermute | solution.py:45
  18.0 0.0 collective-permute-done.13.p1
  18.0 3.4 %collective-permute-start.9 = (bf16[64,2048]{1,0:T(8,128)(2,1)S(1)}, bf16[64,2048]{1,0:T(8,128)(2,1)S(1)}, u32[]{:S(2)}, u32[]{:S(2)}) collective-permute-start(bf16[64,2048]{1,0:T(8,128)(2,1)S(1)} %slice.249), channel_id=1, source_target_pairs={{0,6},{1,7},{2,0},{3,1},{4,2},{5,3},{6,4},{7,5},{8,14},{9,15},{10,... | collective-permute-start | bytes 786440 | tf_op jit(solution)/shard_map/ppermute | solution.py:25
  21.5 0.0 collective-permute-done.14.p2
  21.5 0.0 collective-permute-done.15.p3
  21.5 2.7 %shard_map.95 = (s32[1024,1]{1,0:T(8,128)}, s32[64,1]{1,0:T(8,128)}, s32[128,1]{1,0:T(8,128)}, bf16[128,128]{1,0:T(8,128)(2,1)}, s32[8,128]{1,0:T(8,128)}) custom-call(s32[16,128]{1,0:T(8,128)S(1)} %constant_dynamic-update-slice_fusion.7.p0, s32[16,128]{1,0:T(8,128)S(1)} %collective-permute-done.13.p1, s32[16,128]{1,0:T(8,128)S(1)} %collective-permute-done.14.p2, ...), custom_call_target="tpu_custom_call" | custom-call | flops 99999997952 | bytes 1024 | tf_op jit(solution)/shard_map/pallas_call | solution.py:188
  24.1 0.2 collective-permute-done.8.refs_2_.refs_8_
  24.3 0.8 collective-permute-start.10
  25.1 1.4 %fusion.38 = (s32[1,1]{1,0:T(1,128)}, s32[1,1]{1,0:T(1,128)}) fusion(s32[8,128]{1,0:T(8,128)} %get-tuple-element.378), kind=kLoop, calls=%fused_computation.125 | loop fusion | bytes 16 | tf_op jit(solution)/shard_map/slice | solution.py:539
  27.2 0.0 collective-permute-done.9
  27.2 4.4 %collective-permute-done.10 = bf16[64,2048]{1,0:T(8,128)(2,1)S(1)} collective-permute-done((bf16[64,2048]{1,0:T(8,128)(2,1)S(1)}, bf16[64,2048]{1,0:T(8,128)(2,1)S(1)}, u32[]{:S(2)}, u32[]{:S(2)}) %collective-permute-start.10) | collective-permute-done | bytes 262176 | tf_op jit(solution)/shard_map/ppermute | solution.py:25
  31.6 0.0 collective-permute-done.11.refs_5_
  31.6 0.8 copy-done.8
  32.4 17.3 %shard_map.96 = (f32[2,512,512]{2,1,0:T(8,128)}, f32[2,512,512]{2,1,0:T(8,128)}, f32[8,512]{1,0:T(8,128)}, bf16[160,2048]{1,0:T(8,128)(2,1)}, bf16[160,2048]{1,0...) custom-call(bf16[128,2048]{1,0:T(8,128)(2,1)} %refs_6_.1, ...), custom_call_target="tpu_custom_call" | custom-call | flops 12000000000 | bytes 1024 | tf_op jit(solution)/shard_map/pallas_call | solution.py:275
  49.7 0.3 collective-permute-start.28
  50.0 2.9 %collective-permute-start.16 = (f32[2,512,512]{2,1,0:T(8,128)}, f32[2,512,512]{2,1,0:T(8,128)}, u32[]{:S(2)}, u32[]{:S(2)}) collective-permute-start(f32[2,512,512]{2,1,0:T(8,128)} %get-tuple-element.368), channel_id=1, source_target_pairs={{0,1},{1,0},{2,3},{3,2},{4,5},{5,4},{6,7},{7,6},{8,9},{9,8},{10,11... | collective-permute-start | bytes 6291464 | tf_op jit(solution)/shard_map/ppermute | solution.py:45
  53.0 0.2 while.26
  53.3 1.6 %collective-permute-start.29 = (bf16[160,2048]{1,0:T(8,128)(2,1)}, bf16[160,2048]{1,0:T(8,128)(2,1)S(1)}, u32[]{:S(2)}, u32[]{:S(2)}) collective-permute-start(bf16[160,2048]{1,0:T(8,128)(2,1)} %get-tuple-element.374), channel_id=1, source_target_pairs={{0,2},{1,3},{2,4},{3,5},{4,6},{5,7},{6,0},{7,1},{8,10},{9,11},{10,... | collective-permute-start | bytes 1966088 | tf_op jit(solution)/shard_map/ppermute | solution.py:25
  54.9 0.2 collective-permute-start.30
  55.1 1.7 %collective-permute-start.17 = (f32[8,512]{1,0:T(8,128)S(1)}, f32[8,512]{1,0:T(8,128)S(1)}, u32[]{:S(2)}, u32[]{:S(2)}) collective-permute-start(f32[8,512]{1,0:T(8,128)S(1)} %shard_map.97.own_ref), channel_id=1, source_target_pairs={{0,8},{8,0},{16,24},{24,16},{32,40},{40,32},{48,56},{56,48},{64,72... | collective-permute-start | bytes 49160 | tf_op jit(solution)/shard_map/ppermute | solution.py:33
  56.8 1.4 %collective-permute-done.17.other_ref = f32[8,512]{1,0:T(8,128)S(1)} collective-permute-done((f32[8,512]{1,0:T(8,128)S(1)}, f32[8,512]{1,0:T(8,128)S(1)}, u32[]{:S(2)}, u32[]{:S(2)}) %collective-permute-start.17) | collective-permute-done | bytes 16416 | tf_op jit(solution)/shard_map/ppermute | solution.py:33
  58.3 3.7 %collective-permute-start.18 = (f32[8,512]{1,0:T(8,128)S(1)}, f32[8,512]{1,0:T(8,128)S(1)}, u32[]{:S(2)}, u32[]{:S(2)}) collective-permute-start(f32[8,512]{1,0:T(8,128)S(1)} %shard_map.98.own_ref), channel_id=1, source_target_pairs={{0,24},{8,16},{16,8},{24,0},{32,56},{40,48},{48,40},{56,32},{64,88... | collective-permute-start | bytes 49160 | tf_op jit(solution)/shard_map/ppermute | solution.py:33
  61.9 1.4 %collective-permute-done.18.other_ref = f32[8,512]{1,0:T(8,128)S(1)} collective-permute-done((f32[8,512]{1,0:T(8,128)S(1)}, f32[8,512]{1,0:T(8,128)S(1)}, u32[]{:S(2)}, u32[]{:S(2)}) %collective-permute-start.18) | collective-permute-done | bytes 16416 | tf_op jit(solution)/shard_map/ppermute | solution.py:33
  63.4 1.3 %collective-permute-start.19 = (f32[8,512]{1,0:T(8,128)S(1)}, f32[8,512]{1,0:T(8,128)S(1)}, u32[]{:S(2)}, u32[]{:S(2)}) collective-permute-start(f32[8,512]{1,0:T(8,128)S(1)} %shard_map.99.own_ref), channel_id=1, source_target_pairs={{0,32},{8,40},{16,48},{24,56},{32,0},{40,8},{48,16},{56,24},{64,96... | collective-permute-start | bytes 49160 | tf_op jit(solution)/shard_map/ppermute | solution.py:37
  64.7 1.7 %collective-permute-done.19.other_ref = f32[8,512]{1,0:T(8,128)S(1)} collective-permute-done((f32[8,512]{1,0:T(8,128)S(1)}, f32[8,512]{1,0:T(8,128)S(1)}, u32[]{:S(2)}, u32[]{:S(2)}) %collective-permute-start.19) | collective-permute-done | bytes 16416 | tf_op jit(solution)/shard_map/ppermute | solution.py:37
  66.4 2.6 %collective-permute-start.20 = (f32[8,512]{1,0:T(8,128)S(1)}, f32[8,512]{1,0:T(8,128)S(1)}, u32[]{:S(2)}, u32[]{:S(2)}) collective-permute-start(f32[8,512]{1,0:T(8,128)S(1)} %shard_map.100.own_ref), channel_id=1, source_target_pairs={{0,96},{8,104},{16,112},{24,120},{32,64},{40,72},{48,80},{56,88},{... | collective-permute-start | bytes 49160 | tf_op jit(solution)/shard_map/ppermute | solution.py:37
  68.9 1.6 %collective-permute-done.20.other_ref = f32[8,512]{1,0:T(8,128)S(1)} collective-permute-done((f32[8,512]{1,0:T(8,128)S(1)}, f32[8,512]{1,0:T(8,128)S(1)}, u32[]{:S(2)}, u32[]{:S(2)}) %collective-permute-start.20) | collective-permute-done | bytes 16416 | tf_op jit(solution)/shard_map/ppermute | solution.py:37
  70.6 1.1 collective-permute-start.21
  71.7 12.0 %collective-permute-done.21.other_ref = f32[8,512]{1,0:T(8,128)S(1)} collective-permute-done((f32[8,512]{1,0:T(8,128)S(1)}, f32[8,512]{1,0:T(8,128)S(1)}, u32[]{:S(2)}, u32[]{:S(2)}) %collective-permute-start.21) | collective-permute-done | bytes 16416 | tf_op jit(solution)/shard_map/ppermute | solution.py:41
  83.7 1.0 collective-permute-start.22
  84.8 2.8 %collective-permute-done.22.other_ref = f32[8,512]{1,0:T(8,128)S(1)} collective-permute-done((f32[8,512]{1,0:T(8,128)S(1)}, f32[8,512]{1,0:T(8,128)S(1)}, u32[]{:S(2)}, u32[]{:S(2)}) %collective-permute-start.22) | collective-permute-done | bytes 16416 | tf_op jit(solution)/shard_map/ppermute | solution.py:41
  87.6 1.9 %collective-permute-start.24 = (bf16[128,2048]{1,0:T(8,128)(2,1)}, bf16[128,2048]{1,0:T(8,128)(2,1)}, u32[]{:S(2)}, u32[]{:S(2)}) collective-permute-start(bf16[128,2048]{1,0:T(8,128)(2,1)} %refs_6_.1), channel_id=1, source_target_pairs={{0,1},{1,0},{2,3},{3,2},{4,5},{5,4},{6,7},{7,6},{8,9},{9,8},{10,11... | collective-permute-start | bytes 1572872 | tf_op jit(solution)/shard_map/ppermute | solution.py:45
  89.5 0.6 shard_map.103
  90.1 0.0 collective-permute-done.28.p1
  90.1 0.0 collective-permute-done.29.p2
  90.1 0.0 collective-permute-done.30.p3
  90.1 1.8 %shard_map.104 = (f32[16,128,128]{2,1,0:T(8,128)}, bf16[64,2048]{1,0:T(8,128)(2,1)S(1)}) custom-call(bf16[160,2048]{1,0:T(8,128)(2,1)S(1)} %copy-done, bf16[160,2048]{1,0:T(8,128)(2,1)S(1)} %collective-permute-done.28.p1, bf16[160,2048]{1,0:T(8,128)(2,1)S(1)} %collective-permute-done.29.p2, bf16[160,2048]{1,0:T(8,128)(2,1)S(1)} %collective-permute-done.30.p3, ...), custom_call_target="tpu_custom_call" | custom-call | flops 1000000 | bytes 1024 | tf_op jit(solution)/shard_map/pallas_call | solution.py:403
  91.9 7.6 %all-to-all-start = ((f32[16,128,128]{2,1,0:T(8,128)}), f32[16,128,128]{2,1,0:T(8,128)S(1)}, u32[]{:S(2)}, u32[]{:S(2)}) async-start(f32[16,128,128]{2,1,0:T(8,128)} %get-tuple-element.383), calls=%async_computation | async-start | bytes 2097152 | tf_op jit(solution)/shard_map/all_to_all | solution.py:556
  99.5 0.3 collective-permute-start.25
  99.8 0.2 collective-permute-start.26
  100.1 0.3 collective-permute-start.27
  100.4 0.0 collective-permute-done.24.refs_10_
  100.4 0.2 collective-permute-start.31
  100.6 1.1 collective-permute-done.25.refs_11_
  101.7 0.3 collective-permute-start.23
  102.6 0.0 collective-permute-done.26.refs_12_
  102.6 0.9 collective-permute-done.27.refs_13_
  103.5 0.4 collective-permute-done.23.refs_3_
  103.9 0.0 collective-permute-done.31.refs_15_
  103.9 0.7 copy-done.13
  104.6 13.1 %shard_map.105 = (f32[1024,2048]{1,0:T(8,128)}, f32[8,128]{1,0:T(8,128)}) custom-call(f32[2,512,512]{2,1,0:T(8,128)} %get-tuple-element.367.refs_0_, f32[2,512,512]{2,1,0:T(8,128)} %collective-permute-done.16.refs_1_, f32[512,1]{1,0:T(8,128)} %copy-done.4, f32[512,1]{1,0:T(8,128)} %collective-permute-done.23.refs_3_, ...), custom_call_target="tpu_custom_call" | custom-call | flops 4831838208 | bytes 16777216 | tf_op jit(solution)/shard_map/pallas_call | solution.py:449
  117.7 0.7 copy-done.3
  118.4 0.7 shard_map.106
  (39 shorter events, 0.3 us)
Async XLA Ops:
  0.6 14.5 %collective-permute-start.7 = (bf16[128,2048]{1,0:T(8,128)(2,1)}, bf16[128,2048]{1,0:T(8,128)(2,1)}, u32[]{:S(2)}, u32[]{:S(2)}) collective-permute-start(bf16[128,2048]{1,0:T(8,128)(2,1)} %refs_6_.1), channel_id=1, source_target_pairs={{0,6},{1,7},{2,0},{3,1},{4,2},{5,3},{6,4},{7,5},{8,14},{9,15},{10,... | collective-permute-start | bytes 1572872 | tf_op jit(solution)/shard_map/ppermute | solution.py:25
  6.7 2.0 %collective-permute-start.12 = (s32[8,128]{1,0:T(8,128)}, s32[8,128]{1,0:T(8,128)S(1)}, u32[]{:S(2)}, u32[]{:S(2)}) collective-permute-start(s32[8,128]{1,0:T(8,128)} %get-tuple-element.363), channel_id=1, source_target_pairs={{0,1},{1,0},{2,3},{3,2},{4,5},{5,4},{6,7},{7,6},{8,9},{9,8},{10,11... | collective-permute-start | bytes 12296 | tf_op jit(solution)/shard_map/ppermute | solution.py:45
  8.7 9.4 %collective-permute-start.13 = (s32[16,128]{1,0:T(8,128)S(1)}, s32[16,128]{1,0:T(8,128)S(1)}, u32[]{:S(2)}, u32[]{:S(2)}) collective-permute-start(s32[16,128]{1,0:T(8,128)S(1)} %constant_dynamic-update-slice_fusion.7.p0), channel_id=1, source_target_pairs={{0,6},{1,7},{2,0},{3,1},{4,2},{5,3},{6,4},{7,5},{8,14},{9,15},{10,... | collective-permute-start | bytes 24584 | tf_op jit(solution)/shard_map/ppermute | solution.py:25
  9.1 12.3 %collective-permute-start.14 = (s32[16,128]{1,0:T(8,128)S(1)}, s32[16,128]{1,0:T(8,128)S(1)}, u32[]{:S(2)}, u32[]{:S(2)}) collective-permute-start(s32[16,128]{1,0:T(8,128)S(1)} %constant_dynamic-update-slice_fusion.7.p0), channel_id=1, source_target_pairs={{0,2},{1,3},{2,4},{3,5},{4,6},{5,7},{6,0},{7,1},{8,10},{9,11},{10,... | collective-permute-start | bytes 24584 | tf_op jit(solution)/shard_map/ppermute | solution.py:25
  10.1 11.3 %collective-permute-start.15 = (s32[16,128]{1,0:T(8,128)S(1)}, s32[16,128]{1,0:T(8,128)S(1)}, u32[]{:S(2)}, u32[]{:S(2)}) collective-permute-start(s32[16,128]{1,0:T(8,128)S(1)} %constant_dynamic-update-slice_fusion.7.p0), channel_id=1, source_target_pairs={{0,4},{1,5},{2,6},{3,7},{4,0},{5,1},{6,2},{7,3},{8,12},{9,13},{10,... | collective-permute-start | bytes 24584 | tf_op jit(solution)/shard_map/ppermute | solution.py:25
  10.5 13.8 %collective-permute-start.8 = (bf16[128,2048]{1,0:T(8,128)(2,1)}, bf16[128,2048]{1,0:T(8,128)(2,1)S(1)}, u32[]{:S(2)}, u32[]{:S(2)}) collective-permute-start(bf16[128,2048]{1,0:T(8,128)(2,1)} %refs_6_.1), channel_id=1, source_target_pairs={{0,2},{1,3},{2,4},{3,5},{4,6},{5,7},{6,0},{7,1},{8,10},{9,11},{10,... | collective-permute-start | bytes 1572872 | tf_op jit(solution)/shard_map/ppermute | solution.py:25
  16.1 15.5 %collective-permute-start.11 = (bf16[1024,2048]{1,0:T(8,128)(2,1)}, bf16[1024,2048]{1,0:T(8,128)(2,1)}, u32[]{:S(2)}, u32[]{:S(2)}) collective-permute-start(bf16[1024,2048]{1,0:T(8,128)(2,1)} %refs_4_.1), channel_id=1, source_target_pairs={{0,1},{1,0},{2,3},{3,2},{4,5},{5,4},{6,7},{7,6},{8,9},{9,8},{10,11... | collective-permute-start | bytes 12582920 | tf_op jit(solution)/shard_map/ppermute | solution.py:45
  18.0 9.1 %collective-permute-start.9 = (bf16[64,2048]{1,0:T(8,128)(2,1)S(1)}, bf16[64,2048]{1,0:T(8,128)(2,1)S(1)}, u32[]{:S(2)}, u32[]{:S(2)}) collective-permute-start(bf16[64,2048]{1,0:T(8,128)(2,1)S(1)} %slice.249), channel_id=1, source_target_pairs={{0,6},{1,7},{2,0},{3,1},{4,2},{5,3},{6,4},{7,5},{8,14},{9,15},{10,... | collective-permute-start | bytes 786440 | tf_op jit(solution)/shard_map/ppermute | solution.py:25
  24.3 7.3 %copy-start.6 = (bf16[128,2048]{1,0:T(8,128)(2,1)}, bf16[128,2048]{1,0:T(8,128)(2,1)S(1)}, u32[]{:S(2)}) copy-start(bf16[128,2048]{1,0:T(8,128)(2,1)S(1)} %collective-permute-done.8.refs_2_.refs_8_) | copy-start | bytes 1572868
  24.3 7.2 %collective-permute-start.10 = (bf16[64,2048]{1,0:T(8,128)(2,1)S(1)}, bf16[64,2048]{1,0:T(8,128)(2,1)S(1)}, u32[]{:S(2)}, u32[]{:S(2)}) collective-permute-start(bf16[64,2048]{1,0:T(8,128)(2,1)S(1)} %slice.250), channel_id=1, source_target_pairs={{0,2},{1,3},{2,4},{3,5},{4,6},{5,7},{6,0},{7,1},{8,10},{9,11},{10,... | collective-permute-start | bytes 786440 | tf_op jit(solution)/shard_map/ppermute | solution.py:25
  31.6 0.8 copy-start.8
  49.7 40.3 %collective-permute-start.28 = (bf16[160,2048]{1,0:T(8,128)(2,1)}, bf16[160,2048]{1,0:T(8,128)(2,1)S(1)}, u32[]{:S(2)}, u32[]{:S(2)}) collective-permute-start(bf16[160,2048]{1,0:T(8,128)(2,1)} %get-tuple-element.373), channel_id=1, source_target_pairs={{0,6},{1,7},{2,0},{3,1},{4,2},{5,3},{6,4},{7,5},{8,14},{9,15},{10,... | collective-permute-start | bytes 1966088 | tf_op jit(solution)/shard_map/ppermute | solution.py:25
  50.0 53.9 %collective-permute-start.16 = (f32[2,512,512]{2,1,0:T(8,128)}, f32[2,512,512]{2,1,0:T(8,128)}, u32[]{:S(2)}, u32[]{:S(2)}) collective-permute-start(f32[2,512,512]{2,1,0:T(8,128)} %get-tuple-element.368), channel_id=1, source_target_pairs={{0,1},{1,0},{2,3},{3,2},{4,5},{5,4},{6,7},{7,6},{8,9},{9,8},{10,11... | collective-permute-start | bytes 6291464 | tf_op jit(solution)/shard_map/ppermute | solution.py:45
  53.0 2.1 %copy-start.2 = (f32[8,512]{1,0:T(8,128)S(1)}, f32[8,512]{1,0:T(8,128)}, u32[]{:S(2)}) copy-start(f32[8,512]{1,0:T(8,128)} %get-tuple-element.369.stats_ref) | copy-start | bytes 49156
  53.0 37.1 %copy-start = (bf16[160,2048]{1,0:T(8,128)(2,1)S(1)}, bf16[160,2048]{1,0:T(8,128)(2,1)}, u32[]{:S(2)}) copy-start(bf16[160,2048]{1,0:T(8,128)(2,1)} %get-tuple-element.372.p0) | copy-start | bytes 1966084
  53.0 37.1 %copy-start.1 = (bf16[128,128]{1,0:T(8,128)(2,1)S(1)}, bf16[128,128]{1,0:T(8,128)(2,1)}, u32[]{:S(2)}) copy-start(bf16[128,128]{1,0:T(8,128)(2,1)} %get-tuple-element.377.pick_ref) | copy-start | bytes 98308
  53.3 46.6 %copy-start.7 = (bf16[128,2048]{1,0:T(8,128)(2,1)S(1)}, bf16[128,2048]{1,0:T(8,128)(2,1)}, u32[]{:S(2)}) copy-start(bf16[128,2048]{1,0:T(8,128)(2,1)} %copy-done.6) | copy-start | bytes 1572868
  53.3 46.8 %copy-start.9 = (bf16[128,2048]{1,0:T(8,128)(2,1)S(1)}, bf16[128,2048]{1,0:T(8,128)(2,1)}, u32[]{:S(2)}) copy-start(bf16[128,2048]{1,0:T(8,128)(2,1)} %copy-done.8) | copy-start | bytes 1572868
  53.3 36.8 %collective-permute-start.29 = (bf16[160,2048]{1,0:T(8,128)(2,1)}, bf16[160,2048]{1,0:T(8,128)(2,1)S(1)}, u32[]{:S(2)}, u32[]{:S(2)}) collective-permute-start(bf16[160,2048]{1,0:T(8,128)(2,1)} %get-tuple-element.374), channel_id=1, source_target_pairs={{0,2},{1,3},{2,4},{3,5},{4,6},{5,7},{6,0},{7,1},{8,10},{9,11},{10,... | collective-permute-start | bytes 1966088 | tf_op jit(solution)/shard_map/ppermute | solution.py:25
  54.9 35.2 %collective-permute-start.30 = (bf16[160,2048]{1,0:T(8,128)(2,1)}, bf16[160,2048]{1,0:T(8,128)(2,1)S(1)}, u32[]{:S(2)}, u32[]{:S(2)}) collective-permute-start(bf16[160,2048]{1,0:T(8,128)(2,1)} %get-tuple-element.375), channel_id=1, source_target_pairs={{0,4},{1,5},{2,6},{3,7},{4,0},{5,1},{6,2},{7,3},{8,12},{9,13},{10,... | collective-permute-start | bytes 1966088 | tf_op jit(solution)/shard_map/ppermute | solution.py:25
  55.1 3.1 %collective-permute-start.17 = (f32[8,512]{1,0:T(8,128)S(1)}, f32[8,512]{1,0:T(8,128)S(1)}, u32[]{:S(2)}, u32[]{:S(2)}) collective-permute-start(f32[8,512]{1,0:T(8,128)S(1)} %shard_map.97.own_ref), channel_id=1, source_target_pairs={{0,8},{8,0},{16,24},{24,16},{32,40},{40,32},{48,56},{56,48},{64,72... | collective-permute-start | bytes 49160 | tf_op jit(solution)/shard_map/ppermute | solution.py:33
  58.3 5.1 %collective-permute-start.18 = (f32[8,512]{1,0:T(8,128)S(1)}, f32[8,512]{1,0:T(8,128)S(1)}, u32[]{:S(2)}, u32[]{:S(2)}) collective-permute-start(f32[8,512]{1,0:T(8,128)S(1)} %shard_map.98.own_ref), channel_id=1, source_target_pairs={{0,24},{8,16},{16,8},{24,0},{32,56},{40,48},{48,40},{56,32},{64,88... | collective-permute-start | bytes 49160 | tf_op jit(solution)/shard_map/ppermute | solution.py:33
  63.4 3.0 %collective-permute-start.19 = (f32[8,512]{1,0:T(8,128)S(1)}, f32[8,512]{1,0:T(8,128)S(1)}, u32[]{:S(2)}, u32[]{:S(2)}) collective-permute-start(f32[8,512]{1,0:T(8,128)S(1)} %shard_map.99.own_ref), channel_id=1, source_target_pairs={{0,32},{8,40},{16,48},{24,56},{32,0},{40,8},{48,16},{56,24},{64,96... | collective-permute-start | bytes 49160 | tf_op jit(solution)/shard_map/ppermute | solution.py:37
  66.4 4.2 %collective-permute-start.20 = (f32[8,512]{1,0:T(8,128)S(1)}, f32[8,512]{1,0:T(8,128)S(1)}, u32[]{:S(2)}, u32[]{:S(2)}) collective-permute-start(f32[8,512]{1,0:T(8,128)S(1)} %shard_map.100.own_ref), channel_id=1, source_target_pairs={{0,96},{8,104},{16,112},{24,120},{32,64},{40,72},{48,80},{56,88},{... | collective-permute-start | bytes 49160 | tf_op jit(solution)/shard_map/ppermute | solution.py:37
  70.6 13.1 %collective-permute-start.21 = (f32[8,512]{1,0:T(8,128)S(1)}, f32[8,512]{1,0:T(8,128)S(1)}, u32[]{:S(2)}, u32[]{:S(2)}) collective-permute-start(f32[8,512]{1,0:T(8,128)S(1)} %shard_map.101.own_ref), channel_id=1, source_target_pairs={{0,2},{1,3},{2,0},{3,1},{4,6},{5,7},{6,4},{7,5},{8,10},{9,11},{10,... | collective-permute-start | bytes 49160 | tf_op jit(solution)/shard_map/ppermute | solution.py:41
  83.7 3.9 %collective-permute-start.22 = (f32[8,512]{1,0:T(8,128)S(1)}, f32[8,512]{1,0:T(8,128)S(1)}, u32[]{:S(2)}, u32[]{:S(2)}) collective-permute-start(f32[8,512]{1,0:T(8,128)S(1)} %shard_map.102.own_ref), channel_id=1, source_target_pairs={{0,6},{1,7},{2,4},{3,5},{4,2},{5,3},{6,0},{7,1},{8,14},{9,15},{10,... | collective-permute-start | bytes 49160 | tf_op jit(solution)/shard_map/ppermute | solution.py:41
  87.6 12.8 %collective-permute-start.24 = (bf16[128,2048]{1,0:T(8,128)(2,1)}, bf16[128,2048]{1,0:T(8,128)(2,1)}, u32[]{:S(2)}, u32[]{:S(2)}) collective-permute-start(bf16[128,2048]{1,0:T(8,128)(2,1)} %refs_6_.1), channel_id=1, source_target_pairs={{0,1},{1,0},{2,3},{3,2},{4,5},{5,4},{6,7},{7,6},{8,9},{9,8},{10,11... | collective-permute-start | bytes 1572872 | tf_op jit(solution)/shard_map/ppermute | solution.py:45
  90.1 14.5 %copy-start.4 = (f32[512,1]{1,0:T(8,128)}, f32[512,1]{1,0:T(8,128)S(1)}, u32[]{:S(2)}) copy-start(f32[512,1]{1,0:T(8,128)S(1)} %get-tuple-element.370.refs_2_) | copy-start | bytes 6148
  91.9 12.7 %copy-start.5 = (bf16[64,2048]{1,0:T(8,128)(2,1)}, bf16[64,2048]{1,0:T(8,128)(2,1)S(1)}, u32[]{:S(2)}) copy-start(bf16[64,2048]{1,0:T(8,128)(2,1)S(1)} %get-tuple-element.380.refs_14_) | copy-start | bytes 786436
  91.9 25.8 %all-to-all-start = ((f32[16,128,128]{2,1,0:T(8,128)}), f32[16,128,128]{2,1,0:T(8,128)S(1)}, u32[]{:S(2)}, u32[]{:S(2)}) async-start(f32[16,128,128]{2,1,0:T(8,128)} %get-tuple-element.383), calls=%async_computation | async-start | bytes 2097152 | tf_op jit(solution)/shard_map/all_to_all | solution.py:556
  99.5 2.2 %collective-permute-start.25 = (bf16[128,2048]{1,0:T(8,128)(2,1)}, bf16[128,2048]{1,0:T(8,128)(2,1)S(1)}, u32[]{:S(2)}, u32[]{:S(2)}) collective-permute-start(bf16[128,2048]{1,0:T(8,128)(2,1)} %collective-permute-done.7.refs_1_.refs_7_), channel_id=1, source_target_pairs={{0,1},{1,0},{2,3},{3,2},{4,5},{5,4},{6,7},{7,6},{8,9},{9,8},{10,11... | collective-permute-start | bytes 1572872 | tf_op jit(solution)/shard_map/ppermute | solution.py:45
  99.8 2.8 %collective-permute-start.26 = (bf16[128,2048]{1,0:T(8,128)(2,1)S(1)}, bf16[128,2048]{1,0:T(8,128)(2,1)}, u32[]{:S(2)}, u32[]{:S(2)}) collective-permute-start(bf16[128,2048]{1,0:T(8,128)(2,1)S(1)} %copy-done.7), channel_id=1, source_target_pairs={{0,1},{1,0},{2,3},{3,2},{4,5},{5,4},{6,7},{7,6},{8,9},{9,8},{10,11... | collective-permute-start | bytes 1572872 | tf_op jit(solution)/shard_map/ppermute | solution.py:45
  100.1 3.4 %collective-permute-start.27 = (bf16[128,2048]{1,0:T(8,128)(2,1)S(1)}, bf16[128,2048]{1,0:T(8,128)(2,1)}, u32[]{:S(2)}, u32[]{:S(2)}) collective-permute-start(bf16[128,2048]{1,0:T(8,128)(2,1)S(1)} %copy-done.9), channel_id=1, source_target_pairs={{0,1},{1,0},{2,3},{3,2},{4,5},{5,4},{6,7},{7,6},{8,9},{9,8},{10,11... | collective-permute-start | bytes 1572872 | tf_op jit(solution)/shard_map/ppermute | solution.py:45
  100.4 3.5 %collective-permute-start.31 = (bf16[64,2048]{1,0:T(8,128)(2,1)S(1)}, bf16[64,2048]{1,0:T(8,128)(2,1)S(1)}, u32[]{:S(2)}, u32[]{:S(2)}) collective-permute-start(bf16[64,2048]{1,0:T(8,128)(2,1)S(1)} %get-tuple-element.380.refs_14_), channel_id=1, source_target_pairs={{0,1},{1,0},{2,3},{3,2},{4,5},{5,4},{6,7},{7,6},{8,9},{9,8},{10,11... | collective-permute-start | bytes 786440 | tf_op jit(solution)/shard_map/ppermute | solution.py:45
  101.7 2.2 %copy-start.12 = (bf16[128,2048]{1,0:T(8,128)(2,1)}, bf16[128,2048]{1,0:T(8,128)(2,1)S(1)}, u32[]{:S(2)}) copy-start(bf16[128,2048]{1,0:T(8,128)(2,1)S(1)} %collective-permute-done.25.refs_11_) | copy-start | bytes 1572868
  101.7 2.2 %collective-permute-start.23 = (f32[512,1]{1,0:T(8,128)S(1)}, f32[512,1]{1,0:T(8,128)}, u32[]{:S(2)}, u32[]{:S(2)}) collective-permute-start(f32[512,1]{1,0:T(8,128)S(1)} %get-tuple-element.370.refs_2_), channel_id=1, source_target_pairs={{0,1},{1,0},{2,3},{3,2},{4,5},{5,4},{6,7},{7,6},{8,9},{9,8},{10,11... | collective-permute-start | bytes 6152 | tf_op jit(solution)/shard_map/ppermute | solution.py:45
  103.9 0.7 copy-start.13
  104.6 14.5 %copy-start.10 = (bf16[128,2048]{1,0:T(8,128)(2,1)S(1)}, bf16[128,2048]{1,0:T(8,128)(2,1)}, u32[]{:S(2)}) copy-start(bf16[128,2048]{1,0:T(8,128)(2,1)} %dec_ref.1) | copy-start | bytes 1572868
  104.6 14.5 %copy-start.11 = (bf16[128,2048]{1,0:T(8,128)(2,1)S(1)}, bf16[128,2048]{1,0:T(8,128)(2,1)}, u32[]{:S(2)}) copy-start(bf16[128,2048]{1,0:T(8,128)(2,1)} %enc_ref.1) | copy-start | bytes 1572868
  117.7 0.7 copy-start.3

commit v3 on v2

v3 whole, which is shorter than its diff:
```python
import functools

import jax
import jax.numpy as jnp
from jax import lax
from jax.experimental import pallas as pl
from jax.experimental.pallas import tpu as pltpu
from jax.sharding import PartitionSpec as P

BF = jnp.bfloat16
F32 = jnp.float32
I32 = jnp.int32
SLOTS = 16
HOPS = (0, 1, 3, 2)
BACK = (0, 2, 1, 3)
BLOCK = 128
HALF = 1024
CHUNK = 512
NEAR = 4 * BLOCK
PAYLOAD = BLOCK + 2 * SLOTS


def along_y(x, hop):
    pairs = [(t, ((t // 2 - hop) % 4) * 2 + t % 2) for t in range(8)]
    return lax.ppermute(x, "tok", pairs)


def partner(place, step):
    return 3 - place if step else place ^ 1


def swap_z(x, step):
    return lax.ppermute(x, "vocab", [(v, v // 4 * 4 + partner(v % 4, step)) for v in range(16)])


def swap_x(x, step):
    return lax.ppermute(x, "vocab", [(v, partner(v // 4, step) * 4 + v % 4) for v in range(16)])


def swap_y(x, step):
    return lax.ppermute(x, "tok", [(t, partner(t // 2, step) * 2 + t % 2) for t in range(8)])


def sibling(x):
    return lax.ppermute(x, "tok", [(t, t ^ 1) for t in range(8)])


def place():
    t = lax.axis_index("tok")
    return lax.axis_index("vocab"), t // 2, t % 2


def one(mask):
    return jnp.where(mask, 1.0, 0.0)


def iota(shape, dim):
    return lax.broadcasted_iota(I32, shape, dim)


def transposed(rows):
    return jnp.concatenate([rows, jnp.zeros((120, rows.shape[1]), F32)], axis=0).T


def whole(*shape):
    return pl.BlockSpec(shape, lambda *_: (0,) * len(shape), pipeline_mode=pl.Buffered(1))


VMEM = pl.BlockSpec(memory_space=pltpu.VMEM)


def params(limit=60 << 20):
    return pltpu.CompilerParams(vmem_limit_bytes=limit)


SMALL = 12 << 20


def cost(us):
    return pl.CostEstimate(flops=int(us * 1e9), bytes_accessed=1024, transcendentals=0)


def small(kernel, out_shape, *operands, scratch=()):
    many = isinstance(out_shape, list)
    return pl.pallas_call(
        kernel,
        in_specs=[VMEM] * len(operands),
        out_specs=[VMEM] * len(out_shape) if many else VMEM,
        out_shape=out_shape,
        scratch_shapes=scratch,
        compiler_params=params(SMALL),
    )(*operands)


def relay_kernel(after_ref, before_ref, i1, i2, i3, out_ref):
    _, _, core = place()
    out_ref[...] = jnp.where(core == 0, after_ref[...].astype(F32), before_ref[...].astype(F32)).astype(BF)


def farthest(after, before, ids):
    passed = small(relay_kernel, jax.ShapeDtypeStruct(after.shape, BF), after, before, *ids)
    return lax.ppermute(passed, "tok", [(t, (t + 2 if t % 2 else t - 2) % 8) for t in range(8)])


def rows_kernel(label_ref, dec_id_ref, enc_id_ref, dec_ref, enc_ref, rows_ref, ids_out):
    v, y, _ = place()
    ids = jnp.concatenate(
        [label_ref[...], dec_id_ref[...], enc_id_ref[...], jnp.zeros((5, BLOCK), I32)], axis=0
    )
    ids_out[...] = ids
    chip = lax.shift_right_logical(ids, 11)
    inside = []
    for kind in (1, 2):
        inside += [one(chip[kind : kind + 1] == v * 4 + lax.rem(y + h, 4)) for h in HOPS]
        inside += [jnp.zeros((4, BLOCK), F32)]
    inside = jnp.concatenate(inside, axis=0)
    before = one(iota((BLOCK, BLOCK), 0) < iota((BLOCK, BLOCK), 1)).astype(BF)
    rank = jnp.dot(inside.astype(BF), before, preferred_element_type=F32)
    rank_enc = rank[8:16] + jnp.sum(inside[0:8], axis=1, keepdims=True)
    slot = iota((SLOTS, BLOCK), 0).astype(F32)

    def chosen(rank, inside):
        return jnp.concatenate(
            [one(rank[i : i + 1] == slot) * one(slot < SLOTS - 1) * inside[i : i + 1] for i in range(4)], axis=0
        ).astype(BF)

    got = jnp.dot(chosen(rank[0:8], inside[0:8]), dec_ref[...], preferred_element_type=F32)
    got += jnp.dot(chosen(rank_enc, inside[8:16]), enc_ref[...], preferred_element_type=F32)
    rows_ref[...] = got.astype(BF)


def rows_to_send(labels, dec_ids, enc_ids, dec_grad, enc_grad):
    width = dec_grad.shape[1]
    return pl.pallas_call(
        rows_kernel,
        in_specs=[VMEM] * 5,
        out_specs=[VMEM] * 2,
        out_shape=[jax.ShapeDtypeStruct((4 * SLOTS, width), BF), jax.ShapeDtypeStruct((8, BLOCK), I32)],
        compiler_params=params(),
        cost_estimate=cost(1000),
    )(labels[None], dec_ids[None], enc_ids[None], dec_grad, enc_grad)


def plan_kernel(i0, i1, i2, i3, rows_ref):
    v, y, core = place()
    my_chip = v * 4 + y
    ids = (i0, i1, i2, i3)

    def kind(k):
        return jnp.concatenate([ids[i][k : k + 1, :] for i in range(4)] + [jnp.zeros((4, BLOCK), I32)], axis=0)

    lab, dec, enc = kind(0), kind(1), kind(2)

    def relative(ids):
        return ((ids - my_chip * (2 * HALF)) ^ (core * HALF)).astype(F32)

    def chip_of(ids):
        return lax.shift_right_logical(ids, 11).astype(F32)

    mine = my_chip.astype(F32)
    lab_f, lab_rel, lab_chip = lab.astype(F32), relative(lab), chip_of(lab)
    lab_t, chip_t = transposed(lab_f), transposed(lab_chip)
    earlier = one(iota((BLOCK, BLOCK), 0) < iota((BLOCK, BLOCK), 1))
    later = one(iota((BLOCK, BLOCK), 0) > iota((BLOCK, BLOCK), 1))
    slot = iota((SLOTS, BLOCK), 0).astype(F32)
    lane = iota((BLOCK, BLOCK), 1)
    most = jnp.zeros((1, 1), F32)
    slots = []
    for b in range(4):
        same = one(lab_t[:, b : b + 1] == lab_f[b : b + 1, :])
        same_chip = one(chip_t[:, b : b + 1] == lab_chip[b : b + 1, :])
        first_row = one(jnp.sum(same * earlier, axis=0, keepdims=True) == 0.0)
        first_col = one(jnp.sum(same * later, axis=1, keepdims=True) == 0.0)
        rank = jnp.sum(same_chip * earlier * first_col, axis=0, keepdims=True)
        most = jnp.maximum(most, jnp.max(rank * first_row, axis=1, keepdims=True) + 1.0)
        chosen = one(rank == slot) * (first_row * one(lab_chip[b : b + 1] == mine))
        slots.append(jnp.sum(chosen * (lab_rel[b : b + 1] + 1.0), axis=1, keepdims=True) - 1.0)
        if b == 0:
            rank_col = jnp.sum(same * (first_row * rank), axis=1, keepdims=True)
            chip = chip_t[:, 0:1].astype(I32)
            hop = (chip - y) & 3
            source = jnp.where(hop == 3, 2, jnp.where(hop == 2, 3, hop))
            arrival = (lax.shift_right_logical(chip, 2) * 4 + source) * SLOTS + rank_col.astype(I32)
            arrival = jnp.where(rank_col < SLOTS, arrival.astype(F32), -1.0)

    dec_chip, enc_chip = chip_of(dec), chip_of(enc)
    dec_rel, enc_rel = relative(dec), relative(enc)
    inside = jnp.concatenate([one(dec_chip == mine), one(enc_chip == mine)], axis=0)
    rank = jnp.dot(inside.astype(BF), earlier.astype(BF), preferred_element_type=F32)
    rank_enc = rank[8:16] + jnp.sum(inside[0:8], axis=1, keepdims=True)
    all_chips = iota((64, BLOCK), 0).astype(F32)
    tok_most = jnp.zeros((1, 1), F32)
    places = []
    for b in range(4):
        row = slice(b, b + 1)
        at = one(rank[row] == slot) * inside[row] * (dec_rel[row] + 1.0)
        at += one(rank_enc[row] == slot) * inside[8 + b : 9 + b] * (enc_rel[row] + 1.0)
        places.append(jnp.sum(at * one(slot < SLOTS - 1), axis=1, keepdims=True) - 1.0)
        count = one(dec_chip[row] == all_chips) + one(enc_chip[row] == all_chips)
        count = jnp.sum(count, axis=1, keepdims=True)
        tok_most = jnp.maximum(tok_most, jnp.max(count, axis=0, keepdims=True))
    cols = jnp.concatenate(slots + places, axis=0)
    cols = jnp.where(lane == 0, cols, jnp.where(lane == 1, most, jnp.where(lane == 2, tok_most, arrival)))
    rows_ref[...] = jnp.concatenate([lab_rel, cols.T[0:8]], axis=0)


def plan(ids):
    return small(
        plan_kernel,
        jax.ShapeDtypeStruct((16, BLOCK), F32),
        *ids,
    )


def by_lane(op, x):
    return functools.reduce(op, [x[:, 128 * i : 128 * (i + 1)] for i in range(x.shape[1] // 128)])


def logits_kernel(*refs):
    hidden = refs[:4]
    own_ref, sib_ref, number_ref, rows_ref = refs[4:8]
    own_out, sib_out, stats_ref = refs[9:12]
    payload = refs[12:16]
    states, table, logits, weights, in_sem, hidden_sem, out_sem = refs[16:]
    blocks = []
    for i in range(4):
        blocks.append(
            pltpu.make_async_copy(hidden[i], states.at[pl.ds(BLOCK * i, BLOCK)], hidden_sem.at[i])
        )
        blocks[i].start()
    loads = []
    for j in range(4):
        source = own_ref if j < 2 else sib_ref
        loads.append(
            pltpu.make_async_copy(
                source.at[pl.ds(CHUNK * (j % 2), CHUNK)], table.at[pl.ds(CHUNK * j, CHUNK)], in_sem.at[j]
            )
        )
        loads[j].start()
    for block in blocks:
        block.wait()

    cols = transposed(number_ref[0:8, :]).astype(I32)
    label = jnp.concatenate([cols[:, i : i + 1] for i in range(4)], axis=0)
    slot = transposed(number_ref[8:16, :])[0 : 4 * SLOTS, 0:1].astype(I32)
    stores = []
    peak = None
    for j in range(4):
        loads[j].wait()
        part = lax.dot_general(
            states[...], table[CHUNK * j : CHUNK * (j + 1), :], (((1,), (1,)), ((), ())), preferred_element_type=F32
        )
        logits[j] = part
        target = own_out if j < 2 else sib_out
        stores.append(pltpu.make_async_copy(logits.at[j], target.at[j % 2], out_sem.at[j]))
        stores[j].start()
        top = by_lane(jnp.maximum, part)
        peak = top if peak is None else jnp.maximum(peak, top)

    peak = jnp.max(peak, axis=1, keepdims=True)
    total = picked = None
    for j in range(4):
        part = logits[j]
        is_label = iota((NEAR, CHUNK), 1) + CHUNK * j == label
        weight = jnp.exp(part - peak)
        row_sum = by_lane(jnp.add, weight)
        hit = by_lane(jnp.add, jnp.where(is_label, part, 0.0))
        total = row_sum if total is None else total + row_sum
        picked = hit if picked is None else picked + hit
        at = slice(CHUNK * j, CHUNK * (j + 1))
        weights[0:NEAR, at] = jnp.where(is_label, 0.0, weight).astype(BF)
        slots = iota((4 * SLOTS, CHUNK), 1) + CHUNK * j == slot
        weights[NEAR:, at] = one(slots).astype(BF)

    total = jnp.sum(total, axis=1, keepdims=True)
    picked = jnp.sum(picked, axis=1, keepdims=True)
    lane = iota((NEAR, 128), 1)
    both = jnp.where(lane == 0, peak, jnp.where(lane == 1, total, jnp.where(lane == 2, picked, 0.0)))
    stats = both.T[0:8, :]
    stats_ref[...] = stats
    width = table.shape[1]
    left, digits = stats[0:1, :], []
    for _ in range(3):
        digits.append(left.astype(BF).astype(F32))
        left = left - digits[-1]
    for i in range(4):
        digit = [d[:, BLOCK * i : BLOCK * (i + 1)] for d in digits]
        digit = jnp.concatenate(digit + [jnp.zeros((1, width - 3 * BLOCK), F32)], axis=1)
        rows = rows_ref[SLOTS * i : SLOTS * (i + 1), :].astype(F32)
        payload[i][BLOCK + SLOTS : PAYLOAD, :] = jnp.where(
            iota((SLOTS, width), 0) == SLOTS - 1, digit, rows
        ).astype(BF)
    for j in range(4):
        at = slice(CHUNK * j, CHUNK * (j + 1))
        grad = jnp.dot(weights[...], table[:, at], preferred_element_type=F32).astype(BF)
        for i in range(4):
            payload[i][0:BLOCK, at] = grad[BLOCK * i : BLOCK * (i + 1)]
            payload[i][BLOCK : BLOCK + SLOTS, at] = grad[NEAR + SLOTS * i : NEAR + SLOTS * (i + 1)]
    for store in stores:
        store.wait()


def logits_and_grads(hidden, own, sib, numbers, rows, early):
    width = own.shape[1]
    anywhere = pl.BlockSpec(memory_space=pl.ANY)
    return pl.pallas_call(
        logits_kernel,
        in_specs=[anywhere] * 6 + [VMEM] * 2 + [anywhere],
        out_specs=[anywhere] * 2 + [VMEM] * 5,
        out_shape=[jax.ShapeDtypeStruct((2, NEAR, CHUNK), F32)] * 2
        + [jax.ShapeDtypeStruct((8, NEAR), F32)]
        + [jax.ShapeDtypeStruct((PAYLOAD, width), BF)] * 4,
        scratch_shapes=[
            pltpu.VMEM((NEAR, width), BF),
            pltpu.VMEM((2 * HALF, width), BF),
            pltpu.VMEM((4, NEAR, CHUNK), F32),
            pltpu.VMEM((NEAR + 4 * SLOTS, 2 * HALF), BF),
            pltpu.SemaphoreType.DMA((4,)),
            pltpu.SemaphoreType.DMA((4,)),
            pltpu.SemaphoreType.DMA((4,)),
        ],
        compiler_params=params(30 << 20),
    )(*hidden, own, sib, numbers, rows, *early)


def merged(parts):
    top = functools.reduce(jnp.maximum, [p[0:1] for p in parts])
    total = sum(p[1:2] * jnp.exp(p[0:1] - top) for p in parts)
    return top, total, sum(p[2:3] for p in parts)


def order_kernel(stats_ref, out_ref):
    _, y, _ = place()
    stats = stats_ref[...]
    for i in range(4):
        at = pl.multiple_of(lax.rem(y + HOPS[i], 4) * BLOCK, BLOCK)
        out_ref[:, pl.ds(at, BLOCK)] = stats[:, BLOCK * i : BLOCK * (i + 1)]


def merge_kernel(own_ref, other_ref, out_ref):
    own = own_ref[...]
    out_ref[...] = jnp.concatenate([*merged([own, other_ref[...]]), own[3:8]], axis=0)


def norm_kernel(own_ref, other_ref, row_ref, norm_ref, loss_ref, all_ref):
    _, y, _ = place()
    top, total, picked = merged([own_ref[...], other_ref[...]])
    norm = top + jnp.log(total)
    all_ref[...] = jnp.concatenate([norm, picked, jnp.zeros((6, NEAR), F32)], axis=0)

    def block(i):
        return all_ref[:, pl.ds(pl.multiple_of(lax.rem(y + HOPS[i], 4) * BLOCK, BLOCK), BLOCK)]

    mine = block(0)
    label = jnp.exp(mine[1:2] - mine[0:1]) - 1.0
    row_ref[...] = jnp.concatenate([mine[0:1], label, jnp.zeros((6, BLOCK), F32)], axis=0)
    loss_ref[...] = mine[0:1] - mine[1:2]
    norm_ref[...] = jnp.concatenate([block(i) for i in range(4)], axis=1)


def norms(stats):
    shape = jax.ShapeDtypeStruct((8, NEAR), F32)
    sums = small(order_kernel, shape, stats)
    for swap, step in ((swap_z, 0), (swap_z, 1), (swap_x, 0), (swap_x, 1), (swap_y, 0)):
        sums = small(merge_kernel, shape, sums, swap(sums, step))
    return small(
        norm_kernel,
        [
            jax.ShapeDtypeStruct((8, BLOCK), F32),
            jax.ShapeDtypeStruct((8, NEAR), F32),
            jax.ShapeDtypeStruct((1, BLOCK), F32),
        ],
        sums,
        swap_y(sums, 1),
        scratch=[pltpu.VMEM((8, NEAR), F32)],
    )


def combine_kernel(p0, p1, p2, p3, after_ref, parts_ref, rows_ref):
    payload = (p0, p1, p2, p3)
    peaks = []
    for i in range(4):
        rows = payload[i][BLOCK + SLOTS : PAYLOAD, :]
        rows_ref[SLOTS * i : SLOTS * (i + 1), :] = rows
        digits = rows[:, 0 : 3 * BLOCK].astype(F32)[SLOTS - 1 : SLOTS]
        peaks.append(digits[:, 2 * BLOCK :] + digits[:, BLOCK : 2 * BLOCK] + digits[:, 0:BLOCK])
    top = functools.reduce(jnp.maximum, peaks)
    cols = transposed(jnp.concatenate([jnp.exp(p - top) for p in peaks] + [jnp.zeros((4, BLOCK), F32)], axis=0))
    total = cols[:, 0:1] * payload[0][0:BLOCK, :].astype(F32)
    for i in range(1, 4):
        total += cols[:, i : i + 1] * payload[i][0:BLOCK, :].astype(F32)
    slots = jnp.concatenate([p[BLOCK : BLOCK + SLOTS, :] for p in payload], axis=0)
    left, digits = top, []
    for _ in range(3):
        digits.append(left.astype(BF).astype(F32))
        left = left - digits[-1]
    digits = jnp.concatenate(digits + [jnp.zeros((SLOTS - 3, BLOCK), F32)], axis=0).astype(BF)
    total = total.astype(BF)
    for i in range(parts_ref.shape[0]):
        at = slice(128 * i, 128 * (i + 1))
        parts_ref[i, 0:BLOCK, :] = total[:, at]
        parts_ref[i, BLOCK : BLOCK + 4 * SLOTS, :] = slots[:, at]
        parts_ref[i, BLOCK + 4 * SLOTS :, :] = digits


def combine(payload, after):
    width = payload[0].shape[1]
    return pl.pallas_call(
        combine_kernel,
        in_specs=[VMEM] * 5,
        out_specs=[VMEM] * 2,
        out_shape=[
            jax.ShapeDtypeStruct((16, BLOCK + 5 * SLOTS, width // 16), BF),
            jax.ShapeDtypeStruct((4 * SLOTS, width), BF),
        ],
        compiler_params=params(16 << 20),
    )(*payload, after)


def sum_kernel(groups_ref, row_ref, number_ref, end_ref, out_ref):
    count = groups_ref.shape[0]
    tail = BLOCK + 4 * SLOTS
    scales = []
    for i in range(count):
        digits = groups_ref[i, tail:, :].astype(F32)
        scales.append(jnp.exp(digits[2:3] + digits[1:2] + digits[0:1] - row_ref[0:1, :]))
    scales += [row_ref[1:2, :], number_ref[11:12, :], jnp.zeros((128 - count - 2, BLOCK), F32)]
    cols = jnp.concatenate(scales, axis=0).T
    slots = jnp.concatenate([groups_ref[i, BLOCK:tail, :] for i in range(count)], axis=0)
    at = cols[:, count + 1 : count + 2].astype(I32)
    chosen = one(iota((BLOCK, slots.shape[0]), 1) == at).astype(BF)
    total = cols[:, count : count + 1] * jnp.dot(chosen, slots, preferred_element_type=F32)
    for i in range(count):
        total += cols[:, i : i + 1] * groups_ref[i, 0:BLOCK, :].astype(F32)
    out_ref[...] = total + end_ref[0:1, :]


def table_kernel(*refs):
    logits, norms_of = refs[0:2], refs[2:4]
    numbers = refs[4:6]
    operands = refs[6:16]
    out_ref, end_ref, states, tiles, grads, results, logit_sem, state_sem, out_sem = refs[16:]
    count, _, tile = tiles.shape
    per = CHUNK // tile
    loads = [[], []]
    for j in range(count):
        for k in range(2):
            loads[k].append(
                pltpu.make_async_copy(
                    logits[k].at[j // per, :, pl.ds(tile * (j % per), tile)],
                    tiles.at[j, pl.ds(NEAR * k, NEAR)],
                    logit_sem.at[2 * j + k],
                )
            )
            loads[k][j].start()
    blocks = []
    low = 0
    for i, ref in enumerate(operands):
        rows = ref.shape[0]
        blocks.append(pltpu.make_async_copy(ref, states.at[pl.ds(low, rows)], state_sem.at[i]))
        blocks[i].start()
        low += rows

    norm = [transposed(ref[...])[:, 0:1] for ref in norms_of]
    labels, places = [], []
    for k in range(2):
        cols = transposed(numbers[k][0:8, :]).astype(I32)
        label = jnp.concatenate([cols[:, i : i + 1] for i in range(4)], axis=0)
        at = transposed(numbers[k][8:16, :])[4 * SLOTS : 8 * SLOTS, 0:1].astype(I32)
        labels.append(label ^ (HALF * k))
        places.append(jnp.where(at < 0, -1, at ^ (HALF * k)))
    places = jnp.concatenate(places, axis=0)

    def weigh(j):
        for k in range(2):
            at = slice(NEAR * k, NEAR * (k + 1))
            value = jnp.exp(tiles[j, at, :] - norm[k])
            is_label = iota((NEAR, tile), 1) + tile * j == labels[k]
            grads[j, at, :] = (value - one(is_label)).astype(BF)
        named = iota((8 * SLOTS, tile), 1) + tile * j == places
        grads[j, 2 * NEAR :, :] = one(named).astype(BF)

    end_ref[...] = jnp.zeros_like(end_ref)
    for k in range(2):
        loads[k][0].wait()
    weigh(0)
    for j in range(1, count):
        for k in range(2):
            loads[k][j].wait()
    for block in blocks:
        block.wait()
    stores = []
    for j in range(count):
        results[j] = lax.dot_general(
            grads[j], states[...], (((0,), (0,)), ((), ())), preferred_element_type=F32
        )
        stores.append(pltpu.make_async_copy(results.at[j], out_ref.at[pl.ds(tile * j, tile)], out_sem.at[j]))
        stores[j].start()
        if j + 1 < count:
            weigh(j + 1)
    for store in stores:
        store.wait()


def table_gradient(logits, norm_own, norm_sib, numbers, hidden, rows_own, rows_sib):
    width, tile = hidden[0].shape[1], 256
    count = HALF // tile
    rows = 2 * NEAR + 8 * SLOTS
    anywhere = pl.BlockSpec(memory_space=pl.ANY)
    return pl.pallas_call(
        table_kernel,
        in_specs=[anywhere] * 2 + [VMEM] * 4 + [anywhere] * 10,
        out_specs=[anywhere, VMEM],
        out_shape=[jax.ShapeDtypeStruct((HALF, width), F32), jax.ShapeDtypeStruct((8, 128), F32)],
        scratch_shapes=[
            pltpu.VMEM((rows, width), BF),
            pltpu.VMEM((count, 2 * NEAR, tile), F32),
            pltpu.VMEM((count, rows, tile), BF),
            pltpu.VMEM((count, tile, width), F32),
            pltpu.SemaphoreType.DMA((2 * count,)),
            pltpu.SemaphoreType.DMA((10,)),
            pltpu.SemaphoreType.DMA((count,)),
        ],
        compiler_params=params(),
    )(*logits, norm_own, norm_sib, *numbers, *hidden, rows_own, rows_sib)


def ranks(inside):
    n = inside.shape[-1]
    before = jnp.arange(n)[:, None] < jnp.arange(n)[None, :]
    return jnp.sum((inside[..., :, None] & before).astype(I32), axis=-2)


def pick(slot_of, inside, first_slot):
    slots = first_slot + jnp.arange(SLOTS, dtype=I32)
    return (slot_of[..., None, :] == slots[:, None]) & inside[..., None, :]


def exchange(rows):
    return [rows[0]] + [along_y(rows[BACK[i]], HOPS[i]) for i in range(1, 4)]


def more_label_rows(pairs, own_table, sib_table, first_slot):
    v, y, core = place()
    labels = jnp.stack([p[0] for p in pairs])
    chip = labels // (2 * HALF)
    same = labels[:, :, None] == labels[:, None, :]
    earlier = jnp.arange(BLOCK)[:, None] < jnp.arange(BLOCK)[None, :]
    is_first = ~jnp.any(same & earlier, axis=1)
    same_chip = chip[:, :, None] == chip[:, None, :]
    first_rank = jnp.sum((same_chip & earlier & is_first[:, :, None]).astype(I32), axis=1)
    rank = jnp.sum(jnp.where(same & is_first[:, :, None], first_rank[:, :, None], 0), axis=1)
    relative = (labels - (v * 4 + y) * (2 * HALF)) ^ (core * HALF)
    chosen = pick(rank, (chip == v * 4 + y) & is_first, first_slot)
    at = (jnp.sum(jnp.where(chosen, relative[:, None, :] + 1, 0), axis=2) - 1).reshape(4 * SLOTS, 1)
    row = jnp.arange(HALF, dtype=I32)
    rows = jnp.dot((at == row).astype(BF), own_table, preferred_element_type=F32)
    rows += jnp.dot((at == row + HALF).astype(BF), sib_table, preferred_element_type=F32)
    rows = rows.astype(BF).reshape(4, SLOTS, -1)
    got = jnp.concatenate(exchange([rows[i] for i in range(4)]))
    slot = jnp.arange(4 * SLOTS, dtype=I32)
    source = jnp.stack([v * 4 + (y + h) % 4 for h in HOPS])[slot // SLOTS]
    hit = (chip[0][:, None] == source[None]) & (rank[0][:, None] == (slot % SLOTS + first_slot)[None])
    return jnp.dot(hit.astype(BF), got, preferred_element_type=F32)


def more_token_rows(pairs, dec_grad, enc_grad, first_slot):
    v, y, core = place()
    own = jnp.concatenate([pairs[0][1], pairs[0][2]])
    chips = jnp.stack([v * 4 + (y + h) % 4 for h in HOPS])
    inside = own[None] // (2 * HALF) == chips[:, None]
    chosen = pick(ranks(inside), inside, first_slot).reshape(4 * SLOTS, 2 * BLOCK)
    rows = jnp.dot(chosen.astype(BF), jnp.concatenate([dec_grad, enc_grad]), preferred_element_type=F32)
    rows = rows.astype(BF).reshape(4, SLOTS, -1)
    got = jnp.concatenate(exchange([rows[i] for i in range(4)]))
    got = jnp.concatenate([got, sibling(got)])
    ids = jnp.stack(
        [jnp.concatenate([p[8 * c + 1], p[8 * c + 2]]) for c in range(2) for p in pairs]
    )
    inside = ids // (2 * HALF) == v * 4 + y
    chosen = pick(ranks(inside), inside, first_slot)
    relative = (ids - (v * 4 + y) * (2 * HALF)) ^ (core * HALF)
    at = jnp.sum(jnp.where(chosen, relative[:, None, :] + 1, 0), axis=2).reshape(1, 8 * SLOTS) - 1
    named = at == jnp.arange(HALF, dtype=I32)[:, None]
    return jnp.dot(named.astype(BF), got, preferred_element_type=F32)


def per_device(hidden_states, tied_table, labels, dec_ids, enc_ids, dec_grad, enc_grad):
    after, before = along_y(hidden_states, 1), along_y(hidden_states, -1)
    sib_table = sibling(tied_table)
    rows, own_ids = rows_to_send(labels, dec_ids, enc_ids, dec_grad, enc_grad)
    ids = [own_ids] + [along_y(own_ids, h) for h in HOPS[1:]]
    hidden = [hidden_states, after, before, farthest(after, before, ids[1:])]
    numbers = plan(ids)
    sib_numbers = sibling(numbers)
    hidden_sib = [sibling(h) for h in hidden]

    most = jnp.maximum(numbers[9:11, 0], sib_numbers[9:11, 0]).astype(I32)
    rounds_of_labels = (most[0] + SLOTS - 1) // SLOTS
    rounds_of_tokens = (most[1] + SLOTS) // SLOTS

    def all_ids(own):
        pair = jnp.concatenate([own, sibling(own)])
        return [pair] + [along_y(pair, h) for h in HOPS[1:]]

    own_logits, sib_logits, stats, *payload = logits_and_grads(
        hidden, tied_table, sib_table, numbers, rows, [sib_numbers]
    )

    payload = exchange(payload)
    mine, norm_rows, loss = norms(stats)

    got_logits = sibling(sib_logits)
    group, rows_own = combine(payload, mine)
    groups_of = lax.all_to_all(group, "vocab", 0, 0)

    grad_table, end = table_gradient(
        [own_logits, got_logits],
        norm_rows,
        sibling(norm_rows),
        [numbers, sib_numbers],
        hidden + hidden_sib,
        rows_own,
        sibling(rows_own),
    )

    grad_hidden = small(
        sum_kernel, jax.ShapeDtypeStruct((BLOCK, groups_of.shape[2]), F32), groups_of, mine, numbers, end
    )

    def add_labels(carry):
        r, grad = carry
        ids_r, slot = lax.optimization_barrier((own_ids, r * SLOTS))
        state = more_label_rows(all_ids(ids_r), tied_table, sib_table, slot).astype(BF)
        state = lax.all_to_all(state.reshape(BLOCK, 16, -1).transpose(1, 0, 2), "vocab", 0, 0)
        return r + 1, grad + mine[1][:, None] * jnp.sum(state.astype(F32), axis=0)

    _, grad_hidden = lax.while_loop(lambda c: c[0] < rounds_of_labels, add_labels, (jnp.int32(1), grad_hidden))

    def add_tokens(carry):
        r, grad = carry
        ids_r, dec, enc, slot = lax.optimization_barrier((own_ids, dec_grad, enc_grad, r * SLOTS - 1))
        return r + 1, grad + more_token_rows(all_ids(ids_r), dec, enc, slot)

    _, grad_table = lax.while_loop(lambda c: c[0] < rounds_of_tokens, add_tokens, (jnp.int32(1), grad_table))
    return grad_table, grad_hidden, loss.reshape(BLOCK)


def solution(mesh):
    in_specs = (
        P("tok", None),
        P(("vocab", "tok"), None),
        P("tok"),
        P("tok"),
        P("tok"),
        P("tok", None),
        P("tok", None),
    )
    out_specs = (P(("vocab", "tok"), None), P("tok", "vocab"), P("tok"))
    return jax.shard_map(
        per_device, mesh=mesh, in_specs=in_specs, out_specs=out_specs, check_vma=False
    )
```

time: 119 us -> 117 us (0.983)
  starting transfers between devices: 41.8 us -> 48.6 us
  Pallas kernels: 38.6 us -> 33.4 us
  waiting for transfers between devices: 30.9 us -> 27.2 us
    pallas_call x4 -> x3, Pallas kernels: 34.9 us -> 27.2 us  [the longest x1 13.6 us: logits_and_grads(): pl.pallas_call(logits_kernel, in_specs=[anywhere] * 6 + [VMEM] * 2 + [any...]
    ppermute x9, starting transfers between devices: 9.11 us -> 12.9 us  [sibling(): return lax.ppermute(x, 'tok', [(t, t ^ 1) for t in range(8)])]
    ppermute x2, waiting for transfers between devices: 14.8 us -> 11.6 us  [swap_y(): lax.ppermute(x, 'tok', [(t, partner(t // 2, step) * 2 + t % 2) for t in r...]
    pallas_call x8 -> x10, Pallas kernels: 1.34 us -> 3.75 us  [small(): pl.pallas_call(kernel, in_specs=[VMEM] * len(operands), out_specs=[VMEM]...]
    ppermute x2, starting transfers between devices: 2.18 us -> 4.25 us  [swap_y(): lax.ppermute(x, 'tok', [(t, partner(t // 2, step) * 2 + t % 2) for t in r...]
    unnamed x30 -> x34, local copies, waits for them, and re-layouts: 2.91 us -> 4.72 us
    slice x3 -> x1, local copies, waits for them, and re-layouts: 2.34 us -> 0.57 us  [per_device(): rounds_of_labels = (most[0] + SLOTS - 1) // SLOTS]
    ppermute x0 -> x1, waiting for transfers between devices: none -> 1.38 us  [farthest(): lax.ppermute(passed, 'tok', [(t, (t + 2 if t % 2 else t - 2) % 8) for t i...]
  transfers between devices with their start and end apart: 26 -> 25, of which waited for: 13 -> 12; matrix products, arithmetic and copies ran while one was open for 3% -> 0% of each run, Pallas kernels for 17% -> 16%
where the time goes in v3:
time: 117 us
  starting transfers between devices  48.6 us (42%)
  Pallas kernels  33.4 us (29%)
  waiting for transfers between devices  27.2 us (23%)
  local copies, waits for them, and re-layouts  5.29 us (5%)
  between operations  2.11 us (2%)
    ppermute x8, starting transfers between devices, along_y(): return lax.ppermute(x, 'tok', pairs)  13.7 us
    pallas_call x1, Pallas kernels, logits_and_grads(): pl.pallas_call(logits_kernel, in_specs=[anywhere] * 6 + [VMEM] * 2 + [any...  13.6 us
    ppermute x9, starting transfers between devices, sibling(): return lax.ppermute(x, 'tok', [(t, t ^ 1) for t in range(8)])  12.9 us
    pallas_call x1, Pallas kernels, table_gradient(): pl.pallas_call(table_kernel, in_specs=[anywhere] * 2 + [VMEM] * 4 + [anyw...  12.1 us
    ppermute x2, waiting for transfers between devices, swap_y(): lax.ppermute(x, 'tok', [(t, partner(t // 2, step) * 2 + t % 2) for t in r...  11.6 us
    all_to_all x1, starting transfers between devices, per_device(): groups_of = lax.all_to_all(group, 'vocab', 0, 0)  7.59 us
    ppermute x8, waiting for transfers between devices, along_y(): return lax.ppermute(x, 'tok', pairs)  6.15 us
    ppermute x2, starting transfers between devices, swap_z(): lax.ppermute(x, 'vocab', [(v, v // 4 * 4 + partner(v % 4, step)) for v in...  5.3 us
  transfers between devices with their start and end apart: 25, of which 12 were waited for; matrix products, arithmetic and copies ran while one was open for 0% of the time, Pallas kernels for 16%

profile of v3, /device:TPU:1, one launch (start us, length us, event | category | flops | bytes accessed | tf_op | source)
XLA Modules:
  0.0 116.9 jit_solution(10082247310498452689)
XLA Ops:
  0.6 3.6 %collective-permute-start.15 = (bf16[128,2048]{1,0:T(8,128)(2,1)}, bf16[128,2048]{1,0:T(8,128)(2,1)}, u32[]{:S(2)}, u32[]{:S(2)}) collective-permute-start(bf16[128,2048]{1,0:T(8,128)(2,1)} %refs_6_.1), channel_id=1, source_target_pairs={{0,6},{1,7},{2,0},{3,1},{4,2},{5,3},{6,4},{7,5},{8,14},{9,15},{10,... | collective-permute-start | bytes 1572872 | tf_op jit(solution)/shard_map/ppermute | solution.py:25
  4.3 1.0 collective-permute-start.21
  5.2 2.4 %shard_map.94 = (bf16[64,2048]{1,0:T(8,128)(2,1)}, s32[8,128]{1,0:T(8,128)S(1)}) custom-call(s32[1,128]{1,0:T(1,128)} %bitcast.142, s32[1,128]{1,0:T(1,128)} %bitcast.143, s32[1,128]{1,0:T(1,128)} %bitcast.144, bf16[128,2048]{1,0:T(8,128)(2,1)} %dec_ref.1, bf16[128,2048]{1,0:T(8,128)(2,1)} %enc_ref.1), custom_call_target="tpu_custom_call" | custom-call | flops 999999995904 | bytes 1024 | tf_op jit(solution)/shard_map/pallas_call | solution.py:134
  7.7 3.0 %collective-permute-start.17 = (s32[8,128]{1,0:T(8,128)S(1)}, s32[8,128]{1,0:T(8,128)S(1)}, u32[]{:S(2)}, u32[]{:S(2)}) collective-permute-start(s32[8,128]{1,0:T(8,128)S(1)} %get-tuple-element.601.i0), channel_id=1, source_target_pairs={{0,6},{1,7},{2,0},{3,1},{4,2},{5,3},{6,4},{7,5},{8,14},{9,15},{10,... | collective-permute-start | bytes 12296 | tf_op jit(solution)/shard_map/ppermute | solution.py:25
  10.6 4.5 %collective-permute-done.17.i1 = s32[8,128]{1,0:T(8,128)S(1)} collective-permute-done((s32[8,128]{1,0:T(8,128)S(1)}, s32[8,128]{1,0:T(8,128)S(1)}, u32[]{:S(2)}, u32[]{:S(2)}) %collective-permute-start.17) | collective-permute-done | bytes 4128 | tf_op jit(solution)/shard_map/ppermute | solution.py:25
  15.2 2.5 %collective-permute-start.19 = (s32[8,128]{1,0:T(8,128)S(1)}, s32[8,128]{1,0:T(8,128)S(1)}, u32[]{:S(2)}, u32[]{:S(2)}) collective-permute-start(s32[8,128]{1,0:T(8,128)S(1)} %get-tuple-element.601.i0), channel_id=1, source_target_pairs={{0,4},{1,5},{2,6},{3,7},{4,0},{5,1},{6,2},{7,3},{8,12},{9,13},{10,... | collective-permute-start | bytes 12296 | tf_op jit(solution)/shard_map/ppermute | solution.py:25
  17.6 0.7 collective-permute-done.18.i2
  18.4 0.9 collective-permute-done.19.i3
  19.2 1.3 %shard_map.95 = bf16[128,2048]{1,0:T(8,128)(2,1)S(1)} custom-call(bf16[128,2048]{1,0:T(8,128)(2,1)} %collective-permute-done.15.after_ref.refs_1_.refs_7_, bf16[128,2048]{1,0:T(8,128)(2,1)} %collective-permute-done.16.before_ref.refs_2_.refs_8_, s32[8,128]{1,0:T(8,128)S(1)} %collective-permute-done.17.i1, s32[8,128]{1,0:T(8,128)S(1)} %collective-permute-done.18.i2, ...), custom_call_target="tpu_custom_call" | custom-call | tf_op jit(solution)/shard_map/pallas_call | solution.py:85
  20.6 1.1 collective-permute-start.20
  21.7 1.2 %shard_map.96.refs_6_.refs_4_.number_ref = f32[16,128]{1,0:T(8,128)S(1)} custom-call(s32[8,128]{1,0:T(8,128)S(1)} %get-tuple-element.601.i0, s32[8,128]{1,0:T(8,128)S(1)} %collective-permute-done.17.i1, s32[8,128]{1,0:T(8,128)S(1)} %collective-permute-done.18.i2, s32[8,128]{1,0:T(8,128)S(1)} %collective-permute-done.19.i3), custom_call_target="tpu_custom_call" | custom-call | tf_op jit(solution)/shard_map/pallas_call | solution.py:85
  22.8 5.6 %collective-permute-start.22 = (f32[16,128]{1,0:T(8,128)S(1)}, f32[16,128]{1,0:T(8,128)S(1)}, u32[]{:S(2)}, u32[]{:S(2)}) collective-permute-start(f32[16,128]{1,0:T(8,128)S(1)} %shard_map.96.refs_6_.refs_4_.number_ref), channel_id=1, source_target_pairs={{0,1},{1,0},{2,3},{3,2},{4,5},{5,4},{6,7},{7,6},{8,9},{9,8},{10,11... | collective-permute-start | bytes 24584 | tf_op jit(solution)/shard_map/ppermute | solution.py:45
  28.4 0.8 collective-permute-done.22.refs_8_.refs_5_
  29.2 1.4 %collective-permute-done.20.refs_3_.refs_9_ = bf16[128,2048]{1,0:T(8,128)(2,1)S(1)} collective-permute-done((bf16[128,2048]{1,0:T(8,128)(2,1)S(1)}, bf16[128,2048]{1,0:T(8,128)(2,1)S(1)}, u32[]{:S(2)}, u32[]{:S(2)}) %collective-permute-start.20) | collective-permute-done | bytes 524320 | tf_op jit(solution)/shard_map/ppermute | solution.py:102
  30.6 0.0 collective-permute-done.21.refs_5_
  30.6 0.0 copy-start.4
  30.6 1.1 copy-done.4
  31.8 13.6 %shard_map.97 = (f32[2,512,512]{2,1,0:T(8,128)S(1)}, f32[2,512,512]{2,1,0:T(8,128)}, f32[8,512]{1,0:T(8,128)S(1)}, bf16[160,2048]{1,0:T(8,128)(2,1)S(1)}, bf16[1...) custom-call(bf16[128,2048]{1,0:T(8,128)(2,1)S(1)} %copy-done.1, ...), custom_call_target="tpu_custom_call" | custom-call | tf_op jit(solution)/shard_map/pallas_call | solution.py:306
  45.4 1.3 %copy-done = f32[2,512,512]{2,1,0:T(8,128)} copy-done((f32[2,512,512]{2,1,0:T(8,128)}, f32[2,512,512]{2,1,0:T(8,128)S(1)}, u32[]{:S(2)}) %copy-start) | copy-done | bytes 2097176
  46.7 3.0 %collective-permute-start.23 = (f32[2,512,512]{2,1,0:T(8,128)}, f32[2,512,512]{2,1,0:T(8,128)}, u32[]{:S(2)}, u32[]{:S(2)}) collective-permute-start(f32[2,512,512]{2,1,0:T(8,128)} %get-tuple-element.286), channel_id=1, source_target_pairs={{0,1},{1,0},{2,3},{3,2},{4,5},{5,4},{6,7},{7,6},{8,9},{9,8},{10,11... | collective-permute-start | bytes 6291464 | tf_op jit(solution)/shard_map/ppermute | solution.py:45
  49.8 3.4 %collective-permute-start.35 = (bf16[160,2048]{1,0:T(8,128)(2,1)S(1)}, bf16[160,2048]{1,0:T(8,128)(2,1)S(1)}, u32[]{:S(2)}, u32[]{:S(2)}) collective-permute-start(bf16[160,2048]{1,0:T(8,128)(2,1)S(1)} %get-tuple-element.290), channel_id=1, source_target_pairs={{0,6},{1,7},{2,0},{3,1},{4,2},{5,3},{6,4},{7,5},{8,14},{9,15},{10,... | collective-permute-start | bytes 1966088 | tf_op jit(solution)/shard_map/ppermute | solution.py:25
  53.2 0.0 collective-permute-start.36
  53.2 1.2 %collective-permute-start.37 = (bf16[160,2048]{1,0:T(8,128)(2,1)S(1)}, bf16[160,2048]{1,0:T(8,128)(2,1)S(1)}, u32[]{:S(2)}, u32[]{:S(2)}) collective-permute-start(bf16[160,2048]{1,0:T(8,128)(2,1)S(1)} %get-tuple-element.292), channel_id=1, source_target_pairs={{0,4},{1,5},{2,6},{3,7},{4,0},{5,1},{6,2},{7,3},{8,12},{9,13},{10,... | collective-permute-start | bytes 1966088 | tf_op jit(solution)/shard_map/ppermute | solution.py:25
  54.4 1.6 %collective-permute-start.24 = (f32[8,512]{1,0:T(8,128)S(1)}, f32[8,512]{1,0:T(8,128)S(1)}, u32[]{:S(2)}, u32[]{:S(2)}) collective-permute-start(f32[8,512]{1,0:T(8,128)S(1)} %shard_map.98.own_ref), channel_id=1, source_target_pairs={{0,8},{8,0},{16,24},{24,16},{32,40},{40,32},{48,56},{56,48},{64,72... | collective-permute-start | bytes 49160 | tf_op jit(solution)/shard_map/ppermute | solution.py:33
  56.0 1.4 %collective-permute-done.24.other_ref = f32[8,512]{1,0:T(8,128)S(1)} collective-permute-done((f32[8,512]{1,0:T(8,128)S(1)}, f32[8,512]{1,0:T(8,128)S(1)}, u32[]{:S(2)}, u32[]{:S(2)}) %collective-permute-start.24) | collective-permute-done | bytes 16416 | tf_op jit(solution)/shard_map/ppermute | solution.py:33
  57.5 3.7 %collective-permute-start.25 = (f32[8,512]{1,0:T(8,128)S(1)}, f32[8,512]{1,0:T(8,128)S(1)}, u32[]{:S(2)}, u32[]{:S(2)}) collective-permute-start(f32[8,512]{1,0:T(8,128)S(1)} %shard_map.99.own_ref), channel_id=1, source_target_pairs={{0,24},{8,16},{16,8},{24,0},{32,56},{40,48},{48,40},{56,32},{64,88... | collective-permute-start | bytes 49160 | tf_op jit(solution)/shard_map/ppermute | solution.py:33
  61.1 1.4 %collective-permute-done.25.other_ref = f32[8,512]{1,0:T(8,128)S(1)} collective-permute-done((f32[8,512]{1,0:T(8,128)S(1)}, f32[8,512]{1,0:T(8,128)S(1)}, u32[]{:S(2)}, u32[]{:S(2)}) %collective-permute-start.25) | collective-permute-done | bytes 16416 | tf_op jit(solution)/shard_map/ppermute | solution.py:33
  62.6 1.3 %collective-permute-start.26 = (f32[8,512]{1,0:T(8,128)S(1)}, f32[8,512]{1,0:T(8,128)S(1)}, u32[]{:S(2)}, u32[]{:S(2)}) collective-permute-start(f32[8,512]{1,0:T(8,128)S(1)} %shard_map.100.own_ref), channel_id=1, source_target_pairs={{0,32},{8,40},{16,48},{24,56},{32,0},{40,8},{48,16},{56,24},{64,96... | collective-permute-start | bytes 49160 | tf_op jit(solution)/shard_map/ppermute | solution.py:37
  63.9 1.7 %collective-permute-done.26.other_ref = f32[8,512]{1,0:T(8,128)S(1)} collective-permute-done((f32[8,512]{1,0:T(8,128)S(1)}, f32[8,512]{1,0:T(8,128)S(1)}, u32[]{:S(2)}, u32[]{:S(2)}) %collective-permute-start.26) | collective-permute-done | bytes 16416 | tf_op jit(solution)/shard_map/ppermute | solution.py:37
  65.6 2.6 %collective-permute-start.27 = (f32[8,512]{1,0:T(8,128)S(1)}, f32[8,512]{1,0:T(8,128)S(1)}, u32[]{:S(2)}, u32[]{:S(2)}) collective-permute-start(f32[8,512]{1,0:T(8,128)S(1)} %shard_map.101.own_ref), channel_id=1, source_target_pairs={{0,96},{8,104},{16,112},{24,120},{32,64},{40,72},{48,80},{56,88},{... | collective-permute-start | bytes 49160 | tf_op jit(solution)/shard_map/ppermute | solution.py:37
  68.1 1.6 %collective-permute-done.27.other_ref = f32[8,512]{1,0:T(8,128)S(1)} collective-permute-done((f32[8,512]{1,0:T(8,128)S(1)}, f32[8,512]{1,0:T(8,128)S(1)}, u32[]{:S(2)}, u32[]{:S(2)}) %collective-permute-start.27) | collective-permute-done | bytes 16416 | tf_op jit(solution)/shard_map/ppermute | solution.py:37
  69.8 1.9 %collective-permute-start.28 = (f32[8,512]{1,0:T(8,128)S(1)}, f32[8,512]{1,0:T(8,128)S(1)}, u32[]{:S(2)}, u32[]{:S(2)}) collective-permute-start(f32[8,512]{1,0:T(8,128)S(1)} %shard_map.102.own_ref), channel_id=1, source_target_pairs={{0,2},{1,3},{2,0},{3,1},{4,6},{5,7},{6,4},{7,5},{8,10},{9,11},{10,... | collective-permute-start | bytes 49160 | tf_op jit(solution)/shard_map/ppermute | solution.py:41
  71.7 10.1 %collective-permute-done.28.other_ref = f32[8,512]{1,0:T(8,128)S(1)} collective-permute-done((f32[8,512]{1,0:T(8,128)S(1)}, f32[8,512]{1,0:T(8,128)S(1)}, u32[]{:S(2)}, u32[]{:S(2)}) %collective-permute-start.28) | collective-permute-done | bytes 16416 | tf_op jit(solution)/shard_map/ppermute | solution.py:41
  81.8 2.3 %collective-permute-start.29 = (f32[8,512]{1,0:T(8,128)S(1)}, f32[8,512]{1,0:T(8,128)S(1)}, u32[]{:S(2)}, u32[]{:S(2)}) collective-permute-start(f32[8,512]{1,0:T(8,128)S(1)} %shard_map.103.own_ref), channel_id=1, source_target_pairs={{0,6},{1,7},{2,4},{3,5},{4,2},{5,3},{6,0},{7,1},{8,14},{9,15},{10,... | collective-permute-start | bytes 49160 | tf_op jit(solution)/shard_map/ppermute | solution.py:41
  84.1 1.6 %collective-permute-done.29.other_ref = f32[8,512]{1,0:T(8,128)S(1)} collective-permute-done((f32[8,512]{1,0:T(8,128)S(1)}, f32[8,512]{1,0:T(8,128)S(1)}, u32[]{:S(2)}, u32[]{:S(2)}) %collective-permute-start.29) | collective-permute-done | bytes 16416 | tf_op jit(solution)/shard_map/ppermute | solution.py:41
  85.7 1.9 %collective-permute-start.31 = (bf16[128,2048]{1,0:T(8,128)(2,1)S(1)}, bf16[128,2048]{1,0:T(8,128)(2,1)S(1)}, u32[]{:S(2)}, u32[]{:S(2)}) collective-permute-start(bf16[128,2048]{1,0:T(8,128)(2,1)S(1)} %copy-done.1), channel_id=1, source_target_pairs={{0,1},{1,0},{2,3},{3,2},{4,5},{5,4},{6,7},{7,6},{8,9},{9,8},{10,11... | collective-permute-start | bytes 1572872 | tf_op jit(solution)/shard_map/ppermute | solution.py:45
  87.6 0.5 shard_map.104
  88.2 0.0 collective-permute-done.36.p2
  88.2 0.0 collective-permute-done.37.p3
  88.2 1.5 %shard_map.105 = (bf16[16,208,128]{2,1,0:T(8,128)(2,1)}, bf16[64,2048]{1,0:T(8,128)(2,1)S(1)}) custom-call(bf16[160,2048]{1,0:T(8,128)(2,1)S(1)} %get-tuple-element.289.p0, bf16[160,2048]{1,0:T(8,128)(2,1)S(1)} %collective-permute-done.35.p1, bf16[160,2048]{1,0:T(8,128)(2,1)S(1)} %collective-permute-done.36.p2, ...), custom_call_target="tpu_custom_call" | custom-call | tf_op jit(solution)/shard_map/pallas_call | solution.py:408
  89.7 7.6 %all-to-all-start.1 = ((bf16[16,208,128]{2,1,0:T(8,128)(2,1)}), bf16[16,208,128]{2,1,0:T(8,128)(2,1)S(1)}, u32[]{:S(2)}, u32[]{:S(2)}) async-start(bf16[16,208,128]{2,1,0:T(8,128)(2,1)} %get-tuple-element.297), calls=%async_computation.1 | async-start | bytes 1703936 | tf_op jit(solution)/shard_map/all_to_all | solution.py:615
  97.3 0.4 collective-permute-start.32
  97.7 0.2 collective-permute-start.33
  97.9 0.3 collective-permute-start.34
  98.2 0.0 collective-permute-done.31.refs_10_
  98.2 0.2 collective-permute-start.38
  98.4 1.1 collective-permute-done.32.refs_11_
  99.5 0.3 collective-permute-start.30
  99.8 0.6 fusion.39
  101.6 0.0 collective-permute-done.33.refs_12_
  101.6 0.0 collective-permute-done.38.refs_15_
  101.6 0.0 collective-permute-done.23.refs_1_
  101.7 0.5 copy-done.14
  102.2 0.1 copy-done.13
  102.3 12.1 %shard_map.106 = (f32[1024,2048]{1,0:T(8,128)}, f32[8,128]{1,0:T(8,128)}) custom-call(f32[2,512,512]{2,1,0:T(8,128)} %copy-done, f32[2,512,512]{2,1,0:T(8,128)} %collective-permute-done.23.refs_1_, f32[8,512]{1,0:T(8,128)} %copy-done.8, f32[8,512]{1,0:T(8,128)} %copy-done.14, f32[16,128]{1,0:T(8,128)} %copy-done.5, f32[16,128]{1,0:T(8,128)} %copy-done.7, ...), custom_call_target="tpu_custom_call" | custom-call | tf_op jit(solution)/shard_map/pallas_call | solution.py:510
  114.4 0.0 all-to-all-done.1.groups_ref
  114.4 0.7 copy-done.9
  115.1 0.6 shard_map.107
  115.7 0.0 copy-start.15
  115.7 0.0 copy-start.16
  115.7 0.3 while.27
  116.0 0.0 copy-start.10
  116.0 0.7 copy-done.15
  116.7 0.2 copy-done.16
  (38 shorter events, 0.2 us)
Async XLA Ops:
  0.6 18.6 %collective-permute-start.15 = (bf16[128,2048]{1,0:T(8,128)(2,1)}, bf16[128,2048]{1,0:T(8,128)(2,1)}, u32[]{:S(2)}, u32[]{:S(2)}) collective-permute-start(bf16[128,2048]{1,0:T(8,128)(2,1)} %refs_6_.1), channel_id=1, source_target_pairs={{0,6},{1,7},{2,0},{3,1},{4,2},{5,3},{6,4},{7,5},{8,14},{9,15},{10,... | collective-permute-start | bytes 1572872 | tf_op jit(solution)/shard_map/ppermute | solution.py:25
  4.3 15.0 %collective-permute-start.16 = (bf16[128,2048]{1,0:T(8,128)(2,1)}, bf16[128,2048]{1,0:T(8,128)(2,1)}, u32[]{:S(2)}, u32[]{:S(2)}) collective-permute-start(bf16[128,2048]{1,0:T(8,128)(2,1)} %refs_6_.1), channel_id=1, source_target_pairs={{0,2},{1,3},{2,4},{3,5},{4,6},{5,7},{6,0},{7,1},{8,10},{9,11},{10,... | collective-permute-start | bytes 1572872 | tf_op jit(solution)/shard_map/ppermute | solution.py:25
  4.3 26.4 %collective-permute-start.21 = (bf16[1024,2048]{1,0:T(8,128)(2,1)}, bf16[1024,2048]{1,0:T(8,128)(2,1)}, u32[]{:S(2)}, u32[]{:S(2)}) collective-permute-start(bf16[1024,2048]{1,0:T(8,128)(2,1)} %refs_4_.1), channel_id=1, source_target_pairs={{0,1},{1,0},{2,3},{3,2},{4,5},{5,4},{6,7},{7,6},{8,9},{9,8},{10,11... | collective-permute-start | bytes 12582920 | tf_op jit(solution)/shard_map/ppermute | solution.py:45
  5.2 25.4 %copy-start.1 = (bf16[128,2048]{1,0:T(8,128)(2,1)S(1)}, bf16[128,2048]{1,0:T(8,128)(2,1)}, u32[]{:S(2)}) copy-start(bf16[128,2048]{1,0:T(8,128)(2,1)} %refs_6_.1) | copy-start | bytes 1572868
  7.7 7.5 %collective-permute-start.17 = (s32[8,128]{1,0:T(8,128)S(1)}, s32[8,128]{1,0:T(8,128)S(1)}, u32[]{:S(2)}, u32[]{:S(2)}) collective-permute-start(s32[8,128]{1,0:T(8,128)S(1)} %get-tuple-element.601.i0), channel_id=1, source_target_pairs={{0,6},{1,7},{2,0},{3,1},{4,2},{5,3},{6,4},{7,5},{8,14},{9,15},{10,... | collective-permute-start | bytes 12296 | tf_op jit(solution)/shard_map/ppermute | solution.py:25
  10.6 7.7 %collective-permute-start.18 = (s32[8,128]{1,0:T(8,128)S(1)}, s32[8,128]{1,0:T(8,128)S(1)}, u32[]{:S(2)}, u32[]{:S(2)}) collective-permute-start(s32[8,128]{1,0:T(8,128)S(1)} %get-tuple-element.601.i0), channel_id=1, source_target_pairs={{0,2},{1,3},{2,4},{3,5},{4,6},{5,7},{6,0},{7,1},{8,10},{9,11},{10,... | collective-permute-start | bytes 12296 | tf_op jit(solution)/shard_map/ppermute | solution.py:25
  15.2 4.1 %collective-permute-start.19 = (s32[8,128]{1,0:T(8,128)S(1)}, s32[8,128]{1,0:T(8,128)S(1)}, u32[]{:S(2)}, u32[]{:S(2)}) collective-permute-start(s32[8,128]{1,0:T(8,128)S(1)} %get-tuple-element.601.i0), channel_id=1, source_target_pairs={{0,4},{1,5},{2,6},{3,7},{4,0},{5,1},{6,2},{7,3},{8,12},{9,13},{10,... | collective-permute-start | bytes 12296 | tf_op jit(solution)/shard_map/ppermute | solution.py:25
  20.6 10.0 %collective-permute-start.20 = (bf16[128,2048]{1,0:T(8,128)(2,1)S(1)}, bf16[128,2048]{1,0:T(8,128)(2,1)S(1)}, u32[]{:S(2)}, u32[]{:S(2)}) collective-permute-start(bf16[128,2048]{1,0:T(8,128)(2,1)S(1)} %shard_map.95), channel_id=1, source_target_pairs={{0,6},{1,3},{2,0},{3,5},{4,2},{5,7},{6,4},{7,1},{8,14},{9,11},{10,... | collective-permute-start | bytes 1572872 | tf_op jit(solution)/shard_map/ppermute | solution.py:102
  22.8 75.6 %copy-start.5 = (f32[16,128]{1,0:T(8,128)}, f32[16,128]{1,0:T(8,128)S(1)}, u32[]{:S(2)}) copy-start(f32[16,128]{1,0:T(8,128)S(1)} %shard_map.96.refs_6_.refs_4_.number_ref) | copy-start | bytes 24580
  22.8 6.4 %collective-permute-start.22 = (f32[16,128]{1,0:T(8,128)S(1)}, f32[16,128]{1,0:T(8,128)S(1)}, u32[]{:S(2)}, u32[]{:S(2)}) collective-permute-start(f32[16,128]{1,0:T(8,128)S(1)} %shard_map.96.refs_6_.refs_4_.number_ref), channel_id=1, source_target_pairs={{0,1},{1,0},{2,3},{3,2},{4,5},{5,4},{6,7},{7,6},{8,9},{9,8},{10,11... | collective-permute-start | bytes 24584 | tf_op jit(solution)/shard_map/ppermute | solution.py:45
  29.2 69.2 %copy-start.7 = (f32[16,128]{1,0:T(8,128)}, f32[16,128]{1,0:T(8,128)S(1)}, u32[]{:S(2)}) copy-start(f32[16,128]{1,0:T(8,128)S(1)} %collective-permute-done.22.refs_8_.refs_5_) | copy-start | bytes 24580
  30.6 67.3 %copy-start.2 = (bf16[128,2048]{1,0:T(8,128)(2,1)}, bf16[128,2048]{1,0:T(8,128)(2,1)S(1)}, u32[]{:S(2)}) copy-start(bf16[128,2048]{1,0:T(8,128)(2,1)S(1)} %collective-permute-done.20.refs_3_.refs_9_) | copy-start | bytes 1572868
  30.6 1.1 copy-start.4
  45.4 1.4 %copy-start = (f32[2,512,512]{2,1,0:T(8,128)}, f32[2,512,512]{2,1,0:T(8,128)S(1)}, u32[]{:S(2)}) copy-start(f32[2,512,512]{2,1,0:T(8,128)S(1)} %get-tuple-element.285.refs_0_) | copy-start | bytes 6291460
  46.7 54.9 %collective-permute-start.23 = (f32[2,512,512]{2,1,0:T(8,128)}, f32[2,512,512]{2,1,0:T(8,128)}, u32[]{:S(2)}, u32[]{:S(2)}) collective-permute-start(f32[2,512,512]{2,1,0:T(8,128)} %get-tuple-element.286), channel_id=1, source_target_pairs={{0,1},{1,0},{2,3},{3,2},{4,5},{5,4},{6,7},{7,6},{8,9},{9,8},{10,11... | collective-permute-start | bytes 6291464 | tf_op jit(solution)/shard_map/ppermute | solution.py:45
  49.8 38.4 %collective-permute-start.35 = (bf16[160,2048]{1,0:T(8,128)(2,1)S(1)}, bf16[160,2048]{1,0:T(8,128)(2,1)S(1)}, u32[]{:S(2)}, u32[]{:S(2)}) collective-permute-start(bf16[160,2048]{1,0:T(8,128)(2,1)S(1)} %get-tuple-element.290), channel_id=1, source_target_pairs={{0,6},{1,7},{2,0},{3,1},{4,2},{5,3},{6,4},{7,5},{8,14},{9,15},{10,... | collective-permute-start | bytes 1966088 | tf_op jit(solution)/shard_map/ppermute | solution.py:25
  53.2 35.0 %collective-permute-start.36 = (bf16[160,2048]{1,0:T(8,128)(2,1)S(1)}, bf16[160,2048]{1,0:T(8,128)(2,1)S(1)}, u32[]{:S(2)}, u32[]{:S(2)}) collective-permute-start(bf16[160,2048]{1,0:T(8,128)(2,1)S(1)} %get-tuple-element.291), channel_id=1, source_target_pairs={{0,2},{1,3},{2,4},{3,5},{4,6},{5,7},{6,0},{7,1},{8,10},{9,11},{10,... | collective-permute-start | bytes 1966088 | tf_op jit(solution)/shard_map/ppermute | solution.py:25
  53.2 35.0 %collective-permute-start.37 = (bf16[160,2048]{1,0:T(8,128)(2,1)S(1)}, bf16[160,2048]{1,0:T(8,128)(2,1)S(1)}, u32[]{:S(2)}, u32[]{:S(2)}) collective-permute-start(bf16[160,2048]{1,0:T(8,128)(2,1)S(1)} %get-tuple-element.292), channel_id=1, source_target_pairs={{0,4},{1,5},{2,6},{3,7},{4,0},{5,1},{6,2},{7,3},{8,12},{9,13},{10,... | collective-permute-start | bytes 1966088 | tf_op jit(solution)/shard_map/ppermute | solution.py:25
  54.4 3.1 %collective-permute-start.24 = (f32[8,512]{1,0:T(8,128)S(1)}, f32[8,512]{1,0:T(8,128)S(1)}, u32[]{:S(2)}, u32[]{:S(2)}) collective-permute-start(f32[8,512]{1,0:T(8,128)S(1)} %shard_map.98.own_ref), channel_id=1, source_target_pairs={{0,8},{8,0},{16,24},{24,16},{32,40},{40,32},{48,56},{56,48},{64,72... | collective-permute-start | bytes 49160 | tf_op jit(solution)/shard_map/ppermute | solution.py:33
  57.5 5.1 %collective-permute-start.25 = (f32[8,512]{1,0:T(8,128)S(1)}, f32[8,512]{1,0:T(8,128)S(1)}, u32[]{:S(2)}, u32[]{:S(2)}) collective-permute-start(f32[8,512]{1,0:T(8,128)S(1)} %shard_map.99.own_ref), channel_id=1, source_target_pairs={{0,24},{8,16},{16,8},{24,0},{32,56},{40,48},{48,40},{56,32},{64,88... | collective-permute-start | bytes 49160 | tf_op jit(solution)/shard_map/ppermute | solution.py:33
  62.6 3.0 %collective-permute-start.26 = (f32[8,512]{1,0:T(8,128)S(1)}, f32[8,512]{1,0:T(8,128)S(1)}, u32[]{:S(2)}, u32[]{:S(2)}) collective-permute-start(f32[8,512]{1,0:T(8,128)S(1)} %shard_map.100.own_ref), channel_id=1, source_target_pairs={{0,32},{8,40},{16,48},{24,56},{32,0},{40,8},{48,16},{56,24},{64,96... | collective-permute-start | bytes 49160 | tf_op jit(solution)/shard_map/ppermute | solution.py:37
  65.6 4.2 %collective-permute-start.27 = (f32[8,512]{1,0:T(8,128)S(1)}, f32[8,512]{1,0:T(8,128)S(1)}, u32[]{:S(2)}, u32[]{:S(2)}) collective-permute-start(f32[8,512]{1,0:T(8,128)S(1)} %shard_map.101.own_ref), channel_id=1, source_target_pairs={{0,96},{8,104},{16,112},{24,120},{32,64},{40,72},{48,80},{56,88},{... | collective-permute-start | bytes 49160 | tf_op jit(solution)/shard_map/ppermute | solution.py:37
  69.8 12.0 %collective-permute-start.28 = (f32[8,512]{1,0:T(8,128)S(1)}, f32[8,512]{1,0:T(8,128)S(1)}, u32[]{:S(2)}, u32[]{:S(2)}) collective-permute-start(f32[8,512]{1,0:T(8,128)S(1)} %shard_map.102.own_ref), channel_id=1, source_target_pairs={{0,2},{1,3},{2,0},{3,1},{4,6},{5,7},{6,4},{7,5},{8,10},{9,11},{10,... | collective-permute-start | bytes 49160 | tf_op jit(solution)/shard_map/ppermute | solution.py:41
  81.8 3.9 %collective-permute-start.29 = (f32[8,512]{1,0:T(8,128)S(1)}, f32[8,512]{1,0:T(8,128)S(1)}, u32[]{:S(2)}, u32[]{:S(2)}) collective-permute-start(f32[8,512]{1,0:T(8,128)S(1)} %shard_map.103.own_ref), channel_id=1, source_target_pairs={{0,6},{1,7},{2,4},{3,5},{4,2},{5,3},{6,0},{7,1},{8,14},{9,15},{10,... | collective-permute-start | bytes 49160 | tf_op jit(solution)/shard_map/ppermute | solution.py:41
  85.7 12.5 %collective-permute-start.31 = (bf16[128,2048]{1,0:T(8,128)(2,1)S(1)}, bf16[128,2048]{1,0:T(8,128)(2,1)S(1)}, u32[]{:S(2)}, u32[]{:S(2)}) collective-permute-start(bf16[128,2048]{1,0:T(8,128)(2,1)S(1)} %copy-done.1), channel_id=1, source_target_pairs={{0,1},{1,0},{2,3},{3,2},{4,5},{5,4},{6,7},{7,6},{8,9},{9,8},{10,11... | collective-permute-start | bytes 1572872 | tf_op jit(solution)/shard_map/ppermute | solution.py:45
  88.2 13.5 %copy-start.8 = (f32[8,512]{1,0:T(8,128)}, f32[8,512]{1,0:T(8,128)S(1)}, u32[]{:S(2)}) copy-start(f32[8,512]{1,0:T(8,128)S(1)} %get-tuple-element.288.refs_2_) | copy-start | bytes 49156
  89.7 12.0 %copy-start.3 = (bf16[64,2048]{1,0:T(8,128)(2,1)}, bf16[64,2048]{1,0:T(8,128)(2,1)S(1)}, u32[]{:S(2)}) copy-start(bf16[64,2048]{1,0:T(8,128)(2,1)S(1)} %get-tuple-element.294.refs_14_) | copy-start | bytes 786436
  89.7 24.7 %all-to-all-start.1 = ((bf16[16,208,128]{2,1,0:T(8,128)(2,1)}), bf16[16,208,128]{2,1,0:T(8,128)(2,1)S(1)}, u32[]{:S(2)}, u32[]{:S(2)}) async-start(bf16[16,208,128]{2,1,0:T(8,128)(2,1)} %get-tuple-element.297), calls=%async_computation.1 | async-start | bytes 1703936 | tf_op jit(solution)/shard_map/all_to_all | solution.py:615
  97.3 2.2 %collective-permute-start.32 = (bf16[128,2048]{1,0:T(8,128)(2,1)}, bf16[128,2048]{1,0:T(8,128)(2,1)S(1)}, u32[]{:S(2)}, u32[]{:S(2)}) collective-permute-start(bf16[128,2048]{1,0:T(8,128)(2,1)} %collective-permute-done.15.after_ref.refs_1_.refs_7_), channel_id=1, source_target_pairs={{0,1},{1,0},{2,3},{3,2},{4,5},{5,4},{6,7},{7,6},{8,9},{9,8},{10,11... | collective-permute-start | bytes 1572872 | tf_op jit(solution)/shard_map/ppermute | solution.py:45
  97.7 3.9 %collective-permute-start.33 = (bf16[128,2048]{1,0:T(8,128)(2,1)}, bf16[128,2048]{1,0:T(8,128)(2,1)}, u32[]{:S(2)}, u32[]{:S(2)}) collective-permute-start(bf16[128,2048]{1,0:T(8,128)(2,1)} %collective-permute-done.16.before_ref.refs_2_.refs_8_), channel_id=1, source_target_pairs={{0,1},{1,0},{2,3},{3,2},{4,5},{5,4},{6,7},{7,6},{8,9},{9,8},{10,11... | collective-permute-start | bytes 1572872 | tf_op jit(solution)/shard_map/ppermute | solution.py:45
  97.9 3.7 %collective-permute-start.34 = (bf16[128,2048]{1,0:T(8,128)(2,1)S(1)}, bf16[128,2048]{1,0:T(8,128)(2,1)}, u32[]{:S(2)}, u32[]{:S(2)}) collective-permute-start(bf16[128,2048]{1,0:T(8,128)(2,1)S(1)} %collective-permute-done.20.refs_3_.refs_9_), channel_id=1, source_target_pairs={{0,1},{1,0},{2,3},{3,2},{4,5},{5,4},{6,7},{7,6},{8,9},{9,8},{10,11... | collective-permute-start | bytes 1572872 | tf_op jit(solution)/shard_map/ppermute | solution.py:45
  98.2 3.5 %copy-start.11 = (bf16[128,2048]{1,0:T(8,128)(2,1)}, bf16[128,2048]{1,0:T(8,128)(2,1)S(1)}, u32[]{:S(2)}) copy-start(bf16[128,2048]{1,0:T(8,128)(2,1)S(1)} %collective-permute-done.31.refs_10_) | copy-start | bytes 1572868
  98.2 3.4 %collective-permute-start.38 = (bf16[64,2048]{1,0:T(8,128)(2,1)S(1)}, bf16[64,2048]{1,0:T(8,128)(2,1)S(1)}, u32[]{:S(2)}, u32[]{:S(2)}) collective-permute-start(bf16[64,2048]{1,0:T(8,128)(2,1)S(1)} %get-tuple-element.294.refs_14_), channel_id=1, source_target_pairs={{0,1},{1,0},{2,3},{3,2},{4,5},{5,4},{6,7},{7,6},{8,9},{9,8},{10,11... | collective-permute-start | bytes 786440 | tf_op jit(solution)/shard_map/ppermute | solution.py:45
  99.5 2.2 %copy-start.12 = (bf16[128,2048]{1,0:T(8,128)(2,1)}, bf16[128,2048]{1,0:T(8,128)(2,1)S(1)}, u32[]{:S(2)}) copy-start(bf16[128,2048]{1,0:T(8,128)(2,1)S(1)} %collective-permute-done.32.refs_11_) | copy-start | bytes 1572868
  99.5 2.1 %collective-permute-start.30 = (f32[8,512]{1,0:T(8,128)S(1)}, f32[8,512]{1,0:T(8,128)S(1)}, u32[]{:S(2)}, u32[]{:S(2)}) collective-permute-start(f32[8,512]{1,0:T(8,128)S(1)} %get-tuple-element.288.refs_2_), channel_id=1, source_target_pairs={{0,1},{1,0},{2,3},{3,2},{4,5},{5,4},{6,7},{7,6},{8,9},{9,8},{10,11... | collective-permute-start | bytes 49160 | tf_op jit(solution)/shard_map/ppermute | solution.py:45
  101.6 0.6 copy-start.14
  101.6 0.7 copy-start.13
  102.3 12.1 %copy-start.6 = (f32[16,128]{1,0:T(8,128)S(1)}, f32[16,128]{1,0:T(8,128)}, u32[]{:S(2)}) copy-start(f32[16,128]{1,0:T(8,128)} %copy-done.5) | copy-start | bytes 24580
  114.4 0.7 copy-start.9
  115.7 1.0 copy-start.15
  115.7 1.2 %copy-start.16 = (bf16[128,2048]{1,0:T(8,128)(2,1)S(1)}, bf16[128,2048]{1,0:T(8,128)(2,1)}, u32[]{:S(2)}) copy-start(bf16[128,2048]{1,0:T(8,128)(2,1)} %enc_ref.1) | copy-start | bytes 1572868
  116.0 0.9 copy-start.10
